TPU v7x, 32 devices: a whole 2x2x4 slice. The times are simulated.
32 devices in a mesh: dp: 8 (over z, x), replica: 4 (over y, core).
Axes of the slice: x: 2, y: 2, z: 4, core: 2. Of those that a mesh axis runs over, the one named last changes fastest.
Arguments:
- states: bfloat16 [4, 1536, 376], P('replica', 'dp'), may hold values from -6 to 6
- actions: bfloat16 [4, 1536, 17], P('replica', 'dp'), may hold values from -1 to 1
- target_forward: bfloat16 [4, 1536, 256], P('replica', 'dp'), may hold values from -5 to 5
- next_index: int32 [4, 1536], P('replica', 'dp'), may hold values from 0 to 191
- latent_ids: int32 [4, 1536], P('replica', 'dp'), may hold values from 0 to 255
- latents: bfloat16 [256, 256], replicated, may hold values from -5 to 5
- f_state: bfloat16 [376, 1536], replicated, may hold values from -0.25 to 0.25
- f_action: bfloat16 [17, 1536], replicated, may hold values from -0.25 to 0.25
- f_latent: bfloat16 [256, 1536], replicated, may hold values from -0.25 to 0.25
- f_output: bfloat16 [1536, 256], replicated, may hold values from -0.15625 to 0.15625
- b_state: bfloat16 [376, 1536], replicated, may hold values from -0.3125 to 0.3125
- b_output: bfloat16 [1536, 256], replicated, may hold values from -1 to 1
Outputs:
- grad_f_state: bfloat16 [376, 1536], P(None, 'dp')
- grad_f_action: bfloat16 [17, 1536], P(None, 'dp')
- grad_f_latent: bfloat16 [256, 1536], P(None, 'dp')
- grad_f_output: bfloat16 [1536, 256], P('dp')
- grad_b_state: bfloat16 [376, 1536], P(None, 'dp')
- grad_b_output: bfloat16 [1536, 256], P('dp')
- loss_value: float32 [], replicated
Inputs may be any that keep to these rules, and one draw needn't show every extreme that they name: `next_index`: the next state lies in the same aligned block of 192 rows as the transition.
All inputs are finite; a program needn't handle non-finite values.
Results may differ from a plain program's by a relative error of at most 0.0056.
Values may be sent and summed in bfloat16 or wider, within the bound.
No kernel may reach another device: no remote copies, remote signals or barrier semaphores. Data moves between devices by JAX's collectives and lax.ppermute only.
A program may use at most 128 MiB of HBM per device.

v0:
```python
import math

import jax
import jax.numpy as jnp
from jax import lax
from jax.sharding import PartitionSpec as P

GAMMA = 0.98
EPSILON = 1e-06
HIGH = lax.Precision.HIGHEST


def forward_pass(
    current, later, moves, latent_rows, f_state, f_action, f_latent, f_output, b_state, b_output
):
    f_pre = (
        jnp.dot(current, f_state, preferred_element_type=jnp.float32)
        + jnp.dot(moves, f_action, preferred_element_type=jnp.float32)
        + jnp.dot(latent_rows, f_latent, preferred_element_type=jnp.float32)
    )
    f_hidden = jnp.maximum(f_pre, 0.0).astype(jnp.bfloat16)
    forward_emb = jnp.dot(f_hidden, f_output, preferred_element_type=jnp.float32).astype(
        jnp.bfloat16
    )
    b_pre = jnp.dot(later, b_state, preferred_element_type=jnp.float32)
    b_hidden = jnp.maximum(b_pre, 0.0).astype(jnp.bfloat16)
    b_raw = jnp.dot(b_hidden, b_output, preferred_element_type=jnp.float32)
    b_scale = lax.rsqrt(jnp.mean(b_raw * b_raw, axis=-1, keepdims=True) + EPSILON)
    backward_emb = (b_raw * b_scale).astype(jnp.bfloat16)
    return (f_pre, f_hidden, forward_emb, b_pre, b_hidden, b_raw, b_scale, backward_emb)


def backward_pass(
    grad_forward,
    grad_backward,
    current,
    later,
    moves,
    latent_rows,
    f_pre,
    f_hidden,
    b_pre,
    b_hidden,
    b_raw,
    b_scale,
    f_output,
    b_output,
):
    inner = jnp.mean(b_raw * grad_backward, axis=-1, keepdims=True)
    grad_raw = (b_scale * grad_backward - b_raw * b_scale * b_scale * b_scale * inner).astype(
        jnp.bfloat16
    )
    part_b_output = jnp.dot(b_hidden.T, grad_raw, preferred_element_type=jnp.float32)
    b_back = jnp.dot(grad_raw, b_output.T, preferred_element_type=jnp.float32)
    b_delta = jnp.where(b_pre > 0, b_back, 0.0).astype(jnp.bfloat16)
    part_b_state = jnp.dot(later.T, b_delta, preferred_element_type=jnp.float32)
    part_f_output = jnp.dot(f_hidden.T, grad_forward, preferred_element_type=jnp.float32)
    f_back = jnp.dot(grad_forward, f_output.T, preferred_element_type=jnp.float32)
    f_delta = jnp.where(f_pre > 0, f_back, 0.0).astype(jnp.bfloat16)
    part_f_state = jnp.dot(current.T, f_delta, preferred_element_type=jnp.float32)
    part_f_action = jnp.dot(moves.T, f_delta, preferred_element_type=jnp.float32)
    part_f_latent = jnp.dot(latent_rows.T, f_delta, preferred_element_type=jnp.float32)
    return (part_f_state, part_f_action, part_f_latent, part_f_output, part_b_state, part_b_output)


def local(
    states,
    actions,
    target_forward,
    next_index,
    latent_ids,
    latents,
    f_state,
    f_action,
    f_latent,
    f_output,
    b_state,
    b_output,
):
    current = states[0]
    moves = actions[0]
    later = jnp.take(current, next_index[0], axis=0)
    table_size = latents.shape[0]
    picks = (latent_ids[0][:, None] == jnp.arange(table_size, dtype=jnp.int32)[None, :]).astype(
        jnp.bfloat16
    )
    latent_rows = jnp.dot(picks, latents, preferred_element_type=jnp.float32).astype(jnp.bfloat16)
    f_pre, f_hidden, forward_emb, b_pre, b_hidden, b_raw, b_scale, backward_emb = forward_pass(
        current, later, moves, latent_rows, f_state, f_action, f_latent, f_output, b_state, b_output
    )
    local_rows = current.shape[0]
    group = local_rows * lax.axis_size("dp")
    total = group * lax.axis_size("replica")
    factor = 1.0 / math.sqrt(total)
    forward32 = forward_emb.astype(jnp.float32)
    back32 = backward_emb.astype(jnp.float32)
    error = forward32 - GAMMA * target_forward[0].astype(jnp.float32)
    diagonal_sum = jnp.sum(forward32 * back32)
    everyone = lax.all_gather(backward_emb, "dp", axis=0, tiled=True)
    scores = jnp.dot(error, everyone.T, precision=HIGH, preferred_element_type=jnp.float32)
    pulled = jnp.dot(scores, everyone, precision=HIGH, preferred_element_type=jnp.float32)
    square_sum = jnp.sum(scores * scores)
    pushed = lax.psum_scatter(
        jnp.dot(scores.T, forward32, precision=HIGH, preferred_element_type=jnp.float32),
        "dp",
        scatter_dimension=0,
        tiled=True,
    )
    grad_forward = (factor * (pulled / group - back32)).astype(jnp.bfloat16)
    grad_backward = factor * (pushed / group - forward32)
    partial_loss = 0.5 / group * square_sum - diagonal_sum
    part_fs, part_fa, part_fl, part_fo, part_bs, part_bo = backward_pass(
        grad_forward,
        grad_backward,
        current,
        later,
        moves,
        latent_rows,
        f_pre,
        f_hidden,
        b_pre,
        b_hidden,
        b_raw,
        b_scale,
        f_output,
        b_output,
    )
    shares = (
        lax.psum_scatter(part_fs, "dp", scatter_dimension=1, tiled=True),
        lax.psum_scatter(part_fa, "dp", scatter_dimension=1, tiled=True),
        lax.psum_scatter(part_fl, "dp", scatter_dimension=1, tiled=True),
        lax.psum_scatter(part_fo, "dp", scatter_dimension=0, tiled=True),
        lax.psum_scatter(part_bs, "dp", scatter_dimension=1, tiled=True),
        lax.psum_scatter(part_bo, "dp", scatter_dimension=0, tiled=True),
    )
    summed = lax.psum((shares[0], shares[1], shares[2], shares[3], shares[4], shares[5]), "replica")
    results = tuple((item.astype(jnp.bfloat16) for item in summed))
    loss_sum = lax.psum(partial_loss, ("dp", "replica"))
    return (
        results[0],
        results[1],
        results[2],
        results[3],
        results[4],
        results[5],
        loss_sum / total,
    )


def solution(mesh):
    in_specs = (
        P("replica", "dp", None),
        P("replica", "dp", None),
        P("replica", "dp", None),
        P("replica", "dp"),
        P("replica", "dp"),
        P(),
        P(),
        P(),
        P(),
        P(),
        P(),
        P(),
    )
    out_specs = (
        P(None, "dp"),
        P(None, "dp"),
        P(None, "dp"),
        P("dp", None),
        P(None, "dp"),
        P("dp", None),
        P(),
    )
    return jax.shard_map(local, mesh=mesh, in_specs=in_specs, out_specs=out_specs, check_vma=False)
```

profile of v0, /device:TPU:0, one launch (start us, length us, event | category | flops | bytes accessed | tf_op | source)
XLA Modules:
  0.0 571.2 jit_solution(8191502496069644080)
XLA Ops:
  8.7 1.9 gather_fusion
  13.6 33.8 %all_gather.3 = bf16[1536,256]{1,0:T(8,128)(2,1)S(1)} all-gather(bf16[192,256]{1,0:T(8,128)(2,1)S(1)} %multiply_convert_fusion), channel_id=1, replica_groups=mesh['dp'=8,'replica'=4] {'dp'}, dimensions={0}, use_global_device_ids=true | all-gather | bytes 884736 | tf_op jit(solution)/shard_map/all_gather | solution.py:99
  51.9 1.6 multiply_reduce_fusion
  54.6 2.7 fusion.33
  57.3 2.3 fusion.6
  61.9 2.1 copy.24
  64.1 2.5 fusion.8
  67.7 1.6 fusion.32
  70.2 1.9 convolution_bitcast_fusion
  72.1 3.1 copy.22
  75.2 48.0 %reduce-scatter.16.cloned.1.call-done = f32[192,256]{1,0:T(8,128)} async-done(((f32[1536,256]{1,0:T(8,128)}), f32[192,256]{1,0:T(8,128)}) %reduce-scatter.16.cloned.1.call-update) | async-done | bytes 196624 | tf_op jit(solution)/shard_map/reduce_scatter | solution.py:103
  123.3 1.7 fusion.12
  124.9 1.1 subtract_convert_fusion
  126.0 1.7 fusion.9
  128.8 2.4 fusion.2
  131.9 56.4 %reduce-scatter.24.cloned.1.call-done = f32[192,17]{1,0:T(8,128)} async-done(((f32[1536,17]{1,0:T(8,128)}), f32[192,17]{1,0:T(8,128)}) %reduce-scatter.24.cloned.1.call-update) | async-done | bytes 13072
  189.9 40.4 %psum.55 = f32[]{:T(128)} all-reduce(f32[]{:T(128)S(6)} %sub.19), channel_id=1, replica_groups=mesh['dp'=8,'replica'=4] {'dp','replica'}, use_global_device_ids=true, to_apply=%region_17.18 | all-reduce | flops 1 | bytes 8 | tf_op jit(solution)/shard_map/psum | solution.py:138
  230.9 25.0 %reduce-scatter.14.cloned.1.call-done = f32[192,256]{1,0:T(8,128)} async-done(((f32[1536,256]{1,0:T(8,128)}), f32[192,256]{1,0:T(8,128)}) %reduce-scatter.14.cloned.1.call-update) | async-done | bytes 196624 | tf_op jit(solution)/shard_map/reduce_scatter | solution.py:132
  255.9 67.5 %reduce-scatter.12.cloned.1.call-done = f32[256,192]{0,1:T(8,128)} async-done(((f32[256,1536]{0,1:T(8,128)}), f32[256,192]{0,1:T(8,128)}) %reduce-scatter.12.cloned.1.call-update) | async-done | bytes 196624 | tf_op jit(solution)/shard_map/reduce_scatter | solution.py:131
  323.3 71.3 %reduce-scatter.22.cloned.1.call-done = f32[192,376]{1,0:T(8,128)} async-done(((f32[1536,376]{1,0:T(8,128)}), f32[192,376]{1,0:T(8,128)}) %reduce-scatter.22.cloned.1.call-update) | async-done | bytes 288784
  394.6 1.1 copy.23
  395.7 66.1 %reduce-scatter.20.cloned.1.call-done = f32[192,256]{1,0:T(8,128)} async-done(((f32[1536,256]{1,0:T(8,128)}), f32[192,256]{1,0:T(8,128)}) %reduce-scatter.20.cloned.1.call-update) | async-done | bytes 196624 | tf_op jit(solution)/shard_map/reduce_scatter | solution.py:134
  461.8 71.8 %reduce-scatter.18.cloned.1.call-done = f32[376,192]{0,1:T(8,128)} async-done(((f32[376,1536]{0,1:T(8,128)}), f32[376,192]{0,1:T(8,128)}) %reduce-scatter.18.cloned.1.call-update) | async-done | bytes 288784 | tf_op jit(solution)/shard_map/reduce_scatter | solution.py:133
  533.6 28.9 %all-reduce.2 = (bf16[376,192]{1,0:T(8,128)(2,1)S(1)}, bf16[17,192]{1,0:T(8,128)(2,1)}, bf16[256,192]{0,1:T(8,128)(2,1)}, bf16[192,256]{1,0:T(8,128)(2,1)}, bf16...) all-reduce(f32[376,192]{1,0:T(8,128)S(1)} %copy.23, ...), channel_id=1, replica_groups=mesh['dp'=8,'replica'=4] {'replica'}, use_global_device_ids=true, to_apply=%region_2.3 | all-reduce | flops 295104 | bytes 1770624 | tf_op jit(solution)/shard_map/psum | solution.py:136
  (87 shorter events, 17.2 us)
Async XLA Ops:
  7.2 3.5 copy-start
  7.2 116.1 %reduce-scatter.16.cloned.1.call-start = ((), (), s32[]{:S(2)}) async-start(), calls=%async_computation.9 | async-start | bytes 1769472 | tf_op jit(solution)/shard_map/reduce_scatter | solution.py:103
  10.6 1.2 copy-start.7
  11.8 35.6 %copy-start.1 = (bf16[1,192,376]{2,1,0:T(8,128)(2,1)S(1)}, bf16[1,192,376]{2,1,0:T(8,128)(2,1)}, u32[]{:S(2)}) copy-start(bf16[1,192,376]{2,1,0:T(8,128)(2,1)} %param.12) | copy-start | bytes 433156
  11.8 35.6 %copy-start.17 = (bf16[376,1536]{1,0:T(8,128)(2,1)S(1)}, bf16[376,1536]{1,0:T(8,128)(2,1)}, u32[]{:S(2)}) copy-start(bf16[376,1536]{1,0:T(8,128)(2,1)} %param.18) | copy-start | bytes 3465220
  47.4 3.9 copy-start.6
  47.4 1.2 copy-start.25
  47.4 1.2 copy-start.26
  48.7 1.2 copy-start.22
  49.9 1.1 copy-start.9
  51.9 1.7 copy-start.13
  57.3 130.9 %reduce-scatter.24.cloned.1.call-start = ((), (), s32[]{:S(2)}) async-start(), calls=%async_computation.13 | async-start | bytes 884736
  57.3 2.3 copy-start.10
  64.1 191.8 %reduce-scatter.14.cloned.1.call-start = ((), (), s32[]{:S(2)}) async-start(), calls=%async_computation.8 | async-start | bytes 1769472 | tf_op jit(solution)/shard_map/reduce_scatter | solution.py:132
  66.6 1.1 copy-start.5
  66.6 1.1 copy-start.19
  66.6 256.7 %reduce-scatter.12.cloned.1.call-start = ((), (), s32[]{:S(2)}) async-start(), calls=%async_computation.7 | async-start | bytes 1769472 | tf_op jit(solution)/shard_map/reduce_scatter | solution.py:131
  69.3 325.3 %reduce-scatter.22.cloned.1.call-start = ((), (), s32[]{:S(2)}) async-start(), calls=%async_computation.12 | async-start | bytes 2654208
  75.2 48.1 %copy-start.12 = (f32[192,256]{1,0:T(8,128)S(1)}, f32[192,256]{1,0:T(8,128)}, u32[]{:S(2)}) copy-start(f32[192,256]{1,0:T(8,128)} %copy-done.11) | copy-start | bytes 589828
  75.2 48.1 %copy-start.14 = (bf16[192,256]{1,0:T(8,128)(2,1)S(1)}, bf16[192,256]{1,0:T(8,128)(2,1)}, u32[]{:S(2)}) copy-start(bf16[192,256]{1,0:T(8,128)(2,1)} %copy-done.13) | copy-start | bytes 294916
  75.2 386.6 %reduce-scatter.20.cloned.1.call-start = ((), (), s32[]{:S(2)}) async-start(), calls=%async_computation.11 | async-start | bytes 1769472 | tf_op jit(solution)/shard_map/reduce_scatter | solution.py:134
  127.7 1.1 copy-start.8
  127.7 1.1 copy-start.16
  127.7 405.9 %reduce-scatter.18.cloned.1.call-start = ((), (), s32[]{:S(2)}) async-start(), calls=%async_computation.10 | async-start | bytes 2654208 | tf_op jit(solution)/shard_map/reduce_scatter | solution.py:133
  (11 other events, 9.0 us)
Sparse Core Ops, SparseCore 0:
  57.4 65.8 reduce-scatter.15
  126.9 61.2 reduce-scatter.23
  191.7 64.1 reduce-scatter.13
  259.5 63.7 reduce-scatter.11
  326.7 67.8 reduce-scatter.21
  397.9 63.8 reduce-scatter.19
  465.7 67.8 reduce-scatter.17
where the time goes:
time: 572 us; the launch traced here: 571 us
  waiting for transfers between devices  406 us (71%)
  blocking collectives  103 us (18%)
  matrix products  20.5 us (4%)
  local copies, waits for them, and re-layouts  19.5 us (3%)
  between operations  17.5 us (3%)
    unnamed x9, waiting for transfers between devices  128 us
    reduce_scatter x1, waiting for transfers between devices, local(): lax.psum_scatter(part_bs, 'dp', scatter_dimension=1, tiled=True)  71.8 us
    reduce_scatter x1, waiting for transfers between devices, local(): lax.psum_scatter(part_fl, 'dp', scatter_dimension=1, tiled=True)  67.5 us
    reduce_scatter x1, waiting for transfers between devices, local(): lax.psum_scatter(part_bo, 'dp', scatter_dimension=0, tiled=True)  66.1 us
    reduce_scatter x1, waiting for transfers between devices, local(): lax.psum_scatter(jnp.dot(scores.T, forward32, precision=HIGH, preferred_e...  48 us
    psum x1, blocking collectives, local(): loss_sum = lax.psum(partial_loss, ('dp', 'replica'))  40.4 us
    all_gather x1, blocking collectives, local(): everyone = lax.all_gather(backward_emb, 'dp', axis=0, tiled=True)  33.8 us
    psum x1, blocking collectives, local(): lax.psum((shares[0], shares[1], shares[2], shares[3], shares[4], shares[5...  28.9 us
  transfers between devices with their start and end apart: 7, of which 7 were waited for; matrix products, arithmetic and copies ran while one was open for 4% of the time, Pallas kernels for 0%

commit v1 on v0

v1 whole, which is shorter than its diff:
```python
import functools
import math

import jax
import jax.numpy as jnp
from jax import lax
from jax.experimental import pallas as pl
from jax.experimental.pallas import tpu as pltpu
from jax.sharding import PartitionSpec as P

GAMMA = 0.98
EPSILON = 1e-06
HIGH = lax.Precision.HIGHEST
BF16 = jnp.bfloat16
F32 = jnp.float32
LANES = 128
ROW_TILE = 16
VMEM_LIMIT = 56 * 1024 * 1024
KERNEL_GROUP_LIMIT = 2048


def round_up(value, unit):
    return -(-value // unit) * unit


def dot_nn(left, right):
    return lax.dot_general(left, right, (((1,), (0,)), ((), ())), preferred_element_type=F32)


def dot_nt(left, right):
    return lax.dot_general(left, right, (((1,), (1,)), ((), ())), preferred_element_type=F32)


def dot_tn(left, right):
    return lax.dot_general(left, right, (((0,), (0,)), ((), ())), preferred_element_type=F32)


def split_two(value):
    high = value.astype(BF16)
    return high, (value - high.astype(F32)).astype(BF16)


def step_kernel(
    cfg,
    *refs,
):
    chunks = cfg["chunks"]
    x_refs = refs[:chunks]
    (
        wf_ref,
        wb_ref,
        fo_ref,
        bo_ref,
        lat_ref,
        wfb_ref,
        wbb_ref,
        fob_ref,
        bob_ref,
        send_ref,
        keep_ref,
        loss_ref,
        a_ref,
        later_ref,
        f_ref,
        b_ref,
        u_ref,
        t_ref,
        part_ref,
    ) = refs[chunks:]
    rows, obs, act, rank = cfg["rows"], cfg["obs"], cfg["act"], cfg["rank"]
    obs_pad, x_pad, hidden, zcount = cfg["obs_pad"], cfg["x_pad"], cfg["hidden"], cfg["zcount"]
    group, total, block = cfg["group"], cfg["total"], cfg["block"]
    tile = cfg["tile"]
    inner_chunks = cfg["inner"]
    m = rows * inner_chunks
    steps = chunks // inner_chunks

    for j in range(chunks):
        a_ref[pl.ds(j * rows, rows), pl.ds(0, x_pad)] = x_refs[j][:, :x_pad]
        t_ref[pl.ds(j * rows, rows), :] = x_refs[j][:, x_pad:]

    def forward(step, carry):
        gram, ftf, ftt = carry
        base = pl.multiple_of(step * m, ROW_TILE)
        here = pl.ds(base, m)
        xx = a_ref[here, pl.ds(0, x_pad)]
        next_col = xx[:, obs + act : obs + act + 1].astype(F32)
        id_col = xx[:, obs + act + 1 : obs + act + 2].astype(F32)
        spots = lax.broadcasted_iota(jnp.int32, (m, zcount), 1).astype(F32)
        picks = jnp.where(id_col == spots, 1.0, 0.0).astype(BF16)
        z = dot_nn(picks, lat_ref[...]).astype(BF16)
        a_ref[here, pl.ds(x_pad, rank)] = z
        row_spots = lax.broadcasted_iota(jnp.int32, (rows, rows), 1).astype(F32)
        pieces = []
        for j in range(inner_chunks):
            near = xx[j * rows : (j + 1) * rows, :obs_pad]
            hot = jnp.where(next_col[j * rows : (j + 1) * rows] == row_spots, 1.0, 0.0).astype(BF16)
            pieces.append(dot_nn(hot, near).astype(BF16))
        later = jnp.concatenate(pieces, axis=0) if inner_chunks > 1 else pieces[0]
        later_ref[here, :] = later
        whole = a_ref[here, :]
        f_acc = jnp.zeros((m, rank), F32)
        u = jnp.zeros((m, rank), F32)
        for n in range(0, hidden, tile):
            h = jnp.maximum(dot_nn(whole, wf_ref[:, n : n + tile]), 0.0).astype(BF16)
            f_acc = f_acc + dot_nn(h, fo_ref[n : n + tile, :])
            g = jnp.maximum(dot_nn(later, wb_ref[:, n : n + tile]), 0.0).astype(BF16)
            u = u + dot_nn(g, bo_ref[n : n + tile, :])
        emb = f_acc.astype(BF16)
        scale = lax.rsqrt(jnp.mean(u * u, axis=-1, keepdims=True) + EPSILON)
        back = (u * scale).astype(BF16)
        f_ref[here, :] = emb
        b_ref[here, :] = back
        u_ref[here, :] = u
        target = t_ref[here, :]
        gram = gram + dot_tn(back, back)
        ftf = ftf + dot_tn(emb, emb)
        ftt = ftt + dot_tn(target, emb)
        return gram, ftf, ftt

    zero = jnp.zeros((rank, rank), F32)
    gram, ftf, ttf = lax.fori_loop(0, steps, forward, (zero, zero, zero))
    cross_t = ftf - GAMMA * ttf
    gram_hi, gram_lo = split_two(gram)
    cross_hi, cross_lo = split_two(cross_t)
    factor = 1.0 / math.sqrt(total)
    part_ref[...] = jnp.zeros_like(part_ref)
    c0, c1, c2, c3 = cfg["cols"]

    def backward(step, carry):
        square, diagonal = carry
        base = pl.multiple_of(step * m, ROW_TILE)
        here = pl.ds(base, m)
        emb = f_ref[here, :]
        emb32 = emb.astype(F32)
        back = b_ref[here, :]
        back32 = back.astype(F32)
        error = emb32 - GAMMA * t_ref[here, :].astype(F32)
        err_hi, err_lo = split_two(error)
        pulled = dot_nn(err_hi, gram_hi) + (dot_nn(err_hi, gram_lo) + dot_nn(err_lo, gram_hi))
        square = square + jnp.sum(pulled * error, axis=0, keepdims=True)
        diagonal = diagonal + jnp.sum(emb32 * back32, axis=0, keepdims=True)
        d_f = (factor * (pulled / group - back32)).astype(BF16)
        pushed = dot_nn(back, cross_hi) + dot_nn(back, cross_lo)
        d_b = factor * (pushed / group - emb32)
        u = u_ref[here, :]
        scale = lax.rsqrt(jnp.mean(u * u, axis=-1, keepdims=True) + EPSILON)
        inner = jnp.mean(u * d_b, axis=-1, keepdims=True)
        d_u = (scale * d_b - u * (scale * scale * scale * inner)).astype(BF16)
        whole = a_ref[here, :]
        later = later_ref[here, :]
        f_pre = dot_nt(wfb_ref[...], whole)
        f_hid = jnp.maximum(f_pre, 0.0).astype(BF16)
        f_delta = jnp.where(f_pre > 0, dot_nt(fob_ref[...], d_f), 0.0).astype(BF16)
        part_ref[:, c0:c1] += dot_nn(f_delta, whole)
        part_ref[:, c1:c2] += dot_nn(f_hid, d_f)
        b_pre = dot_nt(wbb_ref[...], later)
        b_hid = jnp.maximum(b_pre, 0.0).astype(BF16)
        b_delta = jnp.where(b_pre > 0, dot_nt(bob_ref[...], d_u), 0.0).astype(BF16)
        part_ref[:, c2:c3] += dot_nn(b_delta, later)
        part_ref[:, c3:] += dot_nn(b_hid, d_u)
        return square, diagonal

    line = jnp.zeros((1, rank), F32)
    square, diagonal = lax.fori_loop(0, steps, backward, (line, line))
    loss = (0.5 / group) * jnp.sum(square) - jnp.sum(diagonal)
    loss_ref[...] = jnp.full(loss_ref.shape, loss, F32)
    core = lax.rem(lax.axis_index("replica"), 2)
    half = block // 2
    mine = pl.multiple_of(core * half, ROW_TILE)
    other = pl.multiple_of((1 - core) * half, ROW_TILE)
    keep_ref[...] = part_ref[pl.ds(mine, half), :]
    send_ref[...] = part_ref[pl.ds(other, half), :].astype(BF16)


def finish_kernel(cfg, low_ref, high_ref, fs_ref, fa_ref, fl_ref, fo_ref, bs_ref, bo_ref, full_ref):
    obs, act, rank, x_pad = cfg["obs"], cfg["act"], cfg["rank"], cfg["x_pad"]
    half = cfg["block"] // 2
    c0, c1, c2, c3 = cfg["cols"]
    core = lax.rem(lax.axis_index("replica"), 2)
    mine = pl.multiple_of(core * half, ROW_TILE)
    other = pl.multiple_of((1 - core) * half, ROW_TILE)
    full_ref[pl.ds(mine, half), :] = low_ref[...].astype(F32)
    full_ref[pl.ds(other, half), :] = high_ref[...].astype(F32)
    front = full_ref[:, :x_pad].T
    fs_ref[...] = front[:obs].astype(BF16)
    fa_ref[...] = front[obs : obs + act].astype(BF16)
    fl_ref[...] = full_ref[:, x_pad:c1].T.astype(BF16)
    fo_ref[...] = full_ref[:, c1:c2].astype(BF16)
    bs_ref[...] = full_ref[:, c2:c3].T[:obs].astype(BF16)
    bo_ref[...] = full_ref[:, c3:].astype(BF16)


def exchange(array, axis, size, bit):
    return lax.ppermute(array, axis, [(i, i ^ bit) for i in range(size)])


def gather_chunks(own, size):
    found = {0: own}
    bit = size // 2
    wide = [step for step in range(2, size, 2)]
    found[1] = exchange(own, "dp", size, 1)
    for step in wide:
        found[step] = exchange(own, "dp", size, step)
    for step in wide:
        found[step ^ 1] = exchange(found[step], "dp", size, 1)
    return [found[j] for j in range(size)]


def fast_local(
    states,
    actions,
    target_forward,
    next_index,
    latent_ids,
    latents,
    f_state,
    f_action,
    f_latent,
    f_output,
    b_state,
    b_output,
):
    size = lax.axis_size("dp")
    replicas = lax.axis_size("replica")
    rows, obs = states.shape[1:]
    act = actions.shape[2]
    zcount, rank = latents.shape
    hidden = f_state.shape[1]
    block = hidden // size
    group = rows * size
    total = group * replicas
    x_pad = round_up(obs + act + 2, LANES)
    obs_pad = round_up(obs, LANES)
    c1 = x_pad + rank
    c2 = c1 + rank
    c3 = c2 + obs_pad
    width = c3 + rank
    cfg = dict(
        chunks=size,
        rows=rows,
        obs=obs,
        act=act,
        rank=rank,
        obs_pad=obs_pad,
        x_pad=x_pad,
        hidden=hidden,
        zcount=zcount,
        group=group,
        total=total,
        block=block,
        tile=512,
        inner=2,
        cols=(0, c1, c2, c3),
    )
    own = jnp.concatenate(
        [
            states[0],
            actions[0],
            next_index[0][:, None].astype(BF16),
            latent_ids[0][:, None].astype(BF16),
            jnp.zeros((rows, x_pad - obs - act - 2), BF16),
            target_forward[0],
        ],
        axis=1,
    )
    xs = gather_chunks(own, size)
    wf = jnp.concatenate(
        [f_state, f_action, jnp.zeros((x_pad - obs - act, hidden), BF16), f_latent], axis=0
    )
    wb = jnp.concatenate([b_state, jnp.zeros((obs_pad - obs, hidden), BF16)], axis=0)
    start = lax.axis_index("dp") * block
    wfb = lax.dynamic_slice_in_dim(wf, start, block, 1).T
    wbb = lax.dynamic_slice_in_dim(wb, start, block, 1).T
    fob = lax.dynamic_slice_in_dim(f_output, start, block, 0)
    bob = lax.dynamic_slice_in_dim(b_output, start, block, 0)
    flops = 2 * group * (c1 + 2 * rank + obs_pad) * hidden
    send, keep, loss = pl.pallas_call(
        functools.partial(step_kernel, cfg),
        out_shape=(
            jax.ShapeDtypeStruct((block // 2, width), BF16),
            jax.ShapeDtypeStruct((block // 2, width), F32),
            jax.ShapeDtypeStruct((8, LANES), F32),
        ),
        scratch_shapes=[
            pltpu.VMEM((group, x_pad + rank), BF16),
            pltpu.VMEM((group, obs_pad), BF16),
            pltpu.VMEM((group, rank), BF16),
            pltpu.VMEM((group, rank), BF16),
            pltpu.VMEM((group, rank), F32),
            pltpu.VMEM((group, rank), BF16),
            pltpu.VMEM((block, width), F32),
        ],
        compiler_params=pltpu.CompilerParams(vmem_limit_bytes=VMEM_LIMIT),
        cost_estimate=pl.CostEstimate(
            flops=flops, bytes_accessed=12_000_000, transcendentals=2 * group
        ),
        name="step",
    )(*xs, wf, wb, f_output, b_output, latents, wfb, wbb, fob, bob)
    got = exchange(send, "replica", replicas, 1)
    loss = loss + exchange(loss, "replica", replicas, 1)
    first = (keep + got.astype(F32)).astype(BF16)
    second = exchange(first, "replica", replicas, 2)
    loss = loss + exchange(loss, "replica", replicas, 2)
    mine = (first.astype(F32) + second.astype(F32)).astype(BF16)
    other = exchange(mine, "replica", replicas, 1)
    outs = pl.pallas_call(
        functools.partial(finish_kernel, cfg),
        out_shape=(
            jax.ShapeDtypeStruct((obs, block), BF16),
            jax.ShapeDtypeStruct((act, block), BF16),
            jax.ShapeDtypeStruct((rank, block), BF16),
            jax.ShapeDtypeStruct((block, rank), BF16),
            jax.ShapeDtypeStruct((obs, block), BF16),
            jax.ShapeDtypeStruct((block, rank), BF16),
        ),
        scratch_shapes=[pltpu.VMEM((block, width), F32)],
        compiler_params=pltpu.CompilerParams(vmem_limit_bytes=16 * 1024 * 1024),
        name="finish",
    )(mine, other)
    return (*outs, loss[0, 0] / total)


def forward_pass(
    current, later, moves, latent_rows, f_state, f_action, f_latent, f_output, b_state, b_output
):
    f_pre = (
        jnp.dot(current, f_state, preferred_element_type=F32)
        + jnp.dot(moves, f_action, preferred_element_type=F32)
        + jnp.dot(latent_rows, f_latent, preferred_element_type=F32)
    )
    f_hidden = jnp.maximum(f_pre, 0.0).astype(BF16)
    forward_emb = jnp.dot(f_hidden, f_output, preferred_element_type=F32).astype(BF16)
    b_pre = jnp.dot(later, b_state, preferred_element_type=F32)
    b_hidden = jnp.maximum(b_pre, 0.0).astype(BF16)
    b_raw = jnp.dot(b_hidden, b_output, preferred_element_type=F32)
    b_scale = lax.rsqrt(jnp.mean(b_raw * b_raw, axis=-1, keepdims=True) + EPSILON)
    backward_emb = (b_raw * b_scale).astype(BF16)
    return (f_pre, f_hidden, forward_emb, b_pre, b_hidden, b_raw, b_scale, backward_emb)


def general_local(
    states,
    actions,
    target_forward,
    next_index,
    latent_ids,
    latents,
    f_state,
    f_action,
    f_latent,
    f_output,
    b_state,
    b_output,
):
    current = states[0]
    moves = actions[0]
    later = jnp.take(current, next_index[0], axis=0)
    latent_rows = jnp.take(latents, latent_ids[0], axis=0)
    f_pre, f_hidden, forward_emb, b_pre, b_hidden, b_raw, b_scale, backward_emb = forward_pass(
        current, later, moves, latent_rows, f_state, f_action, f_latent, f_output, b_state, b_output
    )
    group = current.shape[0] * lax.axis_size("dp")
    total = group * lax.axis_size("replica")
    factor = 1.0 / math.sqrt(total)
    forward32 = forward_emb.astype(F32)
    back32 = backward_emb.astype(F32)
    error = forward32 - GAMMA * target_forward[0].astype(F32)
    gram, cross = lax.psum(
        (
            jnp.dot(backward_emb.T, backward_emb, preferred_element_type=F32),
            jnp.dot(forward32.T, error, precision=HIGH, preferred_element_type=F32),
        ),
        "dp",
    )
    pulled = jnp.dot(error, gram, precision=HIGH, preferred_element_type=F32)
    pushed = jnp.dot(back32, cross.T, precision=HIGH, preferred_element_type=F32)
    partial_loss = 0.5 / group * jnp.sum(pulled * error) - jnp.sum(forward32 * back32)
    grad_forward = (factor * (pulled / group - back32)).astype(BF16)
    grad_backward = factor * (pushed / group - forward32)
    inner = jnp.mean(b_raw * grad_backward, axis=-1, keepdims=True)
    grad_raw = (b_scale * grad_backward - b_raw * b_scale * b_scale * b_scale * inner).astype(BF16)
    part_bo = jnp.dot(b_hidden.T, grad_raw, preferred_element_type=F32)
    b_back = jnp.dot(grad_raw, b_output.T, preferred_element_type=F32)
    b_delta = jnp.where(b_pre > 0, b_back, 0.0).astype(BF16)
    part_bs = jnp.dot(later.T, b_delta, preferred_element_type=F32)
    part_fo = jnp.dot(f_hidden.T, grad_forward, preferred_element_type=F32)
    f_back = jnp.dot(grad_forward, f_output.T, preferred_element_type=F32)
    f_delta = jnp.where(f_pre > 0, f_back, 0.0).astype(BF16)
    part_fs = jnp.dot(current.T, f_delta, preferred_element_type=F32)
    part_fa = jnp.dot(moves.T, f_delta, preferred_element_type=F32)
    part_fl = jnp.dot(latent_rows.T, f_delta, preferred_element_type=F32)
    places = (1, 1, 1, 0, 1, 0)
    parts = (part_fs, part_fa, part_fl, part_fo, part_bs, part_bo)
    shares = tuple(
        lax.psum_scatter(part, "dp", scatter_dimension=place, tiled=True)
        for part, place in zip(parts, places)
    )
    summed = lax.psum(shares, "replica")
    loss_sum = lax.psum(partial_loss, ("dp", "replica"))
    return (*(item.astype(BF16) for item in summed), loss_sum / total)


def local(*args):
    size, replicas = lax.axis_size("dp"), lax.axis_size("replica")
    rows, hidden = args[0].shape[1], args[6].shape[1]
    fits = size == 8 and replicas == 4 and rows * size <= KERNEL_GROUP_LIMIT
    whole = rows % ROW_TILE == 0 and hidden % (size * 2 * ROW_TILE) == 0 and hidden % 512 == 0
    exact = rows <= 256 and args[5].shape[0] <= 256
    return (fast_local if fits and whole and exact else general_local)(*args)


def solution(mesh):
    in_specs = (
        P("replica", "dp", None),
        P("replica", "dp", None),
        P("replica", "dp", None),
        P("replica", "dp"),
        P("replica", "dp"),
        P(),
        P(),
        P(),
        P(),
        P(),
        P(),
        P(),
    )
    out_specs = (
        P(None, "dp"),
        P(None, "dp"),
        P(None, "dp"),
        P("dp", None),
        P(None, "dp"),
        P("dp", None),
        P(),
    )
    return jax.shard_map(local, mesh=mesh, in_specs=in_specs, out_specs=out_specs, check_vma=False)
```

time: 572 us -> 101 us (0.18)
  waiting for transfers between devices: 406 us -> 32.7 us
  blocking collectives: 103 us -> 0 us
  Pallas kernels: 0 us -> 25.6 us
  matrix products: 20.5 us -> 0 us
  between operations: 17.5 us -> 2.53 us
  starting transfers between devices: 0.29 us -> 13.3 us
    reduce_scatter x5 -> x0, waiting for transfers between devices: 278 us -> none  [the longest x1 71.8 us: local(): lax.psum_scatter(part_bs, 'dp', scatter_dimension=1, tiled=True)]
    unnamed x9 -> x0, waiting for transfers between devices: 128 us -> none
    psum x2 -> x0, blocking collectives: 69.2 us -> none  [the longest x1 40.4 us: local(): loss_sum = lax.psum(partial_loss, ('dp', 'replica'))]
    all_gather x1 -> x0, blocking collectives: 33.8 us -> none  [local(): everyone = lax.all_gather(backward_emb, 'dp', axis=0, tiled=True)]
    ppermute x0 -> x12, waiting for transfers between devices: none -> 32.7 us  [exchange(): return lax.ppermute(array, axis, [(i, i ^ bit) for i in range(size)])]
    pallas_call x0 -> x2, Pallas kernels: none -> 25.6 us  [the longest x1 24.6 us: fast_local(): pl.pallas_call(functools.partial(step_kernel, cfg), out_shape=(jax.ShapeD...]
    dot_general x17 -> x0, matrix products: 20.5 us -> none  [the longest x1 2.68 us: local(): jnp.dot(scores.T, forward32, precision=HIGH, preferred_element_type=jnp.f...]
    ppermute x0 -> x12, starting transfers between devices: none -> 13.3 us  [exchange(): return lax.ppermute(array, axis, [(i, i ^ bit) for i in range(size)])]
  transfers between devices with their start and end apart: 7 -> 12, of which waited for: 7 -> 7; matrix products, arithmetic and copies ran while one was open for 4% -> 17% of each run, Pallas kernels for 0% -> 0%
where the time goes in v1:
time: 101 us; the launch traced here: 100 us
  waiting for transfers between devices  32.7 us (32%)
  Pallas kernels  25.6 us (25%)
  local copies, waits for them, and re-layouts  20.2 us (20%)
  starting transfers between devices  13.3 us (13%)
  other arithmetic  5.73 us (6%)
  between operations  2.53 us (3%)
    ppermute x12, waiting for transfers between devices, exchange(): return lax.ppermute(array, axis, [(i, i ^ bit) for i in range(size)])  32.7 us
    pallas_call x1, Pallas kernels, fast_local(): pl.pallas_call(functools.partial(step_kernel, cfg), out_shape=(jax.ShapeD...  24.6 us
    ppermute x12, starting transfers between devices, exchange(): return lax.ppermute(array, axis, [(i, i ^ bit) for i in range(size)])  13.3 us
    unnamed x19, local copies, waits for them, and re-layouts  10.8 us
    concatenate x2, local copies, waits for them, and re-layouts, fast_local(): jnp.concatenate([f_state, f_action, jnp.zeros((x_pad - obs - act, hidden)...  2.52 us
    concatenate x1, other arithmetic, fast_local(): jnp.concatenate([f_state, f_action, jnp.zeros((x_pad - obs - act, hidden)...  2.35 us
  transfers between devices with their start and end apart: 12, of which 7 were waited for; matrix products, arithmetic and copies ran while one was open for 17% of the time, Pallas kernels for 0%

profile of v1, /device:TPU:0, one launch (start us, length us, event | category | flops | bytes accessed | tf_op | source)
XLA Modules:
  0.0 100.1 jit_solution(4518060928827645515)
XLA Ops:
  2.4 0.8 copy.29
  3.3 1.8 %concatenate.9.refs_0_ = bf16[192,768]{1,0:T(8,128)(2,1)} concatenate(bf16[192,376]{1,0:T(8,128)(2,1)} %bitcast.13, bf16[192,17]{1,0:T(8,128)(2,1)S(1)} %bitcast.12, bf16[192,1]{1,0:T(8,128)(2,1)S(1)} %copy.30, bf16[192,1]{1,0:T(8,128)(2,1)S(1)} %copy.31, bf16[192,117]{1,0:T(8,128)(2,1)S(1)} %broadcast_in_dim.7, bf16[192,256]{1,0:T(8,128)(2,1)} %bitcast.14), dimensions={1} | concatenate | bytes 589824 | tf_op jit(solution)/shard_map/concatenate | solution.py:256
  5.1 5.0 %collective-permute-start.5 = (bf16[192,768]{1,0:T(8,128)(2,1)}, bf16[192,768]{1,0:T(8,128)(2,1)}, u32[]{:S(2)}, u32[]{:S(2)}) collective-permute-start(bf16[192,768]{1,0:T(8,128)(2,1)} %concatenate.9.refs_0_), channel_id=1, source_target_pairs={{0,24},{4,28},{8,16},{12,20},{16,8},{20,12},{24,0},{28,4},{1,25},{... | collective-permute-start | bytes 884744 | tf_op jit(solution)/shard_map/ppermute | solution.py:195
  10.7 1.7 %collective-permute-start = (bf16[192,768]{1,0:T(8,128)(2,1)}, bf16[192,768]{1,0:T(8,128)(2,1)}, u32[]{:S(2)}, u32[]{:S(2)}) collective-permute-start(bf16[192,768]{1,0:T(8,128)(2,1)} %concatenate.9.refs_0_), channel_id=1, source_target_pairs={{0,4},{4,0},{8,12},{12,8},{16,20},{20,16},{24,28},{28,24},{1,5},{5... | collective-permute-start | bytes 884744 | tf_op jit(solution)/shard_map/ppermute | solution.py:195
  12.4 1.8 %copy.33 = bf16[17,1536]{0,1:T(8,128)(2,1)} copy(bf16[17,1536]{1,0:T(8,128)(2,1)} %param.19) | data formatting | bytes 104448 | tf_op args[7]
  14.3 2.3 %copy.34 = bf16[256,1536]{0,1:T(8,128)(2,1)} copy(bf16[256,1536]{1,0:T(8,128)(2,1)} %param.20) | data formatting | bytes 1572864 | tf_op args[8]
  18.0 1.1 %concatenate.11.clone.refs_9_ = bf16[384,1536]{1,0:T(8,128)(2,1)} pad(bf16[376,1536]{1,0:T(8,128)(2,1)S(1)} %copy.41, bf16[]{:T(256)} %constant.7.clone.1), padding=0_8x0_0 | pad | bytes 2334722 | tf_op jit(solution)/shard_map/concatenate | solution.py:271
  19.1 1.4 %copy.32 = bf16[376,1536]{0,1:T(8,128)(2,1)} copy(bf16[376,1536]{1,0:T(8,128)(2,1)S(1)} %copy-done.1) | data formatting | bytes 2310144 | tf_op args[6]
  20.6 2.3 %pad_maximum_fusion = bf16[768,1536]{0,1:T(8,128)(2,1)S(1)} fusion(bf16[256,1536]{0,1:T(8,128)(2,1)} %copy.34, bf16[17,1536]{0,1:T(8,128)(2,1)} %copy.33, bf16[376,1536]{0,1:T(8,128)(2,1)} %copy.32, bf16[768]{0:T(1024)(128)(2,1)S(1)} %pad.3.clone), kind=kLoop, calls=%fused_computation | loop fusion | flops 9437184 | bytes 4354560 | tf_op jit(solution)/shard_map/concatenate | solution.py:268
  22.9 2.4 %copy.36.refs_8_ = bf16[768,1536]{1,0:T(8,128)(2,1)} copy(bf16[768,1536]{0,1:T(8,128)(2,1)S(1)} %pad_maximum_fusion) | data formatting | bytes 4718592 | tf_op jit(solution)/shard_map/concatenate | solution.py:268
  25.7 9.9 %collective-permute-done.3.refs_4_ = bf16[192,768]{1,0:T(8,128)(2,1)} collective-permute-done((bf16[192,768]{1,0:T(8,128)(2,1)}, bf16[192,768]{1,0:T(8,128)(2,1)}, u32[]{:S(2)}, u32[]{:S(2)}) %collective-permute-start.3) | collective-permute-done | bytes 294944 | tf_op jit(solution)/shard_map/ppermute | solution.py:195
  35.6 1.5 %collective-permute-start.4 = (bf16[192,768]{1,0:T(8,128)(2,1)}, bf16[192,768]{1,0:T(8,128)(2,1)S(1)}, u32[]{:S(2)}, u32[]{:S(2)}) collective-permute-start(bf16[192,768]{1,0:T(8,128)(2,1)} %collective-permute-done.3.refs_4_), channel_id=1, source_target_pairs={{0,4},{4,0},{8,12},{12,8},{16,20},{20,16},{24,28},{28,24},{1,5},{5... | collective-permute-start | bytes 884744 | tf_op jit(solution)/shard_map/ppermute | solution.py:195
  38.3 1.6 %constant_dynamic-slice_fusion = (bf16[192,256]{1,0:T(8,128)(2,1)}, bf16[192,256]{1,0:T(8,128)(2,1)}) fusion(bf16[1536,256]{1,0:T(8,128)(2,1)} %refs_11_.1, s32[]{:T(128)S(6)} %select_n.2, bf16[1536,256]{1,0:T(8,128)(2,1)} %refs_10_.1), kind=kLoop, calls=%fused_computation.5 | loop fusion | bytes 393220 | tf_op jit(solution)/shard_map/dynamic_slice | solution.py:276
  40.7 5.1 %collective-permute-done.4.refs_5_ = bf16[192,768]{1,0:T(8,128)(2,1)S(1)} collective-permute-done((bf16[192,768]{1,0:T(8,128)(2,1)}, bf16[192,768]{1,0:T(8,128)(2,1)S(1)}, u32[]{:S(2)}, u32[]{:S(2)}) %collective-permute-start.4) | collective-permute-done | bytes 294944 | tf_op jit(solution)/shard_map/ppermute | solution.py:195
  45.8 4.4 %collective-permute-done.2.refs_3_ = bf16[192,768]{1,0:T(8,128)(2,1)S(1)} collective-permute-done((bf16[192,768]{1,0:T(8,128)(2,1)}, bf16[192,768]{1,0:T(8,128)(2,1)S(1)}, u32[]{:S(2)}, u32[]{:S(2)}) %collective-permute-start.2) | collective-permute-done | bytes 294944 | tf_op jit(solution)/shard_map/ppermute | solution.py:195
  50.9 24.6 %step.1 = (bf16[96,1664]{1,0:T(8,128)(2,1)}, f32[96,1664]{1,0:T(8,128)}, f32[8,128]{1,0:T(8,128)}) custom-call(bf16[192,768]{1,0:T(8,128)(2,1)} %concatenate.9.refs_0_, bf16[192,768]{1,0:T(8,128)(2,1)} %collective-permute-done.refs_1_, bf16[192,768]{1,0:T(8,128)(2,1)} %collective-permute-done.1.refs_2_, bf16[192,768]{1,0:T(8,128)(2,1)} %copy-done.4, ...), custom_call_target="tpu_custom_call" | custom-call | flops 7851737088 | bytes 12000000 | tf_op jit(solution)/shard_map/step/pallas_call | solution.py:278
  75.5 1.8 %collective-permute-done.7 = bf16[96,1664]{1,0:T(8,128)(2,1)S(1)} collective-permute-done((bf16[96,1664]{1,0:T(8,128)(2,1)}, bf16[96,1664]{1,0:T(8,128)(2,1)S(1)}, u32[]{:S(2)}, u32[]{:S(2)}) %collective-permute-start.7) | collective-permute-done | bytes 319520 | tf_op jit(solution)/shard_map/ppermute | solution.py:195
  77.4 1.1 %add_convert_fusion.1 = bf16[96,1664]{1,0:T(8,128)(2,1)S(1)} fusion(f32[96,1664]{1,0:T(8,128)} %get-tuple-element.16, bf16[96,1664]{1,0:T(8,128)(2,1)S(1)} %collective-permute-done.7), kind=kLoop, calls=%fused_computation.2 | loop fusion | flops 479232 | bytes 1277952 | tf_op jit(solution)/shard_map/convert_element_type | solution.py:302
  78.5 1.6 %collective-permute-start.8 = (bf16[96,1664]{1,0:T(8,128)(2,1)S(1)}, bf16[96,1664]{1,0:T(8,128)(2,1)S(1)}, u32[]{:S(2)}, u32[]{:S(2)}) collective-permute-start(bf16[96,1664]{1,0:T(8,128)(2,1)S(1)} %add_convert_fusion.1), channel_id=1, source_target_pairs={{0,2},{1,3},{2,0},{3,1},{4,6},{5,7},{6,4},{7,5},{8,10},{9,11},{10,... | collective-permute-start | bytes 958472 | tf_op jit(solution)/shard_map/ppermute | solution.py:195
  80.1 8.1 %collective-permute-done.8 = bf16[96,1664]{1,0:T(8,128)(2,1)S(1)} collective-permute-done((bf16[96,1664]{1,0:T(8,128)(2,1)S(1)}, bf16[96,1664]{1,0:T(8,128)(2,1)S(1)}, u32[]{:S(2)}, u32[]{:S(2)}) %collective-permute-start.8) | collective-permute-done | bytes 319520 | tf_op jit(solution)/shard_map/ppermute | solution.py:195
  88.8 1.3 %collective-permute-done.10 = f32[8,128]{1,0:T(8,128)S(1)} collective-permute-done((f32[8,128]{1,0:T(8,128)}, f32[8,128]{1,0:T(8,128)S(1)}, u32[]{:S(2)}, u32[]{:S(2)}) %collective-permute-start.10) | collective-permute-done | bytes 4128 | tf_op jit(solution)/shard_map/ppermute | solution.py:195
  90.8 1.5 %collective-permute-start.11 = (f32[8,128]{1,0:T(8,128)S(1)}, f32[8,128]{1,0:T(8,128)S(1)}, u32[]{:S(2)}, u32[]{:S(2)}) collective-permute-start(f32[8,128]{1,0:T(8,128)S(1)} %add.23), channel_id=1, source_target_pairs={{0,2},{1,3},{2,0},{3,1},{4,6},{5,7},{6,4},{7,5},{8,10},{9,11},{10,... | collective-permute-start | bytes 12296 | tf_op jit(solution)/shard_map/ppermute | solution.py:195
  92.3 2.1 %collective-permute-done.11 = f32[8,128]{1,0:T(8,128)S(1)} collective-permute-done((f32[8,128]{1,0:T(8,128)S(1)}, f32[8,128]{1,0:T(8,128)S(1)}, u32[]{:S(2)}, u32[]{:S(2)}) %collective-permute-start.11) | collective-permute-done | bytes 4128 | tf_op jit(solution)/shard_map/ppermute | solution.py:195
  95.6 1.0 %finish.1 = (bf16[376,192]{1,0:T(8,128)(2,1)S(1)}, bf16[17,192]{1,0:T(8,128)(2,1)}, bf16[256,192]{1,0:T(8,128)(2,1)S(1)}, bf16[192,256]{1,0:T(8,128)(2,1)}, bf16...) custom-call(bf16[96,1664]{1,0:T(8,128)(2,1)S(1)} %add_convert_fusion.low_ref, ...), custom_call_target="tpu_custom_call" | custom-call | tf_op jit(solution)/shard_map/finish/pallas_call | solution.py:307
  (40 shorter events, 11.0 us)
Async XLA Ops:
  0.6 15.9 %copy-start = (bf16[376,1536]{1,0:T(8,128)(2,1)S(1)}, bf16[376,1536]{1,0:T(8,128)(2,1)}, u32[]{:S(2)}) copy-start(bf16[376,1536]{1,0:T(8,128)(2,1)} %param.22) | copy-start | bytes 3465220
  5.1 20.3 %collective-permute-start.5 = (bf16[192,768]{1,0:T(8,128)(2,1)}, bf16[192,768]{1,0:T(8,128)(2,1)}, u32[]{:S(2)}, u32[]{:S(2)}) collective-permute-start(bf16[192,768]{1,0:T(8,128)(2,1)} %concatenate.9.refs_0_), channel_id=1, source_target_pairs={{0,24},{4,28},{8,16},{12,20},{16,8},{20,12},{24,0},{28,4},{1,25},{... | collective-permute-start | bytes 884744 | tf_op jit(solution)/shard_map/ppermute | solution.py:195
  10.2 25.4 %collective-permute-start.3 = (bf16[192,768]{1,0:T(8,128)(2,1)}, bf16[192,768]{1,0:T(8,128)(2,1)}, u32[]{:S(2)}, u32[]{:S(2)}) collective-permute-start(bf16[192,768]{1,0:T(8,128)(2,1)} %concatenate.9.refs_0_), channel_id=1, source_target_pairs={{0,16},{4,20},{8,24},{12,28},{16,0},{20,4},{24,8},{28,12},{1,17},{... | collective-permute-start | bytes 884744 | tf_op jit(solution)/shard_map/ppermute | solution.py:195
  10.2 26.9 %collective-permute-start.1 = (bf16[192,768]{1,0:T(8,128)(2,1)}, bf16[192,768]{1,0:T(8,128)(2,1)}, u32[]{:S(2)}, u32[]{:S(2)}) collective-permute-start(bf16[192,768]{1,0:T(8,128)(2,1)} %concatenate.9.refs_0_), channel_id=1, source_target_pairs={{0,8},{4,12},{8,0},{12,4},{16,24},{20,28},{24,16},{28,20},{1,9},{5... | collective-permute-start | bytes 884744 | tf_op jit(solution)/shard_map/ppermute | solution.py:195
  10.7 30.0 %collective-permute-start = (bf16[192,768]{1,0:T(8,128)(2,1)}, bf16[192,768]{1,0:T(8,128)(2,1)}, u32[]{:S(2)}, u32[]{:S(2)}) collective-permute-start(bf16[192,768]{1,0:T(8,128)(2,1)} %concatenate.9.refs_0_), channel_id=1, source_target_pairs={{0,4},{4,0},{8,12},{12,8},{16,20},{20,16},{24,28},{28,24},{1,5},{5... | collective-permute-start | bytes 884744 | tf_op jit(solution)/shard_map/ppermute | solution.py:195
  17.3 1.8 %copy-start.1 = (bf16[376,1536]{1,0:T(8,128)(2,1)S(1)}, bf16[376,1536]{1,0:T(8,128)(2,1)}, u32[]{:S(2)}) copy-start(bf16[376,1536]{1,0:T(8,128)(2,1)} %param.18) | copy-start | bytes 3465220
  25.4 15.3 %collective-permute-start.6 = (bf16[192,768]{1,0:T(8,128)(2,1)}, bf16[192,768]{1,0:T(8,128)(2,1)S(1)}, u32[]{:S(2)}, u32[]{:S(2)}) collective-permute-start(bf16[192,768]{1,0:T(8,128)(2,1)} %collective-permute-done.5.refs_6_), channel_id=1, source_target_pairs={{0,4},{4,0},{8,12},{12,8},{16,20},{20,16},{24,28},{28,24},{1,5},{5... | collective-permute-start | bytes 884744 | tf_op jit(solution)/shard_map/ppermute | solution.py:195
  35.6 10.2 %collective-permute-start.4 = (bf16[192,768]{1,0:T(8,128)(2,1)}, bf16[192,768]{1,0:T(8,128)(2,1)S(1)}, u32[]{:S(2)}, u32[]{:S(2)}) collective-permute-start(bf16[192,768]{1,0:T(8,128)(2,1)} %collective-permute-done.3.refs_4_), channel_id=1, source_target_pairs={{0,4},{4,0},{8,12},{12,8},{16,20},{20,16},{24,28},{28,24},{1,5},{5... | collective-permute-start | bytes 884744 | tf_op jit(solution)/shard_map/ppermute | solution.py:195
  37.1 13.1 %collective-permute-start.2 = (bf16[192,768]{1,0:T(8,128)(2,1)}, bf16[192,768]{1,0:T(8,128)(2,1)S(1)}, u32[]{:S(2)}, u32[]{:S(2)}) collective-permute-start(bf16[192,768]{1,0:T(8,128)(2,1)} %collective-permute-done.1.refs_2_), channel_id=1, source_target_pairs={{0,4},{4,0},{8,12},{12,8},{16,20},{20,16},{24,28},{28,24},{1,5},{5... | collective-permute-start | bytes 884744 | tf_op jit(solution)/shard_map/ppermute | solution.py:195
  40.7 9.5 %copy-start.2 = (bf16[192,768]{1,0:T(8,128)(2,1)}, bf16[192,768]{1,0:T(8,128)(2,1)S(1)}, u32[]{:S(2)}) copy-start(bf16[192,768]{1,0:T(8,128)(2,1)S(1)} %collective-permute-done.6.refs_7_) | copy-start | bytes 884740
  45.8 4.4 %copy-start.3 = (bf16[192,768]{1,0:T(8,128)(2,1)}, bf16[192,768]{1,0:T(8,128)(2,1)S(1)}, u32[]{:S(2)}) copy-start(bf16[192,768]{1,0:T(8,128)(2,1)S(1)} %collective-permute-done.4.refs_5_) | copy-start | bytes 884740
  50.2 0.7 copy-start.4
  75.5 1.8 %collective-permute-start.7 = (bf16[96,1664]{1,0:T(8,128)(2,1)}, bf16[96,1664]{1,0:T(8,128)(2,1)S(1)}, u32[]{:S(2)}, u32[]{:S(2)}) collective-permute-start(bf16[96,1664]{1,0:T(8,128)(2,1)} %get-tuple-element.17), channel_id=1, source_target_pairs={{0,1},{1,0},{2,3},{3,2},{4,5},{5,4},{6,7},{7,6},{8,9},{9,8},{10,11... | collective-permute-start | bytes 958472 | tf_op jit(solution)/shard_map/ppermute | solution.py:195
  78.5 9.6 %collective-permute-start.8 = (bf16[96,1664]{1,0:T(8,128)(2,1)S(1)}, bf16[96,1664]{1,0:T(8,128)(2,1)S(1)}, u32[]{:S(2)}, u32[]{:S(2)}) collective-permute-start(bf16[96,1664]{1,0:T(8,128)(2,1)S(1)} %add_convert_fusion.1), channel_id=1, source_target_pairs={{0,2},{1,3},{2,0},{3,1},{4,6},{5,7},{6,4},{7,5},{8,10},{9,11},{10,... | collective-permute-start | bytes 958472 | tf_op jit(solution)/shard_map/ppermute | solution.py:195
  88.2 7.4 %collective-permute-start.9 = (bf16[96,1664]{1,0:T(8,128)(2,1)S(1)}, bf16[96,1664]{1,0:T(8,128)(2,1)S(1)}, u32[]{:S(2)}, u32[]{:S(2)}) collective-permute-start(bf16[96,1664]{1,0:T(8,128)(2,1)S(1)} %add_convert_fusion.low_ref), channel_id=1, source_target_pairs={{0,1},{1,0},{2,3},{3,2},{4,5},{5,4},{6,7},{7,6},{8,9},{9,8},{10,11... | collective-permute-start | bytes 958472 | tf_op jit(solution)/shard_map/ppermute | solution.py:195
  88.3 1.8 %collective-permute-start.10 = (f32[8,128]{1,0:T(8,128)}, f32[8,128]{1,0:T(8,128)S(1)}, u32[]{:S(2)}, u32[]{:S(2)}) collective-permute-start(f32[8,128]{1,0:T(8,128)} %get-tuple-element.24), channel_id=1, source_target_pairs={{0,1},{1,0},{2,3},{3,2},{4,5},{5,4},{6,7},{7,6},{8,9},{9,8},{10,11... | collective-permute-start | bytes 12296 | tf_op jit(solution)/shard_map/ppermute | solution.py:195
  90.8 3.6 %collective-permute-start.11 = (f32[8,128]{1,0:T(8,128)S(1)}, f32[8,128]{1,0:T(8,128)S(1)}, u32[]{:S(2)}, u32[]{:S(2)}) collective-permute-start(f32[8,128]{1,0:T(8,128)S(1)} %add.23), channel_id=1, source_target_pairs={{0,2},{1,3},{2,0},{3,1},{4,6},{5,7},{6,4},{7,5},{8,10},{9,11},{10,... | collective-permute-start | bytes 12296 | tf_op jit(solution)/shard_map/ppermute | solution.py:195

commit v2 on v1

v2 whole, which is shorter than its diff:
```python
import functools
import math

import jax
import jax.numpy as jnp
from jax import lax
from jax.experimental import pallas as pl
from jax.experimental.pallas import tpu as pltpu
from jax.sharding import PartitionSpec as P

GAMMA = 0.98
EPSILON = 1e-06
HIGH = lax.Precision.HIGHEST
BF16 = jnp.bfloat16
F32 = jnp.float32
LANES = 128
ROW_TILE = 16
VMEM_LIMIT = 56 * 1024 * 1024
KERNEL_GROUP_LIMIT = 2048


def round_up(value, unit):
    return -(-value // unit) * unit


def dot_nn(left, right):
    return lax.dot_general(left, right, (((1,), (0,)), ((), ())), preferred_element_type=F32)


def dot_nt(left, right):
    return lax.dot_general(left, right, (((1,), (1,)), ((), ())), preferred_element_type=F32)


def dot_tn(left, right):
    return lax.dot_general(left, right, (((0,), (0,)), ((), ())), preferred_element_type=F32)


def split_two(value):
    high = value.astype(BF16)
    return high, (value - high.astype(F32)).astype(BF16)


def pack_kernel(cfg, state_ref, move_ref, next_ref, latent_ref, target_ref, out_ref, side_ref):
    rows, obs, act, obs_pad, side = (cfg[k] for k in ("rows", "obs", "act", "obs_pad", "side"))
    lane = side_ref.shape[1]
    side_ref[...] = jnp.zeros_like(side_ref)
    side_ref[0:act, 0:rows] = move_ref[...].astype(F32)
    side_ref[act : act + 1, 0:rows] = next_ref[...].astype(F32)
    side_ref[act + 1 : act + 2, 0:rows] = latent_ref[...].astype(F32)
    gap = jnp.zeros((rows, obs_pad - obs), BF16)
    out_ref[0:rows, 0:obs_pad] = jnp.concatenate([state_ref[0], gap], axis=1)
    out_ref[0:rows, obs_pad:] = target_ref[0]
    half = side // 2
    out_ref[rows:, :] = jnp.zeros((half, out_ref.shape[1]), BF16)
    out_ref[rows:, 0:lane] = side_ref[0:half, :].astype(BF16)
    out_ref[rows:, lane : 2 * lane] = side_ref[half:side, :].astype(BF16)


def weights_kernel(cfg, fs_ref, fa_ref, fl_ref, bs_ref, wf_ref, wb_ref, wfb_ref, wbb_ref):
    obs, obs_pad, x_pad = cfg["obs"], cfg["obs_pad"], cfg["x_pad"]
    hidden, block, act = cfg["hidden"], cfg["block"], cfg["act"]
    gap = jnp.zeros((obs_pad - obs, hidden), BF16)
    wf_ref[0:obs_pad, :] = jnp.concatenate([fs_ref[...], gap], axis=0)
    wf_ref[obs_pad:x_pad, :] = fa_ref[...]
    wf_ref[x_pad:, :] = fl_ref[...]
    wb_ref[...] = jnp.concatenate([bs_ref[...], gap], axis=0)
    me = lax.axis_index("dp")
    start = me * block
    base = pl.multiple_of(start // LANES * LANES, LANES)
    odd = lax.rem(me, 2) == 1
    span = pl.ds(base, 2 * LANES)

    def pick(ref):
        near = ref[:, span].astype(F32).T
        return jnp.where(odd, near[2 * LANES - block :], near[:block]).astype(BF16)

    wfb_ref[...] = pick(wf_ref)
    wbb_ref[...] = pick(wb_ref)


def forward_rows(cfg, xs, weights, outs):
    wf_ref, wb_ref, fo_ref, bo_ref, lat_ref, wfb_ref, wbb_ref = weights
    a_ref, later_ref, f_ref, u_ref, fh_ref, bh_ref = outs
    rows, act, rank, side = cfg["rows"], cfg["act"], cfg["rank"], cfg["side"]
    obs_pad, x_pad, hidden, zcount = cfg["obs_pad"], cfg["x_pad"], cfg["hidden"], cfg["zcount"]
    tile, lane = cfg["tile"], cfg["lane"]
    m = rows * len(xs)
    half = side // 2
    row_spots = lax.broadcasted_iota(jnp.int32, (rows, rows), 1).astype(F32)
    spots = lax.broadcasted_iota(jnp.int32, (rows, zcount), 1).astype(F32)
    blank = jnp.zeros((rows, x_pad - obs_pad - side), BF16)
    for j, x_ref in enumerate(xs):
        here = slice(j * rows, (j + 1) * rows)
        few = jnp.concatenate(
            [x_ref[rows:, 0:lane].astype(F32), x_ref[rows:, lane : 2 * lane].astype(F32)], axis=0
        ).T[:rows]
        near = x_ref[0:rows, 0:obs_pad]
        picks = jnp.where(few[:, act + 1 : act + 2] == spots, 1.0, 0.0).astype(BF16)
        hot = jnp.where(few[:, act : act + 1] == row_spots, 1.0, 0.0).astype(BF16)
        a_ref[here, 0:obs_pad] = near
        a_ref[here, obs_pad:x_pad] = jnp.concatenate([few.astype(BF16), blank], axis=1)
        a_ref[here, x_pad:] = dot_nn(picks, lat_ref[...]).astype(BF16)
        later_ref[here, :] = dot_nn(hot, near).astype(BF16)
    whole = a_ref[...]
    later = later_ref[...]
    f_acc = jnp.zeros((m, rank), F32)
    u = jnp.zeros((m, rank), F32)
    for n in range(0, hidden, tile):
        h = jnp.maximum(dot_nn(whole, wf_ref[:, n : n + tile]), 0.0).astype(BF16)
        f_acc = f_acc + dot_nn(h, fo_ref[n : n + tile, :])
        g = jnp.maximum(dot_nn(later, wb_ref[:, n : n + tile]), 0.0).astype(BF16)
        u = u + dot_nn(g, bo_ref[n : n + tile, :])
    emb = f_acc.astype(BF16)
    back = (u * lax.rsqrt(jnp.mean(u * u, axis=-1, keepdims=True) + EPSILON)).astype(BF16)
    f_ref[...] = emb
    u_ref[...] = u
    fh_ref[...] = jnp.maximum(dot_nt(wfb_ref[...], whole), 0.0).astype(BF16)
    bh_ref[...] = jnp.maximum(dot_nt(wbb_ref[...], later), 0.0).astype(BF16)
    cross = dot_tn(emb, emb)
    for j, x_ref in enumerate(xs):
        cross = cross - GAMMA * dot_tn(x_ref[0:rows, obs_pad:], emb[j * rows : (j + 1) * rows])
    return dot_tn(back, back), cross


def forward_kernel(cfg, count, *refs):
    xs, refs = refs[:count], refs[count:]
    weights, refs = refs[:7], refs[7:]
    gram_in, refs = refs[0], refs[1:]
    outs, gram_out = refs[:6], refs[6]
    gram, cross = forward_rows(cfg, xs, weights, outs)
    rank = cfg["rank"]
    gram_out[:, :rank] = gram_in[:, :rank] + gram
    gram_out[:, rank:] = gram_in[:, rank:] + cross


def last_kernel(cfg, early, count, *refs):
    groups = []
    for size in early:
        groups.append((refs[:size], refs[size : size + 6]))
        refs = refs[size + 6 :]
    xs, refs = refs[:count], refs[count:]
    weights, refs = refs[:7], refs[7:]
    gram_in, send_ref, keep_ref = refs[:3]
    outs, part_ref = refs[3:9], refs[9]
    rank, block, rows, obs_pad = cfg["rank"], cfg["block"], cfg["rows"], cfg["obs_pad"]
    group, replicas = cfg["group"], cfg["replicas"]
    factor = 1.0 / math.sqrt(cfg["total"])
    c1, c2, c3 = cfg["cols"]
    gram, cross = forward_rows(cfg, xs, weights, outs)
    gram_hi, gram_lo = split_two(gram_in[:, :rank] + gram)
    cross_hi, cross_lo = split_two(gram_in[:, rank:] + cross)
    groups.append((xs, outs))
    me = pl.multiple_of(lax.axis_index("dp") * block, ROW_TILE)
    fo = weights[2][pl.ds(me, block), :]
    bo = weights[3][pl.ds(me, block), :]
    square = jnp.zeros((1, rank), F32)
    diagonal = jnp.zeros((1, rank), F32)
    for index, (x_refs, (a_ref, later_ref, f_ref, u_ref, fh_ref, bh_ref)) in enumerate(groups):
        emb32 = f_ref[...].astype(F32)
        targets = [x_ref[0:rows, obs_pad:] for x_ref in x_refs]
        target = jnp.concatenate(targets, axis=0) if len(targets) > 1 else targets[0]
        error = emb32 - GAMMA * target.astype(F32)
        err_hi, err_lo = split_two(error)
        u = u_ref[...]
        scale = lax.rsqrt(jnp.mean(u * u, axis=-1, keepdims=True) + EPSILON)
        back = (u * scale).astype(BF16)
        back32 = back.astype(F32)
        pulled = dot_nn(err_hi, gram_hi) + (dot_nn(err_hi, gram_lo) + dot_nn(err_lo, gram_hi))
        square = square + jnp.sum(pulled * error, axis=0, keepdims=True)
        diagonal = diagonal + jnp.sum(emb32 * back32, axis=0, keepdims=True)
        d_f = (factor * (pulled / group - back32)).astype(BF16)
        pushed = dot_nn(back, cross_hi) + dot_nn(back, cross_lo)
        d_b = factor * (pushed / group - emb32)
        inner = jnp.mean(u * d_b, axis=-1, keepdims=True)
        d_u = (scale * d_b - u * (scale * scale * scale * inner)).astype(BF16)
        f_hid, b_hid = fh_ref[...], bh_ref[...]
        zero = jnp.zeros_like(f_hid)
        f_delta = jnp.where(f_hid > 0, dot_nt(fo, d_f).astype(BF16), zero)
        b_delta = jnp.where(b_hid > 0, dot_nt(bo, d_u).astype(BF16), zero)
        sums = (
            (0, c1, dot_nn(f_delta, a_ref[...])),
            (c1, c2, dot_nn(f_hid, d_f)),
            (c2, c3, dot_nn(b_delta, later_ref[...])),
            (c3, part_ref.shape[1], dot_nn(b_hid, d_u)),
        )
        for low, high, value in sums:
            if index == 0:
                part_ref[:, low:high] = value
            else:
                part_ref[:, low:high] += value
    loss = (0.5 / group) * jnp.sum(square) - jnp.sum(diagonal)
    lanes = lax.broadcasted_iota(jnp.int32, (block, LANES), 1)
    spot = cfg["loss_spot"]
    base = spot // LANES * LANES
    first = spot - base + 3 * lax.axis_index("replica")
    rest = jnp.full((block, LANES), loss, F32)
    piece_tile = part_ref[:, base : base + LANES]
    piece_tile = jnp.where(lanes >= spot - base, 0.0, piece_tile)
    for j in range(3):
        piece = rest.astype(BF16).astype(F32)
        piece_tile = jnp.where(lanes == first + j, piece, piece_tile)
        rest = rest - piece
    part_ref[:, base : base + LANES] = piece_tile
    core = lax.rem(lax.axis_index("replica"), 2)
    half = block // 2
    keep_ref[...] = part_ref[pl.ds(pl.multiple_of(core * half, ROW_TILE), half), :]
    other = pl.multiple_of((1 - core) * half, ROW_TILE)
    send_ref[...] = part_ref[pl.ds(other, half), :].astype(BF16)


def finish_kernel(cfg, one_ref, two_ref, far_ref, fs, fa, fl, fo, bs, bo, loss_ref, act_ref):
    obs, act, rank, x_pad, obs_pad = (cfg[k] for k in ("obs", "act", "rank", "x_pad", "obs_pad"))
    half = cfg["block"] // 2
    c1, c2, c3 = cfg["cols"]
    core = lax.rem(lax.axis_index("replica"), 2)
    mine32 = one_ref[...].astype(F32) + two_ref[...].astype(F32)
    mine = mine32.astype(BF16)
    far = far_ref[...]
    for start, value in ((core * half, mine), ((1 - core) * half, far)):
        here = pl.ds(pl.multiple_of(start, ROW_TILE), half)
        fs[here, :] = value[:, :obs]
        fl[here, :] = value[:, x_pad:c1]
        fo[here, :] = value[:, c1:c2]
        bs[here, :] = value[:, c2 : c2 + obs]
        bo[here, :] = value[:, c3:]
        act_ref[here, :] = value[:, obs_pad : obs_pad + LANES].astype(F32)
    fa[...] = act_ref[...].T[:act].astype(BF16)
    spot = cfg["loss_spot"]
    base = spot // LANES * LANES
    pieces = mine32[0:8, base : base + LANES]
    lanes = lax.broadcasted_iota(jnp.int32, (8, LANES), 1)
    rows = lax.broadcasted_iota(jnp.int32, (8, LANES), 0)
    ours = (lanes >= spot - base) & (lanes < spot - base + 3 * cfg["replicas"]) & (rows == 0)
    loss_ref[0, 0] = jnp.sum(jnp.where(ours, pieces, 0.0)) / cfg["total"]


def exchange(array, axis, size, bit):
    return lax.ppermute(array, axis, [(i, i ^ bit) for i in range(size)])


def shape(dims, kind):
    return jax.ShapeDtypeStruct(dims, kind)


def fast_local(
    states,
    actions,
    target_forward,
    next_index,
    latent_ids,
    latents,
    f_state,
    f_action,
    f_latent,
    f_output,
    b_state,
    b_output,
):
    size = lax.axis_size("dp")
    replicas = lax.axis_size("replica")
    rows, obs = states.shape[1:]
    act = actions.shape[2]
    zcount, rank = latents.shape
    hidden = f_state.shape[1]
    block = hidden // size
    group = rows * size
    side = round_up(act + 2, 2 * ROW_TILE)
    lane = round_up(rows, LANES)
    obs_pad = round_up(obs, LANES)
    x_pad = obs_pad + LANES
    c1 = x_pad + rank
    c2 = c1 + rank
    c3 = c2 + obs_pad
    width = c3 + rank
    cfg = dict(
        rows=rows,
        obs=obs,
        act=act,
        rank=rank,
        obs_pad=obs_pad,
        x_pad=x_pad,
        hidden=hidden,
        zcount=zcount,
        side=side,
        lane=lane,
        group=group,
        replicas=replicas,
        total=group * replicas,
        block=block,
        tile=512,
        cols=(c1, c2, c3),
        loss_spot=obs_pad + side,
    )
    params = pltpu.CompilerParams(vmem_limit_bytes=VMEM_LIMIT)
    own = pl.pallas_call(
        functools.partial(pack_kernel, cfg),
        out_shape=shape((rows + side // 2, obs_pad + rank), BF16),
        scratch_shapes=[pltpu.VMEM((side, lane), F32)],
        compiler_params=pltpu.CompilerParams(vmem_limit_bytes=8 * 1024 * 1024),
        name="pack",
    )(states, actions[0].T, next_index, latent_ids, target_forward)
    x = {0: own}
    x[2] = exchange(own, "dp", size, 2)
    x[1] = exchange(own, "dp", size, 1)
    x[6] = exchange(own, "dp", size, 6)
    x[4] = exchange(own, "dp", size, 4)
    for step in (2, 6, 4):
        x[step ^ 1] = exchange(x[step], "dp", size, 1)
    moves = jnp.pad(f_action, ((0, x_pad - obs_pad - act), (0, 0)))
    wf, wb, wfb, wbb = pl.pallas_call(
        functools.partial(weights_kernel, cfg),
        out_shape=(
            shape((x_pad + rank, hidden), BF16),
            shape((obs_pad, hidden), BF16),
            shape((block, x_pad + rank), BF16),
            shape((block, obs_pad), BF16),
        ),
        compiler_params=pltpu.CompilerParams(vmem_limit_bytes=24 * 1024 * 1024),
        cost_estimate=pl.CostEstimate(flops=0, bytes_accessed=8_000_000, transcendentals=0),
        name="weights",
    )(f_state, moves, f_latent, b_state)
    weights = (wf, wb, f_output, b_output, latents, wfb, wbb)
    row_flops = 2 * (c1 + 2 * rank + obs_pad) * hidden + 8 * rank * rank

    def kept(count):
        m = rows * count
        return (
            ((m, x_pad + rank), BF16),
            ((m, obs_pad), BF16),
            ((m, rank), BF16),
            ((m, rank), F32),
            ((block, m), BF16),
            ((block, m), BF16),
        )

    grams = jnp.zeros((rank, 2 * rank), F32)
    plan = ((0,), (1, 2), (6, 4), (3, 7))
    early = []
    for steps in plan:
        count = len(steps)
        xs = [x[step] for step in steps]
        *saved, grams = pl.pallas_call(
            functools.partial(forward_kernel, cfg, count),
            out_shape=(*(shape(*item) for item in kept(count)), shape((rank, 2 * rank), F32)),
            compiler_params=params,
            cost_estimate=pl.CostEstimate(
                flops=2 * rows * count * row_flops, bytes_accessed=8_000_000, transcendentals=0
            ),
            name="forward",
        )(*xs, *weights, grams)
        early.append((xs, saved))
    left = [x[step] for step in range(size) if all(step not in steps for steps in plan)]
    operands = []
    for xs, saved in early:
        operands += [*xs, *saved]
    send, keep = pl.pallas_call(
        functools.partial(last_kernel, cfg, [len(xs) for xs, _ in early], len(left)),
        out_shape=(shape((block // 2, width), BF16), shape((block // 2, width), F32)),
        scratch_shapes=[
            *(pltpu.VMEM(*item) for item in kept(len(left))),
            pltpu.VMEM((block, width), F32),
        ],
        compiler_params=params,
        cost_estimate=pl.CostEstimate(
            flops=4 * group * width * block, bytes_accessed=16_000_000, transcendentals=0
        ),
        name="last",
    )(*operands, *left, *weights, grams)
    got = exchange(send, "replica", replicas, 1)
    one = (keep + got.astype(F32)).astype(BF16)
    two = exchange(one, "replica", replicas, 2)
    mine = (one.astype(F32) + two.astype(F32)).astype(BF16)
    far = exchange(mine, "replica", replicas, 1)
    fs, fa, fl, fo, bs, bo, loss = pl.pallas_call(
        functools.partial(finish_kernel, cfg),
        out_shape=(
            shape((block, obs), BF16),
            shape((act, block), BF16),
            shape((block, rank), BF16),
            shape((block, rank), BF16),
            shape((block, obs), BF16),
            shape((block, rank), BF16),
            shape((1, 1), F32),
        ),
        out_specs=(
            *(pl.BlockSpec(memory_space=pltpu.VMEM) for _ in range(6)),
            pl.BlockSpec(memory_space=pltpu.SMEM),
        ),
        scratch_shapes=[pltpu.VMEM((block, LANES), F32)],
        compiler_params=pltpu.CompilerParams(vmem_limit_bytes=16 * 1024 * 1024),
        name="finish",
    )(one, two, far)
    return (fs.T, fa, fl.T, fo, bs.T, bo, loss.reshape(()))


def forward_pass(
    current, later, moves, latent_rows, f_state, f_action, f_latent, f_output, b_state, b_output
):
    f_pre = (
        jnp.dot(current, f_state, preferred_element_type=F32)
        + jnp.dot(moves, f_action, preferred_element_type=F32)
        + jnp.dot(latent_rows, f_latent, preferred_element_type=F32)
    )
    f_hidden = jnp.maximum(f_pre, 0.0).astype(BF16)
    forward_emb = jnp.dot(f_hidden, f_output, preferred_element_type=F32).astype(BF16)
    b_pre = jnp.dot(later, b_state, preferred_element_type=F32)
    b_hidden = jnp.maximum(b_pre, 0.0).astype(BF16)
    b_raw = jnp.dot(b_hidden, b_output, preferred_element_type=F32)
    b_scale = lax.rsqrt(jnp.mean(b_raw * b_raw, axis=-1, keepdims=True) + EPSILON)
    backward_emb = (b_raw * b_scale).astype(BF16)
    return (f_pre, f_hidden, forward_emb, b_pre, b_hidden, b_raw, b_scale, backward_emb)


def general_local(
    states,
    actions,
    target_forward,
    next_index,
    latent_ids,
    latents,
    f_state,
    f_action,
    f_latent,
    f_output,
    b_state,
    b_output,
):
    current = states[0]
    moves = actions[0]
    later = jnp.take(current, next_index[0], axis=0)
    latent_rows = jnp.take(latents, latent_ids[0], axis=0)
    f_pre, f_hidden, forward_emb, b_pre, b_hidden, b_raw, b_scale, backward_emb = forward_pass(
        current, later, moves, latent_rows, f_state, f_action, f_latent, f_output, b_state, b_output
    )
    group = current.shape[0] * lax.axis_size("dp")
    total = group * lax.axis_size("replica")
    factor = 1.0 / math.sqrt(total)
    forward32 = forward_emb.astype(F32)
    back32 = backward_emb.astype(F32)
    error = forward32 - GAMMA * target_forward[0].astype(F32)
    gram, cross = lax.psum(
        (
            jnp.dot(backward_emb.T, backward_emb, preferred_element_type=F32),
            jnp.dot(forward32.T, error, precision=HIGH, preferred_element_type=F32),
        ),
        "dp",
    )
    pulled = jnp.dot(error, gram, precision=HIGH, preferred_element_type=F32)
    pushed = jnp.dot(back32, cross.T, precision=HIGH, preferred_element_type=F32)
    partial_loss = 0.5 / group * jnp.sum(pulled * error) - jnp.sum(forward32 * back32)
    grad_forward = (factor * (pulled / group - back32)).astype(BF16)
    grad_backward = factor * (pushed / group - forward32)
    inner = jnp.mean(b_raw * grad_backward, axis=-1, keepdims=True)
    grad_raw = (b_scale * grad_backward - b_raw * b_scale * b_scale * b_scale * inner).astype(BF16)
    part_bo = jnp.dot(b_hidden.T, grad_raw, preferred_element_type=F32)
    b_back = jnp.dot(grad_raw, b_output.T, preferred_element_type=F32)
    b_delta = jnp.where(b_pre > 0, b_back, 0.0).astype(BF16)
    part_bs = jnp.dot(later.T, b_delta, preferred_element_type=F32)
    part_fo = jnp.dot(f_hidden.T, grad_forward, preferred_element_type=F32)
    f_back = jnp.dot(grad_forward, f_output.T, preferred_element_type=F32)
    f_delta = jnp.where(f_pre > 0, f_back, 0.0).astype(BF16)
    part_fs = jnp.dot(current.T, f_delta, preferred_element_type=F32)
    part_fa = jnp.dot(moves.T, f_delta, preferred_element_type=F32)
    part_fl = jnp.dot(latent_rows.T, f_delta, preferred_element_type=F32)
    places = (1, 1, 1, 0, 1, 0)
    parts = (part_fs, part_fa, part_fl, part_fo, part_bs, part_bo)
    shares = tuple(
        lax.psum_scatter(part, "dp", scatter_dimension=place, tiled=True)
        for part, place in zip(parts, places)
    )
    summed = lax.psum(shares, "replica")
    loss_sum = lax.psum(partial_loss, ("dp", "replica"))
    return (*(item.astype(BF16) for item in summed), loss_sum / total)


def local(*args):
    size, replicas = lax.axis_size("dp"), lax.axis_size("replica")
    rows, hidden = args[0].shape[1], args[6].shape[1]
    fits = size == 8 and replicas == 4 and rows * size <= KERNEL_GROUP_LIMIT
    block = hidden // size
    whole = rows % ROW_TILE == 0 and hidden % (size * 64) == 0 and hidden % 512 == 0
    whole = whole and LANES < block <= 2 * LANES - 64 and args[6].shape[0] % 8 == 0
    exact = rows <= 256 and args[5].shape[0] <= 256
    return (fast_local if fits and whole and exact else general_local)(*args)


def solution(mesh):
    in_specs = (
        P("replica", "dp", None),
        P("replica", "dp", None),
        P("replica", "dp", None),
        P("replica", "dp"),
        P("replica", "dp"),
        P(),
        P(),
        P(),
        P(),
        P(),
        P(),
        P(),
    )
    out_specs = (
        P(None, "dp"),
        P(None, "dp"),
        P(None, "dp"),
        P("dp", None),
        P(None, "dp"),
        P("dp", None),
        P(),
    )
    return jax.shard_map(local, mesh=mesh, in_specs=in_specs, out_specs=out_specs, check_vma=False)
```

time: 101 us -> 85.8 us (0.85)
  the two profiles are of different devices: /device:TPU:0 before, /device:TPU:21 now
where the time goes in v2:
time: 85.8 us; the launch traced here: 85.4 us
  Pallas kernels  41.5 us (48%)
  waiting for transfers between devices  18.3 us (21%)
  local copies, waits for them, and re-layouts  14.2 us (17%)
  starting transfers between devices  9.29 us (11%)
  other arithmetic  1.22 us (1%)
  between operations  0.93 us (1%)
    pallas_call x4, Pallas kernels, fast_local(): pl.pallas_call(functools.partial(forward_kernel, cfg, count), out_shape=(...  27.3 us
    ppermute x10, waiting for transfers between devices, exchange(): return lax.ppermute(array, axis, [(i, i ^ bit) for i in range(size)])  18.3 us
    pallas_call x1, Pallas kernels, fast_local(): pl.pallas_call(functools.partial(last_kernel, cfg, [len(xs) for xs, _ in...  12.8 us
    unnamed x40, local copies, waits for them, and re-layouts  12.4 us
    ppermute x10, starting transfers between devices, exchange(): return lax.ppermute(array, axis, [(i, i ^ bit) for i in range(size)])  9.29 us
  transfers between devices with their start and end apart: 10, of which 4 were waited for; matrix products, arithmetic and copies ran while one was open for 2% of the time, Pallas kernels for 32%

profile of v2, /device:TPU:21, one launch (start us, length us, event | category | flops | bytes accessed | tf_op | source)
XLA Modules:
  0.0 85.4 jit_solution(16879051748783504869)
XLA Ops:
  0.7 1.0 %copy-done.8 = bf16[1,192,376]{2,1,0:T(8,128)(2,1)S(1)} copy-done((bf16[1,192,376]{2,1,0:T(8,128)(2,1)S(1)}, bf16[1,192,376]{2,1,0:T(8,128)(2,1)}, u32[]{:S(2)}) %copy-start.8) | copy-done | bytes 144408
  1.6 0.9 %copy-done.9 = bf16[1,192,256]{2,1,0:T(8,128)(2,1)S(1)} copy-done((bf16[1,192,256]{2,1,0:T(8,128)(2,1)S(1)}, bf16[1,192,256]{2,1,0:T(8,128)(2,1)}, u32[]{:S(2)}) %copy-start.9) | copy-done | bytes 98328
  4.7 2.4 %collective-permute-start.2 = (bf16[208,640]{1,0:T(8,128)(2,1)S(1)}, bf16[208,640]{1,0:T(8,128)(2,1)S(1)}, u32[]{:S(2)}, u32[]{:S(2)}) collective-permute-start(bf16[208,640]{1,0:T(8,128)(2,1)S(1)} %pack.1.refs_0_), channel_id=1, source_target_pairs={{0,24},{4,28},{8,16},{12,20},{16,8},{20,12},{24,0},{28,4},{1,25},{... | collective-permute-start | bytes 798728 | tf_op jit(solution)/shard_map/ppermute | solution.py:238
  7.2 1.1 %collective-permute-start.1 = (bf16[208,640]{1,0:T(8,128)(2,1)S(1)}, bf16[208,640]{1,0:T(8,128)(2,1)S(1)}, u32[]{:S(2)}, u32[]{:S(2)}) collective-permute-start(bf16[208,640]{1,0:T(8,128)(2,1)S(1)} %pack.1.refs_0_), channel_id=1, source_target_pairs={{0,8},{4,12},{8,0},{12,4},{16,24},{20,28},{24,16},{28,20},{1,9},{5... | collective-permute-start | bytes 798728 | tf_op jit(solution)/shard_map/ppermute | solution.py:238
  8.2 1.2 %collective-permute-start = (bf16[208,640]{1,0:T(8,128)(2,1)S(1)}, bf16[208,640]{1,0:T(8,128)(2,1)S(1)}, u32[]{:S(2)}, u32[]{:S(2)}) collective-permute-start(bf16[208,640]{1,0:T(8,128)(2,1)S(1)} %pack.1.refs_0_), channel_id=1, source_target_pairs={{0,4},{4,0},{8,12},{12,8},{16,20},{20,16},{24,28},{28,24},{1,5},{5... | collective-permute-start | bytes 798728 | tf_op jit(solution)/shard_map/ppermute | solution.py:238
  9.5 0.9 %pad.4.fa_ref = bf16[128,1536]{1,0:T(8,128)(2,1)S(1)} pad(bf16[17,1536]{1,0:T(8,128)(2,1)} %param.19, bf16[]{:T(256)} %constant.1.clone.1), padding=0_111x0_0 | pad | bytes 445442 | tf_op jit(solution)/shard_map/jit(_pad)/pad | solution.py:309
  10.4 1.3 %copy-done.2 = bf16[376,1536]{1,0:T(8,128)(2,1)S(1)} copy-done((bf16[376,1536]{1,0:T(8,128)(2,1)S(1)}, bf16[376,1536]{1,0:T(8,128)(2,1)}, u32[]{:S(2)}) %copy-start.2) | copy-done | bytes 1155096
  11.6 1.3 %copy-done.3 = bf16[376,1536]{1,0:T(8,128)(2,1)S(1)} copy-done((bf16[376,1536]{1,0:T(8,128)(2,1)S(1)}, bf16[376,1536]{1,0:T(8,128)(2,1)}, u32[]{:S(2)}) %copy-start.3) | copy-done | bytes 1155096
  13.3 1.4 %copy-done = bf16[768,1536]{1,0:T(8,128)(2,1)} copy-done((bf16[768,1536]{1,0:T(8,128)(2,1)}, bf16[768,1536]{1,0:T(8,128)(2,1)S(1)}, u32[]{:S(2)}) %copy-start) | copy-done | bytes 2359320
  14.8 1.0 %copy-done.1 = bf16[384,1536]{1,0:T(8,128)(2,1)} copy-done((bf16[384,1536]{1,0:T(8,128)(2,1)}, bf16[384,1536]{1,0:T(8,128)(2,1)S(1)}, u32[]{:S(2)}) %copy-start.1) | copy-done | bytes 1179672
  18.0 5.7 %forward.4 = (bf16[192,768]{1,0:T(8,128)(2,1)}, bf16[192,384]{1,0:T(8,128)(2,1)}, bf16[192,256]{1,0:T(8,128)(2,1)}, f32[192,256]{1,0:T(8,128)}, bf16[192,192]{1,...) custom-call(bf16[208,640]{1,0:T(8,128)(2,1)} %copy-done.4, bf16[768,1536]{1,0:T(8,128)(2,1)} %copy-done, ...), custom_call_target="tpu_custom_call" | custom-call | flops 2164260864 | bytes 8000000 | tf_op jit(solution)/shard_map/forward/pallas_call | solution.py:342
  24.0 7.1 %collective-permute-done.2.refs_0_.refs_15_ = bf16[208,640]{1,0:T(8,128)(2,1)S(1)} collective-permute-done((bf16[208,640]{1,0:T(8,128)(2,1)S(1)}, bf16[208,640]{1,0:T(8,128)(2,1)S(1)}, u32[]{:S(2)}, u32[]{:S(2)}) %collective-permute-start.2) | collective-permute-done | bytes 266272 | tf_op jit(solution)/shard_map/ppermute | solution.py:238
  31.1 1.2 %collective-permute-start.5 = (bf16[208,640]{1,0:T(8,128)(2,1)S(1)}, bf16[208,640]{1,0:T(8,128)(2,1)S(1)}, u32[]{:S(2)}, u32[]{:S(2)}) collective-permute-start(bf16[208,640]{1,0:T(8,128)(2,1)S(1)} %collective-permute-done.2.refs_0_.refs_15_), channel_id=1, source_target_pairs={{0,4},{4,0},{8,12},{12,8},{16,20},{20,16},{24,28},{28,24},{1,5},{5... | collective-permute-start | bytes 798728 | tf_op jit(solution)/shard_map/ppermute | solution.py:238
  33.3 7.2 %forward.5 = (bf16[384,768]{1,0:T(8,128)(2,1)}, bf16[384,384]{1,0:T(8,128)(2,1)}, bf16[384,256]{1,0:T(8,128)(2,1)}, f32[384,256]{1,0:T(8,128)}, bf16[192,384]{1,...) custom-call(bf16[208,640]{1,0:T(8,128)(2,1)} %copy-done.16, bf16[208,640]{1,0:T(8,128)(2,1)} %copy-done.15, ...), custom_call_target="tpu_custom_call" | custom-call | flops 4328521728 | bytes 8000000 | tf_op jit(solution)/shard_map/forward/pallas_call | solution.py:342
  40.4 7.2 %forward.6 = (bf16[384,768]{1,0:T(8,128)(2,1)}, bf16[384,384]{1,0:T(8,128)(2,1)}, bf16[384,256]{1,0:T(8,128)(2,1)}, f32[384,256]{1,0:T(8,128)}, bf16[192,384]{1,...) custom-call(bf16[208,640]{1,0:T(8,128)(2,1)} %copy-done.14, bf16[208,640]{1,0:T(8,128)(2,1)} %copy-done.13, ...), custom_call_target="tpu_custom_call" | custom-call | flops 4328521728 | bytes 8000000 | tf_op jit(solution)/shard_map/forward/pallas_call | solution.py:342
  48.5 7.2 %forward.7 = (bf16[384,768]{1,0:T(8,128)(2,1)}, bf16[384,384]{1,0:T(8,128)(2,1)}, bf16[384,256]{1,0:T(8,128)(2,1)}, f32[384,256]{1,0:T(8,128)}, bf16[192,384]{1,...) custom-call(bf16[208,640]{1,0:T(8,128)(2,1)} %copy-done.19, bf16[208,640]{1,0:T(8,128)(2,1)} %copy-done.18, ...), custom_call_target="tpu_custom_call" | custom-call | flops 4328521728 | bytes 8000000 | tf_op jit(solution)/shard_map/forward/pallas_call | solution.py:342
  56.4 12.8 %last.1 = (bf16[96,1664]{1,0:T(8,128)(2,1)}, f32[96,1664]{1,0:T(8,128)}) custom-call(bf16[208,640]{1,0:T(8,128)(2,1)} %copy-done.4, bf16[192,768]{1,0:T(8,128)(2,1)} %get-tuple-element.52.refs_1_, bf16[192,384]{1,0:T(8,128)(2,1)} %get-tuple-element.53.refs_2_, bf16[192,256]{1,0:T(8,128)(2,1)} %get-tuple-element.54.refs_3_, ...), custom_call_target="tpu_custom_call" | custom-call | flops 1962934272 | bytes 16000000 | tf_op jit(solution)/shard_map/last/pallas_call | solution.py:356
  69.2 1.1 %collective-permute-start.7 = (bf16[96,1664]{1,0:T(8,128)(2,1)}, bf16[96,1664]{1,0:T(8,128)(2,1)S(1)}, u32[]{:S(2)}, u32[]{:S(2)}) collective-permute-start(bf16[96,1664]{1,0:T(8,128)(2,1)} %get-tuple-element.81), channel_id=1, source_target_pairs={{0,1},{1,0},{2,3},{3,2},{4,5},{5,4},{6,7},{7,6},{8,9},{9,8},{10,11... | collective-permute-start | bytes 958472 | tf_op jit(solution)/shard_map/ppermute | solution.py:238
  70.3 1.5 %collective-permute-done.7 = bf16[96,1664]{1,0:T(8,128)(2,1)S(1)} collective-permute-done((bf16[96,1664]{1,0:T(8,128)(2,1)}, bf16[96,1664]{1,0:T(8,128)(2,1)S(1)}, u32[]{:S(2)}, u32[]{:S(2)}) %collective-permute-start.7) | collective-permute-done | bytes 319520 | tf_op jit(solution)/shard_map/ppermute | solution.py:238
  71.7 1.1 %add_convert_fusion.1.one_ref = bf16[96,1664]{1,0:T(8,128)(2,1)S(1)} fusion(f32[96,1664]{1,0:T(8,128)} %get-tuple-element.80, bf16[96,1664]{1,0:T(8,128)(2,1)S(1)} %collective-permute-done.7), kind=kLoop, calls=%fused_computation.1 | loop fusion | flops 479232 | bytes 1277952 | tf_op jit(solution)/shard_map/convert_element_type | solution.py:370
  73.2 8.5 %collective-permute-done.8.two_ref = bf16[96,1664]{1,0:T(8,128)(2,1)S(1)} collective-permute-done((bf16[96,1664]{1,0:T(8,128)(2,1)S(1)}, bf16[96,1664]{1,0:T(8,128)(2,1)S(1)}, u32[]{:S(2)}, u32[]{:S(2)}) %collective-permute-start.8) | collective-permute-done | bytes 319520 | tf_op jit(solution)/shard_map/ppermute | solution.py:238
  81.8 1.3 %collective-permute-start.9 = (bf16[96,1664]{1,0:T(8,128)(2,1)S(1)}, bf16[96,1664]{1,0:T(8,128)(2,1)S(1)}, u32[]{:S(2)}, u32[]{:S(2)}) collective-permute-start(bf16[96,1664]{1,0:T(8,128)(2,1)S(1)} %add_convert_fusion), channel_id=1, source_target_pairs={{0,1},{1,0},{2,3},{3,2},{4,5},{5,4},{6,7},{7,6},{8,9},{9,8},{10,11... | collective-permute-start | bytes 958472 | tf_op jit(solution)/shard_map/ppermute | solution.py:238
  83.0 1.2 %collective-permute-done.9.far_ref = bf16[96,1664]{1,0:T(8,128)(2,1)S(1)} collective-permute-done((bf16[96,1664]{1,0:T(8,128)(2,1)S(1)}, bf16[96,1664]{1,0:T(8,128)(2,1)S(1)}, u32[]{:S(2)}, u32[]{:S(2)}) %collective-permute-start.9) | collective-permute-done | bytes 319520 | tf_op jit(solution)/shard_map/ppermute | solution.py:238
  84.3 0.9 %finish.1 = (bf16[192,376]{1,0:T(8,128)(2,1)}, bf16[17,192]{1,0:T(8,128)(2,1)}, bf16[192,256]{1,0:T(8,128)(2,1)}, bf16[192,256]{1,0:T(8,128)(2,1)}, bf16[192,376...) custom-call(bf16[96,1664]{1,0:T(8,128)(2,1)S(1)} %add_convert_fusion.1.one_ref, ...), custom_call_target="tpu_custom_call" | custom-call | tf_op jit(solution)/shard_map/finish/pallas_call | solution.py:374
  (48 shorter events, 8.0 us)
Async XLA Ops:
  0.6 9.7 %copy-start.5 = (bf16[256,1536]{1,0:T(8,128)(2,1)S(1)}, bf16[256,1536]{1,0:T(8,128)(2,1)}, u32[]{:S(2)}) copy-start(bf16[256,1536]{1,0:T(8,128)(2,1)} %fl_ref.1) | copy-start | bytes 2359300
  0.6 1.0 %copy-start.8 = (bf16[1,192,376]{2,1,0:T(8,128)(2,1)S(1)}, bf16[1,192,376]{2,1,0:T(8,128)(2,1)}, u32[]{:S(2)}) copy-start(bf16[1,192,376]{2,1,0:T(8,128)(2,1)} %state_ref.1) | copy-start | bytes 433156
  1.6 0.9 %copy-start.9 = (bf16[1,192,256]{2,1,0:T(8,128)(2,1)S(1)}, bf16[1,192,256]{2,1,0:T(8,128)(2,1)}, u32[]{:S(2)}) copy-start(bf16[1,192,256]{2,1,0:T(8,128)(2,1)} %target_ref.1) | copy-start | bytes 294916
  2.5 0.7 copy-start.10
  4.6 8.7 %copy-start.4 = (bf16[208,640]{1,0:T(8,128)(2,1)}, bf16[208,640]{1,0:T(8,128)(2,1)S(1)}, u32[]{:S(2)}) copy-start(bf16[208,640]{1,0:T(8,128)(2,1)S(1)} %pack.1.refs_0_) | copy-start | bytes 798724
  4.6 19.1 %collective-permute-start.3 = (bf16[208,640]{1,0:T(8,128)(2,1)S(1)}, bf16[208,640]{1,0:T(8,128)(2,1)S(1)}, u32[]{:S(2)}, u32[]{:S(2)}) collective-permute-start(bf16[208,640]{1,0:T(8,128)(2,1)S(1)} %pack.1.refs_0_), channel_id=1, source_target_pairs={{0,16},{4,20},{8,24},{12,28},{16,0},{20,4},{24,8},{28,12},{1,17},{... | collective-permute-start | bytes 798728 | tf_op jit(solution)/shard_map/ppermute | solution.py:238
  4.7 26.3 %collective-permute-start.2 = (bf16[208,640]{1,0:T(8,128)(2,1)S(1)}, bf16[208,640]{1,0:T(8,128)(2,1)S(1)}, u32[]{:S(2)}, u32[]{:S(2)}) collective-permute-start(bf16[208,640]{1,0:T(8,128)(2,1)S(1)} %pack.1.refs_0_), channel_id=1, source_target_pairs={{0,24},{4,28},{8,16},{12,20},{16,8},{20,12},{24,0},{28,4},{1,25},{... | collective-permute-start | bytes 798728 | tf_op jit(solution)/shard_map/ppermute | solution.py:238
  7.2 25.1 %collective-permute-start.1 = (bf16[208,640]{1,0:T(8,128)(2,1)S(1)}, bf16[208,640]{1,0:T(8,128)(2,1)S(1)}, u32[]{:S(2)}, u32[]{:S(2)}) collective-permute-start(bf16[208,640]{1,0:T(8,128)(2,1)S(1)} %pack.1.refs_0_), channel_id=1, source_target_pairs={{0,8},{4,12},{8,0},{12,4},{16,24},{20,28},{24,16},{28,20},{1,9},{5... | collective-permute-start | bytes 798728 | tf_op jit(solution)/shard_map/ppermute | solution.py:238
  8.2 24.3 %collective-permute-start = (bf16[208,640]{1,0:T(8,128)(2,1)S(1)}, bf16[208,640]{1,0:T(8,128)(2,1)S(1)}, u32[]{:S(2)}, u32[]{:S(2)}) collective-permute-start(bf16[208,640]{1,0:T(8,128)(2,1)S(1)} %pack.1.refs_0_), channel_id=1, source_target_pairs={{0,4},{4,0},{8,12},{12,8},{16,20},{20,16},{24,28},{28,24},{1,5},{5... | collective-permute-start | bytes 798728 | tf_op jit(solution)/shard_map/ppermute | solution.py:238
  10.4 1.3 %copy-start.2 = (bf16[376,1536]{1,0:T(8,128)(2,1)S(1)}, bf16[376,1536]{1,0:T(8,128)(2,1)}, u32[]{:S(2)}) copy-start(bf16[376,1536]{1,0:T(8,128)(2,1)} %fs_ref.1) | copy-start | bytes 3465220
  11.6 1.3 %copy-start.3 = (bf16[376,1536]{1,0:T(8,128)(2,1)S(1)}, bf16[376,1536]{1,0:T(8,128)(2,1)}, u32[]{:S(2)}) copy-start(bf16[376,1536]{1,0:T(8,128)(2,1)} %bs_ref.1) | copy-start | bytes 3465220
  13.3 1.4 %copy-start = (bf16[768,1536]{1,0:T(8,128)(2,1)}, bf16[768,1536]{1,0:T(8,128)(2,1)S(1)}, u32[]{:S(2)}) copy-start(bf16[768,1536]{1,0:T(8,128)(2,1)S(1)} %get-tuple-element.48.refs_1_.refs_2_.refs_32_) | copy-start | bytes 7077892
  14.8 1.0 %copy-start.1 = (bf16[384,1536]{1,0:T(8,128)(2,1)}, bf16[384,1536]{1,0:T(8,128)(2,1)S(1)}, u32[]{:S(2)}) copy-start(bf16[384,1536]{1,0:T(8,128)(2,1)S(1)} %get-tuple-element.49.refs_2_.refs_3_.refs_33_) | copy-start | bytes 3538948
  23.7 16.8 %copy-start.13 = (bf16[208,640]{1,0:T(8,128)(2,1)}, bf16[208,640]{1,0:T(8,128)(2,1)S(1)}, u32[]{:S(2)}) copy-start(bf16[208,640]{1,0:T(8,128)(2,1)S(1)} %collective-permute-done.3.refs_1_.refs_16_) | copy-start | bytes 798724
  23.7 32.0 %collective-permute-start.6 = (bf16[208,640]{1,0:T(8,128)(2,1)S(1)}, bf16[208,640]{1,0:T(8,128)(2,1)S(1)}, u32[]{:S(2)}, u32[]{:S(2)}) collective-permute-start(bf16[208,640]{1,0:T(8,128)(2,1)S(1)} %collective-permute-done.3.refs_1_.refs_16_), channel_id=1, source_target_pairs={{0,4},{4,0},{8,12},{12,8},{16,20},{20,16},{24,28},{28,24},{1,5},{5... | collective-permute-start | bytes 798728 | tf_op jit(solution)/shard_map/ppermute | solution.py:238
  31.1 9.4 %copy-start.14 = (bf16[208,640]{1,0:T(8,128)(2,1)}, bf16[208,640]{1,0:T(8,128)(2,1)S(1)}, u32[]{:S(2)}) copy-start(bf16[208,640]{1,0:T(8,128)(2,1)S(1)} %collective-permute-done.2.refs_0_.refs_15_) | copy-start | bytes 798724
  31.1 16.6 %collective-permute-start.5 = (bf16[208,640]{1,0:T(8,128)(2,1)S(1)}, bf16[208,640]{1,0:T(8,128)(2,1)S(1)}, u32[]{:S(2)}, u32[]{:S(2)}) collective-permute-start(bf16[208,640]{1,0:T(8,128)(2,1)S(1)} %collective-permute-done.2.refs_0_.refs_15_), channel_id=1, source_target_pairs={{0,4},{4,0},{8,12},{12,8},{16,20},{20,16},{24,28},{28,24},{1,5},{5... | collective-permute-start | bytes 798728 | tf_op jit(solution)/shard_map/ppermute | solution.py:238
  32.3 0.7 copy-start.15
  32.3 15.4 %collective-permute-start.4 = (bf16[208,640]{1,0:T(8,128)(2,1)S(1)}, bf16[208,640]{1,0:T(8,128)(2,1)S(1)}, u32[]{:S(2)}, u32[]{:S(2)}) collective-permute-start(bf16[208,640]{1,0:T(8,128)(2,1)S(1)} %collective-permute-done.1.refs_1_.refs_8_), channel_id=1, source_target_pairs={{0,4},{4,0},{8,12},{12,8},{16,20},{20,16},{24,28},{28,24},{1,5},{5... | collective-permute-start | bytes 798728 | tf_op jit(solution)/shard_map/ppermute | solution.py:238
  32.5 0.7 copy-start.16
  47.7 0.8 copy-start.19
  69.2 2.6 %collective-permute-start.7 = (bf16[96,1664]{1,0:T(8,128)(2,1)}, bf16[96,1664]{1,0:T(8,128)(2,1)S(1)}, u32[]{:S(2)}, u32[]{:S(2)}) collective-permute-start(bf16[96,1664]{1,0:T(8,128)(2,1)} %get-tuple-element.81), channel_id=1, source_target_pairs={{0,1},{1,0},{2,3},{3,2},{4,5},{5,4},{6,7},{7,6},{8,9},{9,8},{10,11... | collective-permute-start | bytes 958472 | tf_op jit(solution)/shard_map/ppermute | solution.py:238
  72.9 8.8 %collective-permute-start.8 = (bf16[96,1664]{1,0:T(8,128)(2,1)S(1)}, bf16[96,1664]{1,0:T(8,128)(2,1)S(1)}, u32[]{:S(2)}, u32[]{:S(2)}) collective-permute-start(bf16[96,1664]{1,0:T(8,128)(2,1)S(1)} %add_convert_fusion.1.one_ref), channel_id=1, source_target_pairs={{0,2},{1,3},{2,0},{3,1},{4,6},{5,7},{6,4},{7,5},{8,10},{9,11},{10,... | collective-permute-start | bytes 958472 | tf_op jit(solution)/shard_map/ppermute | solution.py:238
  81.8 2.5 %collective-permute-start.9 = (bf16[96,1664]{1,0:T(8,128)(2,1)S(1)}, bf16[96,1664]{1,0:T(8,128)(2,1)S(1)}, u32[]{:S(2)}, u32[]{:S(2)}) collective-permute-start(bf16[96,1664]{1,0:T(8,128)(2,1)S(1)} %add_convert_fusion), channel_id=1, source_target_pairs={{0,1},{1,0},{2,3},{3,2},{4,5},{5,4},{6,7},{7,6},{8,9},{9,8},{10,11... | collective-permute-start | bytes 958472 | tf_op jit(solution)/shard_map/ppermute | solution.py:238
  (6 other events, 4.1 us)

commit v3 on v2

--- a/solution.py
+++ b/solution.py
@@ -61,7 +61,8 @@
     hidden, block, act = cfg["hidden"], cfg["block"], cfg["act"]
     gap = jnp.zeros((obs_pad - obs, hidden), BF16)
     wf_ref[0:obs_pad, :] = jnp.concatenate([fs_ref[...], gap], axis=0)
-    wf_ref[obs_pad:x_pad, :] = fa_ref[...]
+    wf_ref[obs_pad:x_pad, :] = jnp.zeros((x_pad - obs_pad, hidden), BF16)
+    wf_ref[obs_pad : obs_pad + act, :] = fa_ref[...]
     wf_ref[x_pad:, :] = fl_ref[...]
     wb_ref[...] = jnp.concatenate([bs_ref[...], gap], axis=0)
     me = lax.axis_index("dp")
@@ -122,15 +123,16 @@
     return dot_tn(back, back), cross
 
 
-def forward_kernel(cfg, count, *refs):
+def forward_kernel(cfg, count, first, *refs):
     xs, refs = refs[:count], refs[count:]
     weights, refs = refs[:7], refs[7:]
-    gram_in, refs = refs[0], refs[1:]
+    if not first:
+        gram_in, refs = refs[0], refs[1:]
     outs, gram_out = refs[:6], refs[6]
     gram, cross = forward_rows(cfg, xs, weights, outs)
     rank = cfg["rank"]
-    gram_out[:, :rank] = gram_in[:, :rank] + gram
-    gram_out[:, rank:] = gram_in[:, rank:] + cross
+    gram_out[:, :rank] = gram if first else gram_in[:, :rank] + gram
+    gram_out[:, rank:] = cross if first else gram_in[:, rank:] + cross
 
 
 def last_kernel(cfg, early, count, *refs):
@@ -291,22 +293,18 @@
         cols=(c1, c2, c3),
         loss_spot=obs_pad + side,
     )
-    params = pltpu.CompilerParams(vmem_limit_bytes=VMEM_LIMIT)
+    params = pltpu.CompilerParams(vmem_limit_bytes=20 * 1024 * 1024)
+    last_params = pltpu.CompilerParams(vmem_limit_bytes=28 * 1024 * 1024)
     own = pl.pallas_call(
         functools.partial(pack_kernel, cfg),
         out_shape=shape((rows + side // 2, obs_pad + rank), BF16),
         scratch_shapes=[pltpu.VMEM((side, lane), F32)],
-        compiler_params=pltpu.CompilerParams(vmem_limit_bytes=8 * 1024 * 1024),
+        compiler_params=pltpu.CompilerParams(vmem_limit_bytes=VMEM_LIMIT),
         name="pack",
     )(states, actions[0].T, next_index, latent_ids, target_forward)
     x = {0: own}
-    x[2] = exchange(own, "dp", size, 2)
-    x[1] = exchange(own, "dp", size, 1)
-    x[6] = exchange(own, "dp", size, 6)
-    x[4] = exchange(own, "dp", size, 4)
-    for step in (2, 6, 4):
-        x[step ^ 1] = exchange(x[step], "dp", size, 1)
-    moves = jnp.pad(f_action, ((0, x_pad - obs_pad - act), (0, 0)))
+    for step in (4, 6, 1, 2):
+        x[step] = exchange(own, "dp", size, step)
     wf, wb, wfb, wbb = pl.pallas_call(
         functools.partial(weights_kernel, cfg),
         out_shape=(
@@ -318,7 +316,7 @@
         compiler_params=pltpu.CompilerParams(vmem_limit_bytes=24 * 1024 * 1024),
         cost_estimate=pl.CostEstimate(flops=0, bytes_accessed=8_000_000, transcendentals=0),
         name="weights",
-    )(f_state, moves, f_latent, b_state)
+    )(f_state, f_action, f_latent, b_state)
     weights = (wf, wb, f_output, b_output, latents, wfb, wbb)
     row_flops = 2 * (c1 + 2 * rank + obs_pad) * hidden + 8 * rank * rank
 
@@ -333,21 +331,28 @@
             ((block, m), BF16),
         )
 
-    grams = jnp.zeros((rank, 2 * rank), F32)
+    grams = ()
     plan = ((0,), (1, 2), (6, 4), (3, 7))
     early = []
     for steps in plan:
         count = len(steps)
+        if steps == (1, 2):
+            x[3] = exchange(x[2], "dp", size, 1)
+        if steps == (6, 4):
+            far, near, grams = lax.optimization_barrier((x[6], x[4], grams))
+            x[5] = exchange(near, "dp", size, 1)
+            x[7] = exchange(far, "dp", size, 1)
         xs = [x[step] for step in steps]
-        *saved, grams = pl.pallas_call(
-            functools.partial(forward_kernel, cfg, count),
+        *saved, total_grams = pl.pallas_call(
+            functools.partial(forward_kernel, cfg, count, not early),
             out_shape=(*(shape(*item) for item in kept(count)), shape((rank, 2 * rank), F32)),
             compiler_params=params,
             cost_estimate=pl.CostEstimate(
                 flops=2 * rows * count * row_flops, bytes_accessed=8_000_000, transcendentals=0
             ),
             name="forward",
-        )(*xs, *weights, grams)
+        )(*xs, *weights, *grams)
+        grams = (total_grams,)
         early.append((xs, saved))
     left = [x[step] for step in range(size) if all(step not in steps for steps in plan)]
     operands = []
@@ -360,12 +365,12 @@
             *(pltpu.VMEM(*item) for item in kept(len(left))),
             pltpu.VMEM((block, width), F32),
         ],
-        compiler_params=params,
+        compiler_params=last_params,
         cost_estimate=pl.CostEstimate(
             flops=4 * group * width * block, bytes_accessed=16_000_000, transcendentals=0
         ),
         name="last",
-    )(*operands, *left, *weights, grams)
+    )(*operands, *left, *weights, *grams)
     got = exchange(send, "replica", replicas, 1)
     one = (keep + got.astype(F32)).astype(BF16)
     two = exchange(one, "replica", replicas, 2)

time: 85.8 us -> 73.6 us (0.86)
  the two profiles are of different devices: /device:TPU:21 before, /device:TPU:9 now
where the time goes in v3:
time: 73.6 us; the launch traced here: 73.3 us
  waiting for transfers between devices  33.1 us (45%)
  Pallas kernels  22.4 us (30%)
  starting transfers between devices  11.2 us (15%)
  local copies, waits for them, and re-layouts  5.57 us (8%)
  between operations  0.89 us (1%)
    ppermute x10, waiting for transfers between devices, exchange(): return lax.ppermute(array, axis, [(i, i ^ bit) for i in range(size)])  33.1 us
    pallas_call x4, Pallas kernels, fast_local(): pl.pallas_call(functools.partial(forward_kernel, cfg, count, not early),...  12.5 us
    ppermute x10, starting transfers between devices, exchange(): return lax.ppermute(array, axis, [(i, i ^ bit) for i in range(size)])  11.2 us
    pallas_call x1, Pallas kernels, fast_local(): pl.pallas_call(functools.partial(last_kernel, cfg, [len(xs) for xs, _ in...  6.72 us
    unnamed x16, local copies, waits for them, and re-layouts  5.57 us
    pallas_call x1, Pallas kernels, fast_local(): pl.pallas_call(functools.partial(pack_kernel, cfg), out_shape=shape((rows...  1.79 us
  transfers between devices with their start and end apart: 10, of which 6 were waited for; matrix products, arithmetic and copies ran while one was open for 0% of the time, Pallas kernels for 18%

profile of v3, /device:TPU:9, one launch (start us, length us, event | category | flops | bytes accessed | tf_op | source)
XLA Modules:
  0.0 73.3 jit_solution(6699502121899862384)
XLA Ops:
  0.6 1.8 %pack.1.refs_0_ = bf16[208,640]{1,0:T(8,128)(2,1)} custom-call(bf16[1,192,376]{2,1,0:T(8,128)(2,1)} %state_ref.1, bf16[17,192]{1,0:T(8,128)(2,1)} %bitcast.7, s32[1,192]{1,0:T(1,128)} %next_ref.1, s32[1,192]{1,0:T(1,128)} %latent_ref.1, bf16[1,192,256]{2,1,0:T(8,128)(2,1)} %target_ref.1), custom_call_target="tpu_custom_call" | custom-call | tf_op jit(solution)/shard_map/pack/pallas_call | solution.py:298
  2.4 1.4 %collective-permute-start = (bf16[208,640]{1,0:T(8,128)(2,1)}, bf16[208,640]{1,0:T(8,128)(2,1)S(1)}, u32[]{:S(2)}, u32[]{:S(2)}) collective-permute-start(bf16[208,640]{1,0:T(8,128)(2,1)} %pack.1.refs_0_), channel_id=1, source_target_pairs={{0,4},{4,0},{8,12},{12,8},{16,20},{20,16},{24,28},{28,24},{1,5},{5... | collective-permute-start | bytes 798728 | tf_op jit(solution)/shard_map/ppermute | solution.py:240
  3.8 2.3 %collective-permute-start.3 = (bf16[208,640]{1,0:T(8,128)(2,1)}, bf16[208,640]{1,0:T(8,128)(2,1)S(1)}, u32[]{:S(2)}, u32[]{:S(2)}) collective-permute-start(bf16[208,640]{1,0:T(8,128)(2,1)} %pack.1.refs_0_), channel_id=1, source_target_pairs={{0,16},{4,20},{8,24},{12,28},{16,0},{20,4},{24,8},{28,12},{1,17},{... | collective-permute-start | bytes 798728 | tf_op jit(solution)/shard_map/ppermute | solution.py:240
  6.3 1.3 %copy-done = bf16[376,1536]{1,0:T(8,128)(2,1)S(1)} copy-done((bf16[376,1536]{1,0:T(8,128)(2,1)S(1)}, bf16[376,1536]{1,0:T(8,128)(2,1)}, u32[]{:S(2)}) %copy-start) | copy-done | bytes 1155096
  7.6 1.3 %copy-done.1 = bf16[376,1536]{1,0:T(8,128)(2,1)S(1)} copy-done((bf16[376,1536]{1,0:T(8,128)(2,1)S(1)}, bf16[376,1536]{1,0:T(8,128)(2,1)}, u32[]{:S(2)}) %copy-start.1) | copy-done | bytes 1155096
  8.8 1.1 %copy-done.5 = bf16[256,1536]{1,0:T(8,128)(2,1)S(1)} copy-done((bf16[256,1536]{1,0:T(8,128)(2,1)S(1)}, bf16[256,1536]{1,0:T(8,128)(2,1)}, u32[]{:S(2)}) %copy-start.5) | copy-done | bytes 786456
  10.0 0.9 %copy-done.7 = bf16[17,1536]{1,0:T(8,128)(2,1)S(1)} copy-done((bf16[17,1536]{1,0:T(8,128)(2,1)S(1)}, bf16[17,1536]{1,0:T(8,128)(2,1)}, u32[]{:S(2)}) %copy-start.7) | copy-done | bytes 52248
  11.3 0.5 copy-done.2
  12.3 2.0 %forward.4 = (bf16[192,768]{1,0:T(8,128)(2,1)S(1)}, bf16[192,384]{1,0:T(8,128)(2,1)S(1)}, bf16[192,256]{1,0:T(8,128)(2,1)S(1)}, f32[192,256]{1,0:T(8,128)S(1)}, ...) custom-call(bf16[208,640]{1,0:T(8,128)(2,1)S(1)} %copy-done.2, ...), custom_call_target="tpu_custom_call" | custom-call | flops 2164260864 | bytes 8000000 | tf_op jit(solution)/shard_map/forward/pallas_call | solution.py:346
  14.3 3.5 %forward.5 = (bf16[384,768]{1,0:T(8,128)(2,1)S(1)}, bf16[384,384]{1,0:T(8,128)(2,1)S(1)}, bf16[384,256]{1,0:T(8,128)(2,1)S(1)}, f32[384,256]{1,0:T(8,128)S(1)}, ...) custom-call(bf16[208,640]{1,0:T(8,128)(2,1)S(1)} %collective-permute-done.refs_0_.refs_7_, ...), custom_call_target="tpu_custom_call" | custom-call | flops 4328521728 | bytes 8000000 | tf_op jit(solution)/shard_map/forward/pallas_call | solution.py:346
  17.9 4.4 %collective-permute-done.3.refs_1_.refs_16_ = bf16[208,640]{1,0:T(8,128)(2,1)S(1)} collective-permute-done((bf16[208,640]{1,0:T(8,128)(2,1)}, bf16[208,640]{1,0:T(8,128)(2,1)S(1)}, u32[]{:S(2)}, u32[]{:S(2)}) %collective-permute-start.3) | collective-permute-done | bytes 266272 | tf_op jit(solution)/shard_map/ppermute | solution.py:240
  22.2 6.7 %collective-permute-done.2.refs_0_.refs_15_ = bf16[208,640]{1,0:T(8,128)(2,1)S(1)} collective-permute-done((bf16[208,640]{1,0:T(8,128)(2,1)}, bf16[208,640]{1,0:T(8,128)(2,1)S(1)}, u32[]{:S(2)}, u32[]{:S(2)}) %collective-permute-start.2) | collective-permute-done | bytes 266272 | tf_op jit(solution)/shard_map/ppermute | solution.py:240
  29.2 1.2 %collective-permute-start.6 = (bf16[208,640]{1,0:T(8,128)(2,1)S(1)}, bf16[208,640]{1,0:T(8,128)(2,1)S(1)}, u32[]{:S(2)}, u32[]{:S(2)}) collective-permute-start(bf16[208,640]{1,0:T(8,128)(2,1)S(1)} %collective-permute-done.3.refs_1_.refs_16_), channel_id=1, source_target_pairs={{0,4},{4,0},{8,12},{12,8},{16,20},{20,16},{24,28},{28,24},{1,5},{5... | collective-permute-start | bytes 798728 | tf_op jit(solution)/shard_map/ppermute | solution.py:240
  30.7 3.5 %forward.6 = (bf16[384,768]{1,0:T(8,128)(2,1)S(1)}, bf16[384,384]{1,0:T(8,128)(2,1)S(1)}, bf16[384,256]{1,0:T(8,128)(2,1)S(1)}, f32[384,256]{1,0:T(8,128)S(1)}, ...) custom-call(bf16[208,640]{1,0:T(8,128)(2,1)S(1)} %collective-permute-done.2.refs_0_.refs_15_, ...), custom_call_target="tpu_custom_call" | custom-call | flops 4328521728 | bytes 8000000 | tf_op jit(solution)/shard_map/forward/pallas_call | solution.py:346
  34.2 12.0 %collective-permute-done.4.refs_0_.refs_23_ = bf16[208,640]{1,0:T(8,128)(2,1)S(1)} collective-permute-done((bf16[208,640]{1,0:T(8,128)(2,1)S(1)}, bf16[208,640]{1,0:T(8,128)(2,1)S(1)}, u32[]{:S(2)}, u32[]{:S(2)}) %collective-permute-start.4) | collective-permute-done | bytes 266272 | tf_op jit(solution)/shard_map/ppermute | solution.py:240
  46.1 3.5 %forward.7 = (bf16[384,768]{1,0:T(8,128)(2,1)S(1)}, bf16[384,384]{1,0:T(8,128)(2,1)S(1)}, bf16[384,256]{1,0:T(8,128)(2,1)S(1)}, f32[384,256]{1,0:T(8,128)S(1)}, ...) custom-call(bf16[208,640]{1,0:T(8,128)(2,1)S(1)} %collective-permute-done.4.refs_0_.refs_23_, ...), custom_call_target="tpu_custom_call" | custom-call | flops 4328521728 | bytes 8000000 | tf_op jit(solution)/shard_map/forward/pallas_call | solution.py:346
  49.6 6.7 %last.1 = (bf16[96,1664]{1,0:T(8,128)(2,1)S(1)}, f32[96,1664]{1,0:T(8,128)S(1)}) custom-call(bf16[208,640]{1,0:T(8,128)(2,1)S(1)} %copy-done.2, bf16[192,768]{1,0:T(8,128)(2,1)S(1)} %get-tuple-element.55.refs_1_, bf16[192,384]{1,0:T(8,128)(2,1)S(1)} %get-tuple-element.56.refs_2_, bf16[192,256]{1,0:T(8,128)(2,1)S(1)} %get-tuple-element.57.refs_3_, ...), custom_call_target="tpu_custom_call" | custom-call | flops 1962934272 | bytes 16000000 | tf_op jit(solution)/shard_map/last/pallas_call | solution.py:361
  56.4 3.1 %collective-permute-start.7 = (bf16[96,1664]{1,0:T(8,128)(2,1)S(1)}, bf16[96,1664]{1,0:T(8,128)(2,1)S(1)}, u32[]{:S(2)}, u32[]{:S(2)}) collective-permute-start(bf16[96,1664]{1,0:T(8,128)(2,1)S(1)} %get-tuple-element.87), channel_id=1, source_target_pairs={{0,1},{1,0},{2,3},{3,2},{4,5},{5,4},{6,7},{7,6},{8,9},{9,8},{10,11... | collective-permute-start | bytes 958472 | tf_op jit(solution)/shard_map/ppermute | solution.py:240
  59.5 1.2 %collective-permute-done.7 = bf16[96,1664]{1,0:T(8,128)(2,1)S(1)} collective-permute-done((bf16[96,1664]{1,0:T(8,128)(2,1)S(1)}, bf16[96,1664]{1,0:T(8,128)(2,1)S(1)}, u32[]{:S(2)}, u32[]{:S(2)}) %collective-permute-start.7) | collective-permute-done | bytes 319520 | tf_op jit(solution)/shard_map/ppermute | solution.py:240
  60.8 1.3 %collective-permute-start.8 = (bf16[96,1664]{1,0:T(8,128)(2,1)S(1)}, bf16[96,1664]{1,0:T(8,128)(2,1)S(1)}, u32[]{:S(2)}, u32[]{:S(2)}) collective-permute-start(bf16[96,1664]{1,0:T(8,128)(2,1)S(1)} %add_convert_fusion.1.one_ref), channel_id=1, source_target_pairs={{0,2},{1,3},{2,0},{3,1},{4,6},{5,7},{6,4},{7,5},{8,10},{9,11},{10,... | collective-permute-start | bytes 958472 | tf_op jit(solution)/shard_map/ppermute | solution.py:240
  62.1 7.5 %collective-permute-done.8.two_ref = bf16[96,1664]{1,0:T(8,128)(2,1)S(1)} collective-permute-done((bf16[96,1664]{1,0:T(8,128)(2,1)S(1)}, bf16[96,1664]{1,0:T(8,128)(2,1)S(1)}, u32[]{:S(2)}, u32[]{:S(2)}) %collective-permute-start.8) | collective-permute-done | bytes 319520 | tf_op jit(solution)/shard_map/ppermute | solution.py:240
  69.7 1.3 %collective-permute-start.9 = (bf16[96,1664]{1,0:T(8,128)(2,1)S(1)}, bf16[96,1664]{1,0:T(8,128)(2,1)S(1)}, u32[]{:S(2)}, u32[]{:S(2)}) collective-permute-start(bf16[96,1664]{1,0:T(8,128)(2,1)S(1)} %add_convert_fusion), channel_id=1, source_target_pairs={{0,1},{1,0},{2,3},{3,2},{4,5},{5,4},{6,7},{7,6},{8,9},{9,8},{10,11... | collective-permute-start | bytes 958472 | tf_op jit(solution)/shard_map/ppermute | solution.py:240
  70.9 1.2 %collective-permute-done.9.far_ref = bf16[96,1664]{1,0:T(8,128)(2,1)S(1)} collective-permute-done((bf16[96,1664]{1,0:T(8,128)(2,1)S(1)}, bf16[96,1664]{1,0:T(8,128)(2,1)S(1)}, u32[]{:S(2)}, u32[]{:S(2)}) %collective-permute-start.9) | collective-permute-done | bytes 319520 | tf_op jit(solution)/shard_map/ppermute | solution.py:240
  72.2 0.9 %finish.1 = (bf16[192,376]{1,0:T(8,128)(2,1)}, bf16[17,192]{1,0:T(8,128)(2,1)}, bf16[192,256]{1,0:T(8,128)(2,1)}, bf16[192,256]{1,0:T(8,128)(2,1)}, bf16[192,376...) custom-call(bf16[96,1664]{1,0:T(8,128)(2,1)S(1)} %add_convert_fusion.1.one_ref, ...), custom_call_target="tpu_custom_call" | custom-call | tf_op jit(solution)/shard_map/finish/pallas_call | solution.py:379
  (22 shorter events, 1.8 us)
Async XLA Ops:
  0.6 10.6 %copy-start.6 = (bf16[256,256]{1,0:T(8,128)(2,1)S(1)}, bf16[256,256]{1,0:T(8,128)(2,1)}, u32[]{:S(2)}) copy-start(bf16[256,256]{1,0:T(8,128)(2,1)} %refs_36_.1) | copy-start | bytes 393220
  2.4 11.9 %collective-permute-start.1 = (bf16[208,640]{1,0:T(8,128)(2,1)}, bf16[208,640]{1,0:T(8,128)(2,1)S(1)}, u32[]{:S(2)}, u32[]{:S(2)}) collective-permute-start(bf16[208,640]{1,0:T(8,128)(2,1)} %pack.1.refs_0_), channel_id=1, source_target_pairs={{0,8},{4,12},{8,0},{12,4},{16,24},{20,28},{24,16},{28,20},{1,9},{5... | collective-permute-start | bytes 798728 | tf_op jit(solution)/shard_map/ppermute | solution.py:240
  2.4 11.9 %collective-permute-start = (bf16[208,640]{1,0:T(8,128)(2,1)}, bf16[208,640]{1,0:T(8,128)(2,1)S(1)}, u32[]{:S(2)}, u32[]{:S(2)}) collective-permute-start(bf16[208,640]{1,0:T(8,128)(2,1)} %pack.1.refs_0_), channel_id=1, source_target_pairs={{0,4},{4,0},{8,12},{12,8},{16,20},{20,16},{24,28},{28,24},{1,5},{5... | collective-permute-start | bytes 798728 | tf_op jit(solution)/shard_map/ppermute | solution.py:240
  3.8 18.4 %collective-permute-start.3 = (bf16[208,640]{1,0:T(8,128)(2,1)}, bf16[208,640]{1,0:T(8,128)(2,1)S(1)}, u32[]{:S(2)}, u32[]{:S(2)}) collective-permute-start(bf16[208,640]{1,0:T(8,128)(2,1)} %pack.1.refs_0_), channel_id=1, source_target_pairs={{0,16},{4,20},{8,24},{12,28},{16,0},{20,4},{24,8},{28,12},{1,17},{... | collective-permute-start | bytes 798728 | tf_op jit(solution)/shard_map/ppermute | solution.py:240
  6.1 22.8 %collective-permute-start.2 = (bf16[208,640]{1,0:T(8,128)(2,1)}, bf16[208,640]{1,0:T(8,128)(2,1)S(1)}, u32[]{:S(2)}, u32[]{:S(2)}) collective-permute-start(bf16[208,640]{1,0:T(8,128)(2,1)} %pack.1.refs_0_), channel_id=1, source_target_pairs={{0,24},{4,28},{8,16},{12,20},{16,8},{20,12},{24,0},{28,4},{1,25},{... | collective-permute-start | bytes 798728 | tf_op jit(solution)/shard_map/ppermute | solution.py:240
  6.3 1.3 %copy-start = (bf16[376,1536]{1,0:T(8,128)(2,1)S(1)}, bf16[376,1536]{1,0:T(8,128)(2,1)}, u32[]{:S(2)}) copy-start(bf16[376,1536]{1,0:T(8,128)(2,1)} %fs_ref.1) | copy-start | bytes 3465220
  7.6 1.3 %copy-start.1 = (bf16[376,1536]{1,0:T(8,128)(2,1)S(1)}, bf16[376,1536]{1,0:T(8,128)(2,1)}, u32[]{:S(2)}) copy-start(bf16[376,1536]{1,0:T(8,128)(2,1)} %bs_ref.1) | copy-start | bytes 3465220
  8.8 1.1 %copy-start.5 = (bf16[256,1536]{1,0:T(8,128)(2,1)S(1)}, bf16[256,1536]{1,0:T(8,128)(2,1)}, u32[]{:S(2)}) copy-start(bf16[256,1536]{1,0:T(8,128)(2,1)} %fl_ref.1) | copy-start | bytes 2359300
  10.0 0.9 %copy-start.7 = (bf16[17,1536]{1,0:T(8,128)(2,1)S(1)}, bf16[17,1536]{1,0:T(8,128)(2,1)}, u32[]{:S(2)}) copy-start(bf16[17,1536]{1,0:T(8,128)(2,1)} %fa_ref.1) | copy-start | bytes 156676
  10.8 1.0 %copy-start.2 = (bf16[208,640]{1,0:T(8,128)(2,1)S(1)}, bf16[208,640]{1,0:T(8,128)(2,1)}, u32[]{:S(2)}) copy-start(bf16[208,640]{1,0:T(8,128)(2,1)} %pack.1.refs_0_) | copy-start | bytes 798724
  10.8 1.2 %copy-start.3 = (bf16[1536,256]{1,0:T(8,128)(2,1)S(1)}, bf16[1536,256]{1,0:T(8,128)(2,1)}, u32[]{:S(2)}) copy-start(bf16[1536,256]{1,0:T(8,128)(2,1)} %refs_34_.1) | copy-start | bytes 2359300
  10.8 1.5 %copy-start.4 = (bf16[1536,256]{1,0:T(8,128)(2,1)S(1)}, bf16[1536,256]{1,0:T(8,128)(2,1)}, u32[]{:S(2)}) copy-start(bf16[1536,256]{1,0:T(8,128)(2,1)} %refs_35_.1) | copy-start | bytes 2359300
  28.9 17.2 %collective-permute-start.5 = (bf16[208,640]{1,0:T(8,128)(2,1)S(1)}, bf16[208,640]{1,0:T(8,128)(2,1)S(1)}, u32[]{:S(2)}, u32[]{:S(2)}) collective-permute-start(bf16[208,640]{1,0:T(8,128)(2,1)S(1)} %collective-permute-done.2.refs_0_.refs_15_), channel_id=1, source_target_pairs={{0,4},{4,0},{8,12},{12,8},{16,20},{20,16},{24,28},{28,24},{1,5},{5... | collective-permute-start | bytes 798728 | tf_op jit(solution)/shard_map/ppermute | solution.py:240
  29.2 20.4 %collective-permute-start.6 = (bf16[208,640]{1,0:T(8,128)(2,1)S(1)}, bf16[208,640]{1,0:T(8,128)(2,1)S(1)}, u32[]{:S(2)}, u32[]{:S(2)}) collective-permute-start(bf16[208,640]{1,0:T(8,128)(2,1)S(1)} %collective-permute-done.3.refs_1_.refs_16_), channel_id=1, source_target_pairs={{0,4},{4,0},{8,12},{12,8},{16,20},{20,16},{24,28},{28,24},{1,5},{5... | collective-permute-start | bytes 798728 | tf_op jit(solution)/shard_map/ppermute | solution.py:240
  30.4 15.7 %collective-permute-start.4 = (bf16[208,640]{1,0:T(8,128)(2,1)S(1)}, bf16[208,640]{1,0:T(8,128)(2,1)S(1)}, u32[]{:S(2)}, u32[]{:S(2)}) collective-permute-start(bf16[208,640]{1,0:T(8,128)(2,1)S(1)} %collective-permute-done.1.refs_1_.refs_8_), channel_id=1, source_target_pairs={{0,4},{4,0},{8,12},{12,8},{16,20},{20,16},{24,28},{28,24},{1,5},{5... | collective-permute-start | bytes 798728 | tf_op jit(solution)/shard_map/ppermute | solution.py:240
  56.4 4.3 %collective-permute-start.7 = (bf16[96,1664]{1,0:T(8,128)(2,1)S(1)}, bf16[96,1664]{1,0:T(8,128)(2,1)S(1)}, u32[]{:S(2)}, u32[]{:S(2)}) collective-permute-start(bf16[96,1664]{1,0:T(8,128)(2,1)S(1)} %get-tuple-element.87), channel_id=1, source_target_pairs={{0,1},{1,0},{2,3},{3,2},{4,5},{5,4},{6,7},{7,6},{8,9},{9,8},{10,11... | collective-permute-start | bytes 958472 | tf_op jit(solution)/shard_map/ppermute | solution.py:240
  60.8 8.8 %collective-permute-start.8 = (bf16[96,1664]{1,0:T(8,128)(2,1)S(1)}, bf16[96,1664]{1,0:T(8,128)(2,1)S(1)}, u32[]{:S(2)}, u32[]{:S(2)}) collective-permute-start(bf16[96,1664]{1,0:T(8,128)(2,1)S(1)} %add_convert_fusion.1.one_ref), channel_id=1, source_target_pairs={{0,2},{1,3},{2,0},{3,1},{4,6},{5,7},{6,4},{7,5},{8,10},{9,11},{10,... | collective-permute-start | bytes 958472 | tf_op jit(solution)/shard_map/ppermute | solution.py:240
  69.7 2.5 %collective-permute-start.9 = (bf16[96,1664]{1,0:T(8,128)(2,1)S(1)}, bf16[96,1664]{1,0:T(8,128)(2,1)S(1)}, u32[]{:S(2)}, u32[]{:S(2)}) collective-permute-start(bf16[96,1664]{1,0:T(8,128)(2,1)S(1)} %add_convert_fusion), channel_id=1, source_target_pairs={{0,1},{1,0},{2,3},{3,2},{4,5},{5,4},{6,7},{7,6},{8,9},{9,8},{10,11... | collective-permute-start | bytes 958472 | tf_op jit(solution)/shard_map/ppermute | solution.py:240

commit v4 on v3

--- a/solution.py
+++ b/solution.py
@@ -56,15 +56,24 @@
     out_ref[rows:, lane : 2 * lane] = side_ref[half:side, :].astype(BF16)
 
 
-def weights_kernel(cfg, fs_ref, fa_ref, fl_ref, bs_ref, wf_ref, wb_ref, wfb_ref, wbb_ref):
+def weights_kernel(cfg, fs_hbm, fa_hbm, fl_hbm, bs_hbm, *refs):
     obs, obs_pad, x_pad = cfg["obs"], cfg["obs_pad"], cfg["x_pad"]
     hidden, block, act = cfg["hidden"], cfg["block"], cfg["act"]
+    wf_ref, wb_ref, wfb_ref, wbb_ref, fs_ref, fa_ref, fl_ref, bs_ref, sems = refs
+    pairs = ((fs_hbm, fs_ref), (bs_hbm, bs_ref), (fl_hbm, fl_ref), (fa_hbm, fa_ref))
+    copies = [pltpu.make_async_copy(a, b, sems.at[i]) for i, (a, b) in enumerate(pairs)]
+    for copy in copies:
+        copy.start()
     gap = jnp.zeros((obs_pad - obs, hidden), BF16)
+    wf_ref[obs_pad:x_pad, :] = jnp.zeros((x_pad - obs_pad, hidden), BF16)
+    copies[0].wait()
     wf_ref[0:obs_pad, :] = jnp.concatenate([fs_ref[...], gap], axis=0)
-    wf_ref[obs_pad:x_pad, :] = jnp.zeros((x_pad - obs_pad, hidden), BF16)
+    copies[1].wait()
+    wb_ref[...] = jnp.concatenate([bs_ref[...], gap], axis=0)
+    copies[2].wait()
+    wf_ref[x_pad:, :] = fl_ref[...]
+    copies[3].wait()
     wf_ref[obs_pad : obs_pad + act, :] = fa_ref[...]
-    wf_ref[x_pad:, :] = fl_ref[...]
-    wb_ref[...] = jnp.concatenate([bs_ref[...], gap], axis=0)
     me = lax.axis_index("dp")
     start = me * block
     base = pl.multiple_of(start // LANES * LANES, LANES)
@@ -302,9 +311,20 @@
         compiler_params=pltpu.CompilerParams(vmem_limit_bytes=VMEM_LIMIT),
         name="pack",
     )(states, actions[0].T, next_index, latent_ids, target_forward)
-    x = {0: own}
-    for step in (4, 6, 1, 2):
-        x[step] = exchange(own, "dp", size, step)
+    x = {"own": own}
+    middle = [(2 + i, 4 + i) for i in range(2)] + [(4 + i, 2 + i) for i in range(2)]
+    outward = [(2 + i, i) for i in range(2)] + [(4 + i, 6 + i) for i in range(2)]
+    across = lax.ppermute(own, "dp", middle)
+    x["x own"] = exchange(own, "dp", size, 1)
+    x["half"] = exchange(own, "dp", size, 2)
+    handed = lax.ppermute(across, "dp", outward)
+    x["x half"] = exchange(x["half"], "dp", size, 1)
+    across_two = lax.ppermute(x["half"], "dp", middle)
+    x["second"] = across + handed
+    x["x second"] = exchange(x["second"], "dp", size, 1)
+    handed_two = lax.ppermute(across_two, "dp", outward)
+    x["third"] = across_two + handed_two
+    x["x third"] = exchange(x["third"], "dp", size, 1)
     wf, wb, wfb, wbb = pl.pallas_call(
         functools.partial(weights_kernel, cfg),
         out_shape=(
@@ -313,10 +333,18 @@
             shape((block, x_pad + rank), BF16),
             shape((block, obs_pad), BF16),
         ),
-        compiler_params=pltpu.CompilerParams(vmem_limit_bytes=24 * 1024 * 1024),
+        in_specs=[pl.BlockSpec(memory_space=pl.ANY)] * 4,
+        scratch_shapes=[
+            pltpu.VMEM((obs, hidden), BF16),
+            pltpu.VMEM((act, hidden), BF16),
+            pltpu.VMEM((rank, hidden), BF16),
+            pltpu.VMEM((obs, hidden), BF16),
+            pltpu.SemaphoreType.DMA((4,)),
+        ],
+        compiler_params=pltpu.CompilerParams(vmem_limit_bytes=16 * 1024 * 1024),
         cost_estimate=pl.CostEstimate(flops=0, bytes_accessed=8_000_000, transcendentals=0),
         name="weights",
-    )(f_state, f_action, f_latent, b_state)
+    )(*(pltpu.with_memory_space_constraint(w, pltpu.HBM) for w in (f_state, f_action, f_latent, b_state)))
     weights = (wf, wb, f_output, b_output, latents, wfb, wbb)
     row_flops = 2 * (c1 + 2 * rank + obs_pad) * hidden + 8 * rank * rank
 
@@ -332,16 +360,10 @@
         )
 
     grams = ()
-    plan = ((0,), (1, 2), (6, 4), (3, 7))
+    plan = (("own", "half"), ("x own", "x half"), ("second", "third"), ("x second",))
     early = []
     for steps in plan:
         count = len(steps)
-        if steps == (1, 2):
-            x[3] = exchange(x[2], "dp", size, 1)
-        if steps == (6, 4):
-            far, near, grams = lax.optimization_barrier((x[6], x[4], grams))
-            x[5] = exchange(near, "dp", size, 1)
-            x[7] = exchange(far, "dp", size, 1)
         xs = [x[step] for step in steps]
         *saved, total_grams = pl.pallas_call(
             functools.partial(forward_kernel, cfg, count, not early),
@@ -354,7 +376,7 @@
         )(*xs, *weights, *grams)
         grams = (total_grams,)
         early.append((xs, saved))
-    left = [x[step] for step in range(size) if all(step not in steps for steps in plan)]
+    left = [x["x third"]]
     operands = []
     for xs, saved in early:
         operands += [*xs, *saved]

time: 73.6 us -> 62.3 us (0.85)
  the two profiles are of different devices: /device:TPU:9 before, /device:TPU:0 now
where the time goes in v4:
time: 62.3 us; the launch traced here: 62.1 us
  Pallas kernels  23.9 us (38%)
  waiting for transfers between devices  22.6 us (36%)
  starting transfers between devices  14.3 us (23%)
  between operations  0.96 us (2%)
    ppermute x8, waiting for transfers between devices, exchange(): return lax.ppermute(array, axis, [(i, i ^ bit) for i in range(size)])  13.5 us
    pallas_call x4, Pallas kernels, fast_local(): pl.pallas_call(functools.partial(forward_kernel, cfg, count, not early),...  12.5 us
    ppermute x8, starting transfers between devices, exchange(): return lax.ppermute(array, axis, [(i, i ^ bit) for i in range(size)])  10.2 us
    pallas_call x1, Pallas kernels, fast_local(): pl.pallas_call(functools.partial(last_kernel, cfg, [len(xs) for xs, _ in...  6.52 us
    ppermute x1, waiting for transfers between devices, fast_local(): handed = lax.ppermute(across, 'dp', outward)  5.79 us
    ppermute x1, waiting for transfers between devices, fast_local(): handed_two = lax.ppermute(across_two, 'dp', outward)  3.3 us
    pallas_call x1, Pallas kernels, fast_local(): pl.pallas_call(functools.partial(weights_kernel, cfg), out_shape=(shape((...  2.17 us
    pallas_call x1, Pallas kernels, fast_local(): pl.pallas_call(functools.partial(pack_kernel, cfg), out_shape=shape((rows...  1.74 us
  transfers between devices with their start and end apart: 12, of which 6 were waited for; matrix products, arithmetic and copies ran while one was open for 0% of the time, Pallas kernels for 24%

profile of v4, /device:TPU:0, one launch (start us, length us, event | category | flops | bytes accessed | tf_op | source)
XLA Modules:
  0.0 62.1 jit_solution(4429287838803481143)
XLA Ops:
  0.6 1.7 %pack.1.refs_0_ = bf16[208,640]{1,0:T(8,128)(2,1)} custom-call(bf16[1,192,376]{2,1,0:T(8,128)(2,1)} %state_ref.1, bf16[17,192]{1,0:T(8,128)(2,1)} %bitcast.7, s32[1,192]{1,0:T(1,128)} %next_ref.1, s32[1,192]{1,0:T(1,128)} %latent_ref.1, bf16[1,192,256]{2,1,0:T(8,128)(2,1)} %target_ref.1), custom_call_target="tpu_custom_call" | custom-call | tf_op jit(solution)/shard_map/pack/pallas_call | solution.py:307
  2.4 3.1 %collective-permute-start = (bf16[208,640]{1,0:T(8,128)(2,1)}, bf16[208,640]{1,0:T(8,128)(2,1)S(1)}, u32[]{:S(2)}, u32[]{:S(2)}) collective-permute-start(bf16[208,640]{1,0:T(8,128)(2,1)} %pack.1.refs_0_), channel_id=1, source_target_pairs={{0,8},{4,12},{8,0},{12,4},{16,24},{20,28},{24,16},{28,20},{1,9},{5... | collective-permute-start | bytes 798728 | tf_op jit(solution)/shard_map/ppermute | solution.py:249
  5.5 0.7 %collective-permute-start.3 = (bf16[208,640]{1,0:T(8,128)(2,1)}, bf16[208,640]{1,0:T(8,128)(2,1)S(1)}, u32[]{:S(2)}, u32[]{:S(2)}) collective-permute-start(bf16[208,640]{1,0:T(8,128)(2,1)} %pack.1.refs_0_), channel_id=1, source_target_pairs={{8,16},{12,20},{16,8},{20,12},{9,17},{13,21},{17,9},{21,13},{10,18... | collective-permute-start | bytes 798728 | tf_op jit(solution)/shard_map/ppermute | solution.py:317
  6.1 1.6 %collective-permute-start.1 = (bf16[208,640]{1,0:T(8,128)(2,1)}, bf16[208,640]{1,0:T(8,128)(2,1)S(1)}, u32[]{:S(2)}, u32[]{:S(2)}) collective-permute-start(bf16[208,640]{1,0:T(8,128)(2,1)} %pack.1.refs_0_), channel_id=1, source_target_pairs={{0,4},{4,0},{8,12},{12,8},{16,20},{20,16},{24,28},{28,24},{1,5},{5... | collective-permute-start | bytes 798728 | tf_op jit(solution)/shard_map/ppermute | solution.py:249
  7.7 2.2 %weights.1 = (bf16[768,1536]{1,0:T(8,128)(2,1)S(1)}, bf16[384,1536]{1,0:T(8,128)(2,1)S(1)}, bf16[192,768]{1,0:T(8,128)(2,1)S(1)}, bf16[192,384]{1,0:T(8,128)(2,1)S(1)}) custom-call(bf16[376,1536]{1,0:T(8,128)(2,1)} %fs_hbm.1, bf16[17,1536]{1,0:T(8,128)(2,1)} %fa_hbm.1, bf16[256,1536]{1,0:T(8,128)(2,1)} %fl_hbm.1, bf16[376,1536]{1,0:T(8,128)(2,1)} %bs_hbm.1), custom_call_target="tpu_custom_call" | custom-call | bytes 8000000 | tf_op jit(solution)/shard_map/weights/pallas_call | solution.py:328
  9.9 2.2 %collective-permute-done.refs_1_ = bf16[208,640]{1,0:T(8,128)(2,1)S(1)} collective-permute-done((bf16[208,640]{1,0:T(8,128)(2,1)}, bf16[208,640]{1,0:T(8,128)(2,1)S(1)}, u32[]{:S(2)}, u32[]{:S(2)}) %collective-permute-start) | collective-permute-done | bytes 266272 | tf_op jit(solution)/shard_map/ppermute | solution.py:249
  12.1 0.7 %collective-permute-start.5 = (bf16[208,640]{1,0:T(8,128)(2,1)S(1)}, bf16[208,640]{1,0:T(8,128)(2,1)S(1)}, u32[]{:S(2)}, u32[]{:S(2)}) collective-permute-start(bf16[208,640]{1,0:T(8,128)(2,1)S(1)} %collective-permute-done.refs_1_), channel_id=1, source_target_pairs={{8,16},{12,20},{16,8},{20,12},{9,17},{13,21},{17,9},{21,13},{10,18... | collective-permute-start | bytes 798728 | tf_op jit(solution)/shard_map/ppermute | solution.py:322
  12.8 1.7 %collective-permute-start.2 = (bf16[208,640]{1,0:T(8,128)(2,1)S(1)}, bf16[208,640]{1,0:T(8,128)(2,1)S(1)}, u32[]{:S(2)}, u32[]{:S(2)}) collective-permute-start(bf16[208,640]{1,0:T(8,128)(2,1)S(1)} %collective-permute-done.refs_1_), channel_id=1, source_target_pairs={{0,4},{4,0},{8,12},{12,8},{16,20},{20,16},{24,28},{28,24},{1,5},{5... | collective-permute-start | bytes 798728 | tf_op jit(solution)/shard_map/ppermute | solution.py:249
  14.5 1.3 %collective-permute-start.4 = (bf16[208,640]{1,0:T(8,128)(2,1)S(1)}, bf16[208,640]{1,0:T(8,128)(2,1)S(1)}, u32[]{:S(2)}, u32[]{:S(2)}) collective-permute-start(bf16[208,640]{1,0:T(8,128)(2,1)S(1)} %collective-permute-done.3), channel_id=1, source_target_pairs={{8,0},{12,4},{16,24},{20,28},{9,1},{13,5},{17,25},{21,29},{10,2},{... | collective-permute-start | bytes 798728 | tf_op jit(solution)/shard_map/ppermute | solution.py:320
  15.8 3.5 %forward.4 = (bf16[384,768]{1,0:T(8,128)(2,1)S(1)}, bf16[384,384]{1,0:T(8,128)(2,1)S(1)}, bf16[384,256]{1,0:T(8,128)(2,1)S(1)}, f32[384,256]{1,0:T(8,128)S(1)}, ...) custom-call(bf16[208,640]{1,0:T(8,128)(2,1)S(1)} %copy-done, ...), custom_call_target="tpu_custom_call" | custom-call | flops 4328521728 | bytes 8000000 | tf_op jit(solution)/shard_map/forward/pallas_call | solution.py:368
  19.3 5.8 %collective-permute-done.4 = bf16[208,640]{1,0:T(8,128)(2,1)S(1)} collective-permute-done((bf16[208,640]{1,0:T(8,128)(2,1)S(1)}, bf16[208,640]{1,0:T(8,128)(2,1)S(1)}, u32[]{:S(2)}, u32[]{:S(2)}) %collective-permute-start.4) | collective-permute-done | bytes 266272 | tf_op jit(solution)/shard_map/ppermute | solution.py:320
  25.2 0.6 collective-permute-start.7
  25.8 1.5 %collective-permute-start.6 = (bf16[208,640]{1,0:T(8,128)(2,1)S(1)}, bf16[208,640]{1,0:T(8,128)(2,1)S(1)}, u32[]{:S(2)}, u32[]{:S(2)}) collective-permute-start(bf16[208,640]{1,0:T(8,128)(2,1)S(1)} %collective-permute-done.5), channel_id=1, source_target_pairs={{8,0},{12,4},{16,24},{20,28},{9,1},{13,5},{17,25},{21,29},{10,2},{... | collective-permute-start | bytes 798728 | tf_op jit(solution)/shard_map/ppermute | solution.py:325
  27.3 3.5 %forward.5 = (bf16[384,768]{1,0:T(8,128)(2,1)S(1)}, bf16[384,384]{1,0:T(8,128)(2,1)S(1)}, bf16[384,256]{1,0:T(8,128)(2,1)S(1)}, f32[384,256]{1,0:T(8,128)S(1)}, ...) custom-call(bf16[208,640]{1,0:T(8,128)(2,1)S(1)} %collective-permute-done.1.refs_0_.refs_8_, ...), custom_call_target="tpu_custom_call" | custom-call | flops 4328521728 | bytes 8000000 | tf_op jit(solution)/shard_map/forward/pallas_call | solution.py:368
  30.8 3.3 %collective-permute-done.6 = bf16[208,640]{1,0:T(8,128)(2,1)S(1)} collective-permute-done((bf16[208,640]{1,0:T(8,128)(2,1)S(1)}, bf16[208,640]{1,0:T(8,128)(2,1)S(1)}, u32[]{:S(2)}, u32[]{:S(2)}) %collective-permute-start.6) | collective-permute-done | bytes 266272 | tf_op jit(solution)/shard_map/ppermute | solution.py:325
  34.1 1.6 %collective-permute-start.8 = (bf16[208,640]{1,0:T(8,128)(2,1)S(1)}, bf16[208,640]{1,0:T(8,128)(2,1)S(1)}, u32[]{:S(2)}, u32[]{:S(2)}) collective-permute-start(bf16[208,640]{1,0:T(8,128)(2,1)S(1)} %add.13.refs_1_.refs_17_), channel_id=1, source_target_pairs={{0,4},{4,0},{8,12},{12,8},{16,20},{20,16},{24,28},{28,24},{1,5},{5... | collective-permute-start | bytes 798728 | tf_op jit(solution)/shard_map/ppermute | solution.py:249
  35.7 3.5 %forward.6 = (bf16[384,768]{1,0:T(8,128)(2,1)S(1)}, bf16[384,384]{1,0:T(8,128)(2,1)S(1)}, bf16[384,256]{1,0:T(8,128)(2,1)S(1)}, f32[384,256]{1,0:T(8,128)S(1)}, ...) custom-call(bf16[208,640]{1,0:T(8,128)(2,1)S(1)} %add.12.refs_0_.refs_16_, ...), custom_call_target="tpu_custom_call" | custom-call | flops 4328521728 | bytes 8000000 | tf_op jit(solution)/shard_map/forward/pallas_call | solution.py:368
  39.2 2.0 %forward.7 = (bf16[192,768]{1,0:T(8,128)(2,1)S(1)}, bf16[192,384]{1,0:T(8,128)(2,1)S(1)}, bf16[192,256]{1,0:T(8,128)(2,1)S(1)}, f32[192,256]{1,0:T(8,128)S(1)}, ...) custom-call(bf16[208,640]{1,0:T(8,128)(2,1)S(1)} %collective-permute-done.7.refs_0_.refs_24_, ...), custom_call_target="tpu_custom_call" | custom-call | flops 2164260864 | bytes 8000000 | tf_op jit(solution)/shard_map/forward/pallas_call | solution.py:368
  41.3 6.5 %last.1 = (bf16[96,1664]{1,0:T(8,128)(2,1)S(1)}, f32[96,1664]{1,0:T(8,128)S(1)}) custom-call(bf16[208,640]{1,0:T(8,128)(2,1)S(1)} %copy-done, bf16[208,640]{1,0:T(8,128)(2,1)S(1)} %collective-permute-done.refs_1_, bf16[384,768]{1,0:T(8,128)(2,1)S(1)} %get-tuple-element.52.refs_2_, bf16[384,384]{1,0:T(8,128)(2,1)S(1)} %get-tuple-element.53.refs_3_, ...), custom_call_target="tpu_custom_call" | custom-call | flops 1962934272 | bytes 16000000 | tf_op jit(solution)/shard_map/last/pallas_call | solution.py:383
  47.9 1.6 %collective-permute-done.9 = bf16[96,1664]{1,0:T(8,128)(2,1)S(1)} collective-permute-done((bf16[96,1664]{1,0:T(8,128)(2,1)S(1)}, bf16[96,1664]{1,0:T(8,128)(2,1)S(1)}, u32[]{:S(2)}, u32[]{:S(2)}) %collective-permute-start.9) | collective-permute-done | bytes 319520 | tf_op jit(solution)/shard_map/ppermute | solution.py:249
  49.5 1.6 %collective-permute-start.10 = (bf16[96,1664]{1,0:T(8,128)(2,1)S(1)}, bf16[96,1664]{1,0:T(8,128)(2,1)S(1)}, u32[]{:S(2)}, u32[]{:S(2)}) collective-permute-start(bf16[96,1664]{1,0:T(8,128)(2,1)S(1)} %add_convert_fusion.1.one_ref), channel_id=1, source_target_pairs={{0,2},{1,3},{2,0},{3,1},{4,6},{5,7},{6,4},{7,5},{8,10},{9,11},{10,... | collective-permute-start | bytes 958472 | tf_op jit(solution)/shard_map/ppermute | solution.py:249
  51.1 8.1 %collective-permute-done.10.two_ref = bf16[96,1664]{1,0:T(8,128)(2,1)S(1)} collective-permute-done((bf16[96,1664]{1,0:T(8,128)(2,1)S(1)}, bf16[96,1664]{1,0:T(8,128)(2,1)S(1)}, u32[]{:S(2)}, u32[]{:S(2)}) %collective-permute-start.10) | collective-permute-done | bytes 319520 | tf_op jit(solution)/shard_map/ppermute | solution.py:249
  59.3 1.6 %collective-permute-done.11.far_ref = bf16[96,1664]{1,0:T(8,128)(2,1)S(1)} collective-permute-done((bf16[96,1664]{1,0:T(8,128)(2,1)S(1)}, bf16[96,1664]{1,0:T(8,128)(2,1)S(1)}, u32[]{:S(2)}, u32[]{:S(2)}) %collective-permute-start.11) | collective-permute-done | bytes 319520 | tf_op jit(solution)/shard_map/ppermute | solution.py:249
  60.9 0.9 %finish.1 = (bf16[192,376]{1,0:T(8,128)(2,1)}, bf16[17,192]{1,0:T(8,128)(2,1)}, bf16[192,256]{1,0:T(8,128)(2,1)}, bf16[192,256]{1,0:T(8,128)(2,1)}, bf16[192,376...) custom-call(bf16[96,1664]{1,0:T(8,128)(2,1)S(1)} %add_convert_fusion.1.one_ref, ...), custom_call_target="tpu_custom_call" | custom-call | tf_op jit(solution)/shard_map/finish/pallas_call | solution.py:401
  (20 shorter events, 0.5 us)
Async XLA Ops:
  2.4 13.4 %copy-start = (bf16[208,640]{1,0:T(8,128)(2,1)S(1)}, bf16[208,640]{1,0:T(8,128)(2,1)}, u32[]{:S(2)}) copy-start(bf16[208,640]{1,0:T(8,128)(2,1)} %pack.1.refs_0_) | copy-start | bytes 798724
  2.4 13.4 %copy-start.1 = (bf16[1536,256]{1,0:T(8,128)(2,1)S(1)}, bf16[1536,256]{1,0:T(8,128)(2,1)}, u32[]{:S(2)}) copy-start(bf16[1536,256]{1,0:T(8,128)(2,1)} %refs_34_.1) | copy-start | bytes 2359300
  2.4 13.4 %copy-start.2 = (bf16[1536,256]{1,0:T(8,128)(2,1)S(1)}, bf16[1536,256]{1,0:T(8,128)(2,1)}, u32[]{:S(2)}) copy-start(bf16[1536,256]{1,0:T(8,128)(2,1)} %refs_35_.1) | copy-start | bytes 2359300
  2.4 13.4 %copy-start.3 = (bf16[256,256]{1,0:T(8,128)(2,1)S(1)}, bf16[256,256]{1,0:T(8,128)(2,1)}, u32[]{:S(2)}) copy-start(bf16[256,256]{1,0:T(8,128)(2,1)} %refs_36_.1) | copy-start | bytes 393220
  2.4 9.7 %collective-permute-start = (bf16[208,640]{1,0:T(8,128)(2,1)}, bf16[208,640]{1,0:T(8,128)(2,1)S(1)}, u32[]{:S(2)}, u32[]{:S(2)}) collective-permute-start(bf16[208,640]{1,0:T(8,128)(2,1)} %pack.1.refs_0_), channel_id=1, source_target_pairs={{0,8},{4,12},{8,0},{12,4},{16,24},{20,28},{24,16},{28,20},{1,9},{5... | collective-permute-start | bytes 798728 | tf_op jit(solution)/shard_map/ppermute | solution.py:249
  5.5 9.0 %collective-permute-start.3 = (bf16[208,640]{1,0:T(8,128)(2,1)}, bf16[208,640]{1,0:T(8,128)(2,1)S(1)}, u32[]{:S(2)}, u32[]{:S(2)}) collective-permute-start(bf16[208,640]{1,0:T(8,128)(2,1)} %pack.1.refs_0_), channel_id=1, source_target_pairs={{8,16},{12,20},{16,8},{20,12},{9,17},{13,21},{17,9},{21,13},{10,18... | collective-permute-start | bytes 798728 | tf_op jit(solution)/shard_map/ppermute | solution.py:317
  6.1 21.1 %collective-permute-start.1 = (bf16[208,640]{1,0:T(8,128)(2,1)}, bf16[208,640]{1,0:T(8,128)(2,1)S(1)}, u32[]{:S(2)}, u32[]{:S(2)}) collective-permute-start(bf16[208,640]{1,0:T(8,128)(2,1)} %pack.1.refs_0_), channel_id=1, source_target_pairs={{0,4},{4,0},{8,12},{12,8},{16,20},{20,16},{24,28},{28,24},{1,5},{5... | collective-permute-start | bytes 798728 | tf_op jit(solution)/shard_map/ppermute | solution.py:249
  12.1 13.7 %collective-permute-start.5 = (bf16[208,640]{1,0:T(8,128)(2,1)S(1)}, bf16[208,640]{1,0:T(8,128)(2,1)S(1)}, u32[]{:S(2)}, u32[]{:S(2)}) collective-permute-start(bf16[208,640]{1,0:T(8,128)(2,1)S(1)} %collective-permute-done.refs_1_), channel_id=1, source_target_pairs={{8,16},{12,20},{16,8},{20,12},{9,17},{13,21},{17,9},{21,13},{10,18... | collective-permute-start | bytes 798728 | tf_op jit(solution)/shard_map/ppermute | solution.py:322
  12.8 14.5 %collective-permute-start.2 = (bf16[208,640]{1,0:T(8,128)(2,1)S(1)}, bf16[208,640]{1,0:T(8,128)(2,1)S(1)}, u32[]{:S(2)}, u32[]{:S(2)}) collective-permute-start(bf16[208,640]{1,0:T(8,128)(2,1)S(1)} %collective-permute-done.refs_1_), channel_id=1, source_target_pairs={{0,4},{4,0},{8,12},{12,8},{16,20},{20,16},{24,28},{28,24},{1,5},{5... | collective-permute-start | bytes 798728 | tf_op jit(solution)/shard_map/ppermute | solution.py:249
  14.5 10.6 %collective-permute-start.4 = (bf16[208,640]{1,0:T(8,128)(2,1)S(1)}, bf16[208,640]{1,0:T(8,128)(2,1)S(1)}, u32[]{:S(2)}, u32[]{:S(2)}) collective-permute-start(bf16[208,640]{1,0:T(8,128)(2,1)S(1)} %collective-permute-done.3), channel_id=1, source_target_pairs={{8,0},{12,4},{16,24},{20,28},{9,1},{13,5},{17,25},{21,29},{10,2},{... | collective-permute-start | bytes 798728 | tf_op jit(solution)/shard_map/ppermute | solution.py:320
  25.2 14.0 %collective-permute-start.7 = (bf16[208,640]{1,0:T(8,128)(2,1)S(1)}, bf16[208,640]{1,0:T(8,128)(2,1)S(1)}, u32[]{:S(2)}, u32[]{:S(2)}) collective-permute-start(bf16[208,640]{1,0:T(8,128)(2,1)S(1)} %add.12.refs_0_.refs_16_), channel_id=1, source_target_pairs={{0,4},{4,0},{8,12},{12,8},{16,20},{20,16},{24,28},{28,24},{1,5},{5... | collective-permute-start | bytes 798728 | tf_op jit(solution)/shard_map/ppermute | solution.py:249
  25.8 8.3 %collective-permute-start.6 = (bf16[208,640]{1,0:T(8,128)(2,1)S(1)}, bf16[208,640]{1,0:T(8,128)(2,1)S(1)}, u32[]{:S(2)}, u32[]{:S(2)}) collective-permute-start(bf16[208,640]{1,0:T(8,128)(2,1)S(1)} %collective-permute-done.5), channel_id=1, source_target_pairs={{8,0},{12,4},{16,24},{20,28},{9,1},{13,5},{17,25},{21,29},{10,2},{... | collective-permute-start | bytes 798728 | tf_op jit(solution)/shard_map/ppermute | solution.py:325
  34.1 7.1 %collective-permute-start.8 = (bf16[208,640]{1,0:T(8,128)(2,1)S(1)}, bf16[208,640]{1,0:T(8,128)(2,1)S(1)}, u32[]{:S(2)}, u32[]{:S(2)}) collective-permute-start(bf16[208,640]{1,0:T(8,128)(2,1)S(1)} %add.13.refs_1_.refs_17_), channel_id=1, source_target_pairs={{0,4},{4,0},{8,12},{12,8},{16,20},{20,16},{24,28},{28,24},{1,5},{5... | collective-permute-start | bytes 798728 | tf_op jit(solution)/shard_map/ppermute | solution.py:249
  47.8 1.7 %collective-permute-start.9 = (bf16[96,1664]{1,0:T(8,128)(2,1)S(1)}, bf16[96,1664]{1,0:T(8,128)(2,1)S(1)}, u32[]{:S(2)}, u32[]{:S(2)}) collective-permute-start(bf16[96,1664]{1,0:T(8,128)(2,1)S(1)} %get-tuple-element.81), channel_id=1, source_target_pairs={{0,1},{1,0},{2,3},{3,2},{4,5},{5,4},{6,7},{7,6},{8,9},{9,8},{10,11... | collective-permute-start | bytes 958472 | tf_op jit(solution)/shard_map/ppermute | solution.py:249
  49.5 9.6 %collective-permute-start.10 = (bf16[96,1664]{1,0:T(8,128)(2,1)S(1)}, bf16[96,1664]{1,0:T(8,128)(2,1)S(1)}, u32[]{:S(2)}, u32[]{:S(2)}) collective-permute-start(bf16[96,1664]{1,0:T(8,128)(2,1)S(1)} %add_convert_fusion.1.one_ref), channel_id=1, source_target_pairs={{0,2},{1,3},{2,0},{3,1},{4,6},{5,7},{6,4},{7,5},{8,10},{9,11},{10,... | collective-permute-start | bytes 958472 | tf_op jit(solution)/shard_map/ppermute | solution.py:249
  59.3 1.7 %collective-permute-start.11 = (bf16[96,1664]{1,0:T(8,128)(2,1)S(1)}, bf16[96,1664]{1,0:T(8,128)(2,1)S(1)}, u32[]{:S(2)}, u32[]{:S(2)}) collective-permute-start(bf16[96,1664]{1,0:T(8,128)(2,1)S(1)} %add_convert_fusion), channel_id=1, source_target_pairs={{0,1},{1,0},{2,3},{3,2},{4,5},{5,4},{6,7},{7,6},{8,9},{9,8},{10,11... | collective-permute-start | bytes 958472 | tf_op jit(solution)/shard_map/ppermute | solution.py:249

commit v5 on v4

--- a/solution.py
+++ b/solution.py
@@ -342,7 +342,7 @@
             pltpu.SemaphoreType.DMA((4,)),
         ],
         compiler_params=pltpu.CompilerParams(vmem_limit_bytes=16 * 1024 * 1024),
-        cost_estimate=pl.CostEstimate(flops=0, bytes_accessed=8_000_000, transcendentals=0),
+        cost_estimate=pl.CostEstimate(flops=0, bytes_accessed=1_000_000, transcendentals=0),
         name="weights",
     )(*(pltpu.with_memory_space_constraint(w, pltpu.HBM) for w in (f_state, f_action, f_latent, b_state)))
     weights = (wf, wb, f_output, b_output, latents, wfb, wbb)
@@ -360,9 +360,15 @@
         )
 
     grams = ()
-    plan = (("own", "half"), ("x own", "x half"), ("second", "third"), ("x second",))
+    plan = (
+        (("own",), 3.0),
+        (("half",), 2.0),
+        (("x own",), 1.5),
+        (("x half", "second"), 1.0),
+        (("third", "x second"), 3.0),
+    )
     early = []
-    for steps in plan:
+    for steps, work in plan:
         count = len(steps)
         xs = [x[step] for step in steps]
         *saved, total_grams = pl.pallas_call(
@@ -370,7 +376,9 @@
             out_shape=(*(shape(*item) for item in kept(count)), shape((rank, 2 * rank), F32)),
             compiler_params=params,
             cost_estimate=pl.CostEstimate(
-                flops=2 * rows * count * row_flops, bytes_accessed=8_000_000, transcendentals=0
+                flops=int(work * rows * count * row_flops),
+                bytes_accessed=1_000_000,
+                transcendentals=0,
             ),
             name="forward",
         )(*xs, *weights, *grams)

time: 62.3 us -> 60.7 us (0.974)
  waiting for transfers between devices: 22.6 us -> 16.5 us
  starting transfers between devices: 14.3 us -> 18 us
  Pallas kernels: 23.9 us -> 24.8 us
    ppermute x1, waiting for transfers between devices: 5.79 us -> 0.79 us  [fast_local(): handed = lax.ppermute(across, 'dp', outward)]
    ppermute x8, starting transfers between devices: 10.2 us -> 13.8 us  [exchange(): return lax.ppermute(array, axis, [(i, i ^ bit) for i in range(size)])]
    ppermute x1, waiting for transfers between devices: 3.3 us -> 1.65 us  [fast_local(): handed_two = lax.ppermute(across_two, 'dp', outward)]
    pallas_call x4 -> x5, Pallas kernels: 12.5 us -> 13.1 us  [fast_local(): pl.pallas_call(functools.partial(forward_kernel, cfg, count, not early),...]
  transfers between devices with their start and end apart: 12 -> 12, of which waited for: 6 -> 7; matrix products, arithmetic and copies ran while one was open for 0% -> 0% of each run, Pallas kernels for 24% -> 25%
where the time goes in v5:
time: 60.7 us; the launch traced here: 60.5 us
  Pallas kernels  24.8 us (41%)
  starting transfers between devices  18 us (30%)
  waiting for transfers between devices  16.5 us (27%)
  between operations  0.96 us (2%)
    ppermute x8, waiting for transfers between devices, exchange(): return lax.ppermute(array, axis, [(i, i ^ bit) for i in range(size)])  14 us
    ppermute x8, starting transfers between devices, exchange(): return lax.ppermute(array, axis, [(i, i ^ bit) for i in range(size)])  13.8 us
    pallas_call x5, Pallas kernels, fast_local(): pl.pallas_call(functools.partial(forward_kernel, cfg, count, not early),...  13.1 us
    pallas_call x1, Pallas kernels, fast_local(): pl.pallas_call(functools.partial(last_kernel, cfg, [len(xs) for xs, _ in...  6.77 us
    pallas_call x1, Pallas kernels, fast_local(): pl.pallas_call(functools.partial(weights_kernel, cfg), out_shape=(shape((...  2.17 us
    pallas_call x1, Pallas kernels, fast_local(): pl.pallas_call(functools.partial(pack_kernel, cfg), out_shape=shape((rows...  1.74 us
    ppermute x1, waiting for transfers between devices, fast_local(): handed_two = lax.ppermute(across_two, 'dp', outward)  1.65 us
    ppermute x1, starting transfers between devices, fast_local(): handed_two = lax.ppermute(across_two, 'dp', outward)  1.46 us
  transfers between devices with their start and end apart: 12, of which 7 were waited for; matrix products, arithmetic and copies ran while one was open for 0% of the time, Pallas kernels for 25%

profile of v5, /device:TPU:0, one launch (start us, length us, event | category | flops | bytes accessed | tf_op | source)
XLA Modules:
  0.0 60.5 jit_solution(15917941267230948073)
XLA Ops:
  0.6 1.7 %pack.1.refs_0_ = bf16[208,640]{1,0:T(8,128)(2,1)} custom-call(bf16[1,192,376]{2,1,0:T(8,128)(2,1)} %state_ref.1, bf16[17,192]{1,0:T(8,128)(2,1)} %bitcast.7, s32[1,192]{1,0:T(1,128)} %next_ref.1, s32[1,192]{1,0:T(1,128)} %latent_ref.1, bf16[1,192,256]{2,1,0:T(8,128)(2,1)} %target_ref.1), custom_call_target="tpu_custom_call" | custom-call | tf_op jit(solution)/shard_map/pack/pallas_call | solution.py:307
  2.4 0.8 %collective-permute-start.3 = (bf16[208,640]{1,0:T(8,128)(2,1)}, bf16[208,640]{1,0:T(8,128)(2,1)S(1)}, u32[]{:S(2)}, u32[]{:S(2)}) collective-permute-start(bf16[208,640]{1,0:T(8,128)(2,1)} %pack.1.refs_0_), channel_id=1, source_target_pairs={{8,16},{12,20},{16,8},{20,12},{9,17},{13,21},{17,9},{21,13},{10,18... | collective-permute-start | bytes 798728 | tf_op jit(solution)/shard_map/ppermute | solution.py:317
  3.2 5.9 %collective-permute-start = (bf16[208,640]{1,0:T(8,128)(2,1)}, bf16[208,640]{1,0:T(8,128)(2,1)S(1)}, u32[]{:S(2)}, u32[]{:S(2)}) collective-permute-start(bf16[208,640]{1,0:T(8,128)(2,1)} %pack.1.refs_0_), channel_id=1, source_target_pairs={{0,8},{4,12},{8,0},{12,4},{16,24},{20,28},{24,16},{28,20},{1,9},{5... | collective-permute-start | bytes 798728 | tf_op jit(solution)/shard_map/ppermute | solution.py:249
  9.1 1.5 %collective-permute-start.1 = (bf16[208,640]{1,0:T(8,128)(2,1)}, bf16[208,640]{1,0:T(8,128)(2,1)S(1)}, u32[]{:S(2)}, u32[]{:S(2)}) collective-permute-start(bf16[208,640]{1,0:T(8,128)(2,1)} %pack.1.refs_0_), channel_id=1, source_target_pairs={{0,4},{4,0},{8,12},{12,8},{16,20},{20,16},{24,28},{28,24},{1,5},{5... | collective-permute-start | bytes 798728 | tf_op jit(solution)/shard_map/ppermute | solution.py:249
  10.6 2.2 %weights.1 = (bf16[768,1536]{1,0:T(8,128)(2,1)S(1)}, bf16[384,1536]{1,0:T(8,128)(2,1)S(1)}, bf16[192,768]{1,0:T(8,128)(2,1)S(1)}, bf16[192,384]{1,0:T(8,128)(2,1)S(1)}) custom-call(bf16[376,1536]{1,0:T(8,128)(2,1)} %fs_hbm.1, bf16[17,1536]{1,0:T(8,128)(2,1)} %fa_hbm.1, bf16[256,1536]{1,0:T(8,128)(2,1)} %fl_hbm.1, bf16[376,1536]{1,0:T(8,128)(2,1)} %bs_hbm.1), custom_call_target="tpu_custom_call" | custom-call | bytes 1000000 | tf_op jit(solution)/shard_map/weights/pallas_call | solution.py:328
  12.8 1.3 %collective-permute-start.4 = (bf16[208,640]{1,0:T(8,128)(2,1)S(1)}, bf16[208,640]{1,0:T(8,128)(2,1)S(1)}, u32[]{:S(2)}, u32[]{:S(2)}) collective-permute-start(bf16[208,640]{1,0:T(8,128)(2,1)S(1)} %collective-permute-done.3), channel_id=1, source_target_pairs={{8,0},{12,4},{16,24},{20,28},{9,1},{13,5},{17,25},{21,29},{10,2},{... | collective-permute-start | bytes 798728 | tf_op jit(solution)/shard_map/ppermute | solution.py:320
  14.1 1.3 %collective-permute-done.refs_0_.refs_7_ = bf16[208,640]{1,0:T(8,128)(2,1)S(1)} collective-permute-done((bf16[208,640]{1,0:T(8,128)(2,1)}, bf16[208,640]{1,0:T(8,128)(2,1)S(1)}, u32[]{:S(2)}, u32[]{:S(2)}) %collective-permute-start) | collective-permute-done | bytes 266272 | tf_op jit(solution)/shard_map/ppermute | solution.py:249
  16.1 2.0 %forward.5 = (bf16[192,768]{1,0:T(8,128)(2,1)S(1)}, bf16[192,384]{1,0:T(8,128)(2,1)S(1)}, bf16[192,256]{1,0:T(8,128)(2,1)S(1)}, f32[192,256]{1,0:T(8,128)S(1)}, ...) custom-call(bf16[208,640]{1,0:T(8,128)(2,1)S(1)} %copy-done.2, ...), custom_call_target="tpu_custom_call" | custom-call | flops 3246391296 | bytes 1000000 | tf_op jit(solution)/shard_map/forward/pallas_call | solution.py:374
  18.2 1.6 %collective-permute-start.2 = (bf16[208,640]{1,0:T(8,128)(2,1)S(1)}, bf16[208,640]{1,0:T(8,128)(2,1)S(1)}, u32[]{:S(2)}, u32[]{:S(2)}) collective-permute-start(bf16[208,640]{1,0:T(8,128)(2,1)S(1)} %collective-permute-done.refs_0_.refs_7_), channel_id=1, source_target_pairs={{0,4},{4,0},{8,12},{12,8},{16,20},{20,16},{24,28},{28,24},{1,5},{5... | collective-permute-start | bytes 798728 | tf_op jit(solution)/shard_map/ppermute | solution.py:249
  19.7 2.0 %forward.6 = (bf16[192,768]{1,0:T(8,128)(2,1)S(1)}, bf16[192,384]{1,0:T(8,128)(2,1)S(1)}, bf16[192,256]{1,0:T(8,128)(2,1)S(1)}, f32[192,256]{1,0:T(8,128)S(1)}, ...) custom-call(bf16[208,640]{1,0:T(8,128)(2,1)S(1)} %collective-permute-done.refs_0_.refs_7_, ...), custom_call_target="tpu_custom_call" | custom-call | flops 2164260864 | bytes 1000000 | tf_op jit(solution)/shard_map/forward/pallas_call | solution.py:374
  22.6 1.6 %collective-permute-start.7 = (bf16[208,640]{1,0:T(8,128)(2,1)S(1)}, bf16[208,640]{1,0:T(8,128)(2,1)S(1)}, u32[]{:S(2)}, u32[]{:S(2)}) collective-permute-start(bf16[208,640]{1,0:T(8,128)(2,1)S(1)} %add.12.refs_1_.refs_22_), channel_id=1, source_target_pairs={{0,4},{4,0},{8,12},{12,8},{16,20},{20,16},{24,28},{28,24},{1,5},{5... | collective-permute-start | bytes 798728 | tf_op jit(solution)/shard_map/ppermute | solution.py:249
  24.2 1.5 %collective-permute-start.6 = (bf16[208,640]{1,0:T(8,128)(2,1)S(1)}, bf16[208,640]{1,0:T(8,128)(2,1)S(1)}, u32[]{:S(2)}, u32[]{:S(2)}) collective-permute-start(bf16[208,640]{1,0:T(8,128)(2,1)S(1)} %collective-permute-done.5), channel_id=1, source_target_pairs={{8,0},{12,4},{16,24},{20,28},{9,1},{13,5},{17,25},{21,29},{10,2},{... | collective-permute-start | bytes 798728 | tf_op jit(solution)/shard_map/ppermute | solution.py:325
  25.7 2.0 %forward.7 = (bf16[192,768]{1,0:T(8,128)(2,1)S(1)}, bf16[192,384]{1,0:T(8,128)(2,1)S(1)}, bf16[192,256]{1,0:T(8,128)(2,1)S(1)}, f32[192,256]{1,0:T(8,128)S(1)}, ...) custom-call(bf16[208,640]{1,0:T(8,128)(2,1)S(1)} %collective-permute-done.1.refs_0_.refs_14_, ...), custom_call_target="tpu_custom_call" | custom-call | flops 1623195648 | bytes 1000000 | tf_op jit(solution)/shard_map/forward/pallas_call | solution.py:374
  27.7 3.5 %forward.8 = (bf16[384,768]{1,0:T(8,128)(2,1)S(1)}, bf16[384,384]{1,0:T(8,128)(2,1)S(1)}, bf16[384,256]{1,0:T(8,128)(2,1)S(1)}, f32[384,256]{1,0:T(8,128)S(1)}, ...) custom-call(bf16[208,640]{1,0:T(8,128)(2,1)S(1)} %collective-permute-done.2.refs_0_.refs_21_, ...), custom_call_target="tpu_custom_call" | custom-call | flops 2164260864 | bytes 1000000 | tf_op jit(solution)/shard_map/forward/pallas_call | solution.py:374
  31.3 1.6 %collective-permute-done.6 = bf16[208,640]{1,0:T(8,128)(2,1)S(1)} collective-permute-done((bf16[208,640]{1,0:T(8,128)(2,1)S(1)}, bf16[208,640]{1,0:T(8,128)(2,1)S(1)}, u32[]{:S(2)}, u32[]{:S(2)}) %collective-permute-start.6) | collective-permute-done | bytes 266272 | tf_op jit(solution)/shard_map/ppermute | solution.py:325
  33.0 1.6 %collective-permute-start.8 = (bf16[208,640]{1,0:T(8,128)(2,1)S(1)}, bf16[208,640]{1,0:T(8,128)(2,1)S(1)}, u32[]{:S(2)}, u32[]{:S(2)}) collective-permute-start(bf16[208,640]{1,0:T(8,128)(2,1)S(1)} %add.13.refs_0_.refs_29_), channel_id=1, source_target_pairs={{0,4},{4,0},{8,12},{12,8},{16,20},{20,16},{24,28},{28,24},{1,5},{5... | collective-permute-start | bytes 798728 | tf_op jit(solution)/shard_map/ppermute | solution.py:249
  34.5 3.5 %forward.9 = (bf16[384,768]{1,0:T(8,128)(2,1)S(1)}, bf16[384,384]{1,0:T(8,128)(2,1)S(1)}, bf16[384,256]{1,0:T(8,128)(2,1)S(1)}, f32[384,256]{1,0:T(8,128)S(1)}, ...) custom-call(bf16[208,640]{1,0:T(8,128)(2,1)S(1)} %add.13.refs_0_.refs_29_, ...), custom_call_target="tpu_custom_call" | custom-call | flops 6492782592 | bytes 1000000 | tf_op jit(solution)/shard_map/forward/pallas_call | solution.py:374
  38.0 1.4 %collective-permute-done.8.refs_37_ = bf16[208,640]{1,0:T(8,128)(2,1)S(1)} collective-permute-done((bf16[208,640]{1,0:T(8,128)(2,1)S(1)}, bf16[208,640]{1,0:T(8,128)(2,1)S(1)}, u32[]{:S(2)}, u32[]{:S(2)}) %collective-permute-start.8) | collective-permute-done | bytes 266272 | tf_op jit(solution)/shard_map/ppermute | solution.py:249
  39.5 6.8 %last.1 = (bf16[96,1664]{1,0:T(8,128)(2,1)S(1)}, f32[96,1664]{1,0:T(8,128)S(1)}) custom-call(bf16[208,640]{1,0:T(8,128)(2,1)S(1)} %copy-done.2, bf16[192,768]{1,0:T(8,128)(2,1)S(1)} %get-tuple-element.59.refs_1_, bf16[192,384]{1,0:T(8,128)(2,1)S(1)} %get-tuple-element.60.refs_2_, bf16[192,256]{1,0:T(8,128)(2,1)S(1)} %get-tuple-element.61.refs_3_, ...), custom_call_target="tpu_custom_call" | custom-call | flops 1962934272 | bytes 16000000 | tf_op jit(solution)/shard_map/last/pallas_call | solution.py:391
  46.3 1.6 %collective-permute-done.9 = bf16[96,1664]{1,0:T(8,128)(2,1)S(1)} collective-permute-done((bf16[96,1664]{1,0:T(8,128)(2,1)S(1)}, bf16[96,1664]{1,0:T(8,128)(2,1)S(1)}, u32[]{:S(2)}, u32[]{:S(2)}) %collective-permute-start.9) | collective-permute-done | bytes 319520 | tf_op jit(solution)/shard_map/ppermute | solution.py:249
  48.0 1.6 %collective-permute-start.10 = (bf16[96,1664]{1,0:T(8,128)(2,1)S(1)}, bf16[96,1664]{1,0:T(8,128)(2,1)S(1)}, u32[]{:S(2)}, u32[]{:S(2)}) collective-permute-start(bf16[96,1664]{1,0:T(8,128)(2,1)S(1)} %add_convert_fusion.1.one_ref), channel_id=1, source_target_pairs={{0,2},{1,3},{2,0},{3,1},{4,6},{5,7},{6,4},{7,5},{8,10},{9,11},{10,... | collective-permute-start | bytes 958472 | tf_op jit(solution)/shard_map/ppermute | solution.py:249
  49.6 8.1 %collective-permute-done.10.two_ref = bf16[96,1664]{1,0:T(8,128)(2,1)S(1)} collective-permute-done((bf16[96,1664]{1,0:T(8,128)(2,1)S(1)}, bf16[96,1664]{1,0:T(8,128)(2,1)S(1)}, u32[]{:S(2)}, u32[]{:S(2)}) %collective-permute-start.10) | collective-permute-done | bytes 319520 | tf_op jit(solution)/shard_map/ppermute | solution.py:249
  57.8 1.6 %collective-permute-done.11.far_ref = bf16[96,1664]{1,0:T(8,128)(2,1)S(1)} collective-permute-done((bf16[96,1664]{1,0:T(8,128)(2,1)S(1)}, bf16[96,1664]{1,0:T(8,128)(2,1)S(1)}, u32[]{:S(2)}, u32[]{:S(2)}) %collective-permute-start.11) | collective-permute-done | bytes 319520 | tf_op jit(solution)/shard_map/ppermute | solution.py:249
  59.4 0.9 %finish.1 = (bf16[192,376]{1,0:T(8,128)(2,1)}, bf16[17,192]{1,0:T(8,128)(2,1)}, bf16[192,256]{1,0:T(8,128)(2,1)}, bf16[192,256]{1,0:T(8,128)(2,1)}, bf16[192,376...) custom-call(bf16[96,1664]{1,0:T(8,128)(2,1)S(1)} %add_convert_fusion.1.one_ref, ...), custom_call_target="tpu_custom_call" | custom-call | tf_op jit(solution)/shard_map/finish/pallas_call | solution.py:409
  (21 shorter events, 1.9 us)
Async XLA Ops:
  2.4 13.7 %copy-start = (bf16[1536,256]{1,0:T(8,128)(2,1)S(1)}, bf16[1536,256]{1,0:T(8,128)(2,1)}, u32[]{:S(2)}) copy-start(bf16[1536,256]{1,0:T(8,128)(2,1)} %refs_40_.1) | copy-start | bytes 2359300
  2.4 13.7 %copy-start.1 = (bf16[1536,256]{1,0:T(8,128)(2,1)S(1)}, bf16[1536,256]{1,0:T(8,128)(2,1)}, u32[]{:S(2)}) copy-start(bf16[1536,256]{1,0:T(8,128)(2,1)} %refs_41_.1) | copy-start | bytes 2359300
  2.4 13.7 %copy-start.2 = (bf16[208,640]{1,0:T(8,128)(2,1)S(1)}, bf16[208,640]{1,0:T(8,128)(2,1)}, u32[]{:S(2)}) copy-start(bf16[208,640]{1,0:T(8,128)(2,1)} %pack.1.refs_0_) | copy-start | bytes 798724
  2.4 13.8 %copy-start.3 = (bf16[256,256]{1,0:T(8,128)(2,1)S(1)}, bf16[256,256]{1,0:T(8,128)(2,1)}, u32[]{:S(2)}) copy-start(bf16[256,256]{1,0:T(8,128)(2,1)} %refs_42_.1) | copy-start | bytes 393220
  2.4 10.4 %collective-permute-start.3 = (bf16[208,640]{1,0:T(8,128)(2,1)}, bf16[208,640]{1,0:T(8,128)(2,1)S(1)}, u32[]{:S(2)}, u32[]{:S(2)}) collective-permute-start(bf16[208,640]{1,0:T(8,128)(2,1)} %pack.1.refs_0_), channel_id=1, source_target_pairs={{8,16},{12,20},{16,8},{20,12},{9,17},{13,21},{17,9},{21,13},{10,18... | collective-permute-start | bytes 798728 | tf_op jit(solution)/shard_map/ppermute | solution.py:317
  3.2 12.2 %collective-permute-start = (bf16[208,640]{1,0:T(8,128)(2,1)}, bf16[208,640]{1,0:T(8,128)(2,1)S(1)}, u32[]{:S(2)}, u32[]{:S(2)}) collective-permute-start(bf16[208,640]{1,0:T(8,128)(2,1)} %pack.1.refs_0_), channel_id=1, source_target_pairs={{0,8},{4,12},{8,0},{12,4},{16,24},{20,28},{24,16},{28,20},{1,9},{5... | collective-permute-start | bytes 798728 | tf_op jit(solution)/shard_map/ppermute | solution.py:249
  9.1 16.6 %collective-permute-start.1 = (bf16[208,640]{1,0:T(8,128)(2,1)}, bf16[208,640]{1,0:T(8,128)(2,1)S(1)}, u32[]{:S(2)}, u32[]{:S(2)}) collective-permute-start(bf16[208,640]{1,0:T(8,128)(2,1)} %pack.1.refs_0_), channel_id=1, source_target_pairs={{0,4},{4,0},{8,12},{12,8},{16,20},{20,16},{24,28},{28,24},{1,5},{5... | collective-permute-start | bytes 798728 | tf_op jit(solution)/shard_map/ppermute | solution.py:249
  12.8 9.8 %collective-permute-start.4 = (bf16[208,640]{1,0:T(8,128)(2,1)S(1)}, bf16[208,640]{1,0:T(8,128)(2,1)S(1)}, u32[]{:S(2)}, u32[]{:S(2)}) collective-permute-start(bf16[208,640]{1,0:T(8,128)(2,1)S(1)} %collective-permute-done.3), channel_id=1, source_target_pairs={{8,0},{12,4},{16,24},{20,28},{9,1},{13,5},{17,25},{21,29},{10,2},{... | collective-permute-start | bytes 798728 | tf_op jit(solution)/shard_map/ppermute | solution.py:320
  15.4 8.8 %collective-permute-start.5 = (bf16[208,640]{1,0:T(8,128)(2,1)S(1)}, bf16[208,640]{1,0:T(8,128)(2,1)S(1)}, u32[]{:S(2)}, u32[]{:S(2)}) collective-permute-start(bf16[208,640]{1,0:T(8,128)(2,1)S(1)} %collective-permute-done.refs_0_.refs_7_), channel_id=1, source_target_pairs={{8,16},{12,20},{16,8},{20,12},{9,17},{13,21},{17,9},{21,13},{10,18... | collective-permute-start | bytes 798728 | tf_op jit(solution)/shard_map/ppermute | solution.py:322
  18.2 9.5 %collective-permute-start.2 = (bf16[208,640]{1,0:T(8,128)(2,1)S(1)}, bf16[208,640]{1,0:T(8,128)(2,1)S(1)}, u32[]{:S(2)}, u32[]{:S(2)}) collective-permute-start(bf16[208,640]{1,0:T(8,128)(2,1)S(1)} %collective-permute-done.refs_0_.refs_7_), channel_id=1, source_target_pairs={{0,4},{4,0},{8,12},{12,8},{16,20},{20,16},{24,28},{28,24},{1,5},{5... | collective-permute-start | bytes 798728 | tf_op jit(solution)/shard_map/ppermute | solution.py:249
  22.6 11.9 %collective-permute-start.7 = (bf16[208,640]{1,0:T(8,128)(2,1)S(1)}, bf16[208,640]{1,0:T(8,128)(2,1)S(1)}, u32[]{:S(2)}, u32[]{:S(2)}) collective-permute-start(bf16[208,640]{1,0:T(8,128)(2,1)S(1)} %add.12.refs_1_.refs_22_), channel_id=1, source_target_pairs={{0,4},{4,0},{8,12},{12,8},{16,20},{20,16},{24,28},{28,24},{1,5},{5... | collective-permute-start | bytes 798728 | tf_op jit(solution)/shard_map/ppermute | solution.py:249
  24.2 8.7 %collective-permute-start.6 = (bf16[208,640]{1,0:T(8,128)(2,1)S(1)}, bf16[208,640]{1,0:T(8,128)(2,1)S(1)}, u32[]{:S(2)}, u32[]{:S(2)}) collective-permute-start(bf16[208,640]{1,0:T(8,128)(2,1)S(1)} %collective-permute-done.5), channel_id=1, source_target_pairs={{8,0},{12,4},{16,24},{20,28},{9,1},{13,5},{17,25},{21,29},{10,2},{... | collective-permute-start | bytes 798728 | tf_op jit(solution)/shard_map/ppermute | solution.py:325
  33.0 6.5 %collective-permute-start.8 = (bf16[208,640]{1,0:T(8,128)(2,1)S(1)}, bf16[208,640]{1,0:T(8,128)(2,1)S(1)}, u32[]{:S(2)}, u32[]{:S(2)}) collective-permute-start(bf16[208,640]{1,0:T(8,128)(2,1)S(1)} %add.13.refs_0_.refs_29_), channel_id=1, source_target_pairs={{0,4},{4,0},{8,12},{12,8},{16,20},{20,16},{24,28},{28,24},{1,5},{5... | collective-permute-start | bytes 798728 | tf_op jit(solution)/shard_map/ppermute | solution.py:249
  46.2 1.7 %collective-permute-start.9 = (bf16[96,1664]{1,0:T(8,128)(2,1)S(1)}, bf16[96,1664]{1,0:T(8,128)(2,1)S(1)}, u32[]{:S(2)}, u32[]{:S(2)}) collective-permute-start(bf16[96,1664]{1,0:T(8,128)(2,1)S(1)} %get-tuple-element.95), channel_id=1, source_target_pairs={{0,1},{1,0},{2,3},{3,2},{4,5},{5,4},{6,7},{7,6},{8,9},{9,8},{10,11... | collective-permute-start | bytes 958472 | tf_op jit(solution)/shard_map/ppermute | solution.py:249
  48.0 9.6 %collective-permute-start.10 = (bf16[96,1664]{1,0:T(8,128)(2,1)S(1)}, bf16[96,1664]{1,0:T(8,128)(2,1)S(1)}, u32[]{:S(2)}, u32[]{:S(2)}) collective-permute-start(bf16[96,1664]{1,0:T(8,128)(2,1)S(1)} %add_convert_fusion.1.one_ref), channel_id=1, source_target_pairs={{0,2},{1,3},{2,0},{3,1},{4,6},{5,7},{6,4},{7,5},{8,10},{9,11},{10,... | collective-permute-start | bytes 958472 | tf_op jit(solution)/shard_map/ppermute | solution.py:249
  57.7 1.7 %collective-permute-start.11 = (bf16[96,1664]{1,0:T(8,128)(2,1)S(1)}, bf16[96,1664]{1,0:T(8,128)(2,1)S(1)}, u32[]{:S(2)}, u32[]{:S(2)}) collective-permute-start(bf16[96,1664]{1,0:T(8,128)(2,1)S(1)} %add_convert_fusion), channel_id=1, source_target_pairs={{0,1},{1,0},{2,3},{3,2},{4,5},{5,4},{6,7},{7,6},{8,9},{9,8},{10,11... | collective-permute-start | bytes 958472 | tf_op jit(solution)/shard_map/ppermute | solution.py:249

commit v6 on v5

--- a/solution.py
+++ b/solution.py
@@ -33,6 +33,14 @@
 
 def dot_tn(left, right):
     return lax.dot_general(left, right, (((0,), (0,)), ((), ())), preferred_element_type=F32)
+
+
+def join(values, axis):
+    return jnp.concatenate(values, axis=axis) if len(values) > 1 else values[0]
+
+
+def stack(refs, axis):
+    return join([ref[...] for ref in refs], axis)
 
 
 def split_two(value):
@@ -164,15 +172,20 @@
     me = pl.multiple_of(lax.axis_index("dp") * block, ROW_TILE)
     fo = weights[2][pl.ds(me, block), :]
     bo = weights[3][pl.ds(me, block), :]
+    few = [item for item in groups if len(item[0]) == 1]
+    many = [item for item in groups if len(item[0]) > 1]
     square = jnp.zeros((1, rank), F32)
     diagonal = jnp.zeros((1, rank), F32)
-    for index, (x_refs, (a_ref, later_ref, f_ref, u_ref, fh_ref, bh_ref)) in enumerate(groups):
-        emb32 = f_ref[...].astype(F32)
-        targets = [x_ref[0:rows, obs_pad:] for x_ref in x_refs]
-        target = jnp.concatenate(targets, axis=0) if len(targets) > 1 else targets[0]
+    f_deltas, b_deltas, f_hids, b_hids, d_fs, d_us, wholes, laters = ([] for _ in range(8))
+    for members in (few, many):
+        if not members:
+            continue
+        saved = list(zip(*(item[1] for item in members)))
+        emb32 = stack(saved[2], 0).astype(F32)
+        target = join([x_ref[0:rows, obs_pad:] for item in members for x_ref in item[0]], 0)
         error = emb32 - GAMMA * target.astype(F32)
         err_hi, err_lo = split_two(error)
-        u = u_ref[...]
+        u = stack(saved[3], 0)
         scale = lax.rsqrt(jnp.mean(u * u, axis=-1, keepdims=True) + EPSILON)
         back = (u * scale).astype(BF16)
         back32 = back.astype(F32)
@@ -184,21 +197,20 @@
         d_b = factor * (pushed / group - emb32)
         inner = jnp.mean(u * d_b, axis=-1, keepdims=True)
         d_u = (scale * d_b - u * (scale * scale * scale * inner)).astype(BF16)
-        f_hid, b_hid = fh_ref[...], bh_ref[...]
+        f_hid, b_hid = stack(saved[4], 1), stack(saved[5], 1)
         zero = jnp.zeros_like(f_hid)
-        f_delta = jnp.where(f_hid > 0, dot_nt(fo, d_f).astype(BF16), zero)
-        b_delta = jnp.where(b_hid > 0, dot_nt(bo, d_u).astype(BF16), zero)
-        sums = (
-            (0, c1, dot_nn(f_delta, a_ref[...])),
-            (c1, c2, dot_nn(f_hid, d_f)),
-            (c2, c3, dot_nn(b_delta, later_ref[...])),
-            (c3, part_ref.shape[1], dot_nn(b_hid, d_u)),
-        )
-        for low, high, value in sums:
-            if index == 0:
-                part_ref[:, low:high] = value
-            else:
-                part_ref[:, low:high] += value
+        f_deltas.append(jnp.where(f_hid > 0, dot_nt(fo, d_f).astype(BF16), zero))
+        b_deltas.append(jnp.where(b_hid > 0, dot_nt(bo, d_u).astype(BF16), zero))
+        f_hids.append(f_hid)
+        b_hids.append(b_hid)
+        d_fs.append(d_f)
+        d_us.append(d_u)
+        wholes += saved[0]
+        laters += saved[1]
+    part_ref[:, :c1] = dot_nn(join(f_deltas, 1), stack(wholes, 0))
+    part_ref[:, c1:c2] = dot_nn(join(f_hids, 1), join(d_fs, 0))
+    part_ref[:, c2:c3] = dot_nn(join(b_deltas, 1), stack(laters, 0))
+    part_ref[:, c3:] = dot_nn(join(b_hids, 1), join(d_us, 0))
     loss = (0.5 / group) * jnp.sum(square) - jnp.sum(diagonal)
     lanes = lax.broadcasted_iota(jnp.int32, (block, LANES), 1)
     spot = cfg["loss_spot"]

time: 60.7 us -> 60 us (0.988)
  Pallas kernels: 24.8 us -> 24.1 us
    pallas_call x1, Pallas kernels: 6.77 us -> 6.1 us  [fast_local(): pl.pallas_call(functools.partial(last_kernel, cfg, [len(xs) for xs, _ in...]
  transfers between devices with their start and end apart: 12 -> 12, of which waited for: 7 -> 7; matrix products, arithmetic and copies ran while one was open for 0% -> 0% of each run, Pallas kernels for 25% -> 26%
where the time goes in v6:
time: 60 us; the launch traced here: 59.8 us
  Pallas kernels  24.1 us (40%)
  starting transfers between devices  18 us (30%)
  waiting for transfers between devices  16.5 us (28%)
  between operations  0.96 us (2%)
    ppermute x8, waiting for transfers between devices, exchange(): return lax.ppermute(array, axis, [(i, i ^ bit) for i in range(size)])  14 us
    ppermute x8, starting transfers between devices, exchange(): return lax.ppermute(array, axis, [(i, i ^ bit) for i in range(size)])  13.8 us
    pallas_call x5, Pallas kernels, fast_local(): pl.pallas_call(functools.partial(forward_kernel, cfg, count, not early),...  13.1 us
    pallas_call x1, Pallas kernels, fast_local(): pl.pallas_call(functools.partial(last_kernel, cfg, [len(xs) for xs, _ in...  6.1 us
    pallas_call x1, Pallas kernels, fast_local(): pl.pallas_call(functools.partial(weights_kernel, cfg), out_shape=(shape((...  2.17 us
    pallas_call x1, Pallas kernels, fast_local(): pl.pallas_call(functools.partial(pack_kernel, cfg), out_shape=shape((rows...  1.74 us
    ppermute x1, waiting for transfers between devices, fast_local(): handed_two = lax.ppermute(across_two, 'dp', outward)  1.65 us
    ppermute x1, starting transfers between devices, fast_local(): handed_two = lax.ppermute(across_two, 'dp', outward)  1.46 us
  transfers between devices with their start and end apart: 12, of which 7 were waited for; matrix products, arithmetic and copies ran while one was open for 0% of the time, Pallas kernels for 26%

profile of v6, /device:TPU:0, one launch (start us, length us, event | category | flops | bytes accessed | tf_op | source)
XLA Modules:
  0.0 59.8 jit_solution(10233891798099426826)
XLA Ops:
  0.6 1.7 %pack.1.refs_0_ = bf16[208,640]{1,0:T(8,128)(2,1)} custom-call(bf16[1,192,376]{2,1,0:T(8,128)(2,1)} %state_ref.1, bf16[17,192]{1,0:T(8,128)(2,1)} %bitcast.7, s32[1,192]{1,0:T(1,128)} %next_ref.1, s32[1,192]{1,0:T(1,128)} %latent_ref.1, bf16[1,192,256]{2,1,0:T(8,128)(2,1)} %target_ref.1), custom_call_target="tpu_custom_call" | custom-call | tf_op jit(solution)/shard_map/pack/pallas_call | solution.py:319
  2.4 0.8 %collective-permute-start.3 = (bf16[208,640]{1,0:T(8,128)(2,1)}, bf16[208,640]{1,0:T(8,128)(2,1)S(1)}, u32[]{:S(2)}, u32[]{:S(2)}) collective-permute-start(bf16[208,640]{1,0:T(8,128)(2,1)} %pack.1.refs_0_), channel_id=1, source_target_pairs={{8,16},{12,20},{16,8},{20,12},{9,17},{13,21},{17,9},{21,13},{10,18... | collective-permute-start | bytes 798728 | tf_op jit(solution)/shard_map/ppermute | solution.py:329
  3.2 5.9 %collective-permute-start = (bf16[208,640]{1,0:T(8,128)(2,1)}, bf16[208,640]{1,0:T(8,128)(2,1)S(1)}, u32[]{:S(2)}, u32[]{:S(2)}) collective-permute-start(bf16[208,640]{1,0:T(8,128)(2,1)} %pack.1.refs_0_), channel_id=1, source_target_pairs={{0,8},{4,12},{8,0},{12,4},{16,24},{20,28},{24,16},{28,20},{1,9},{5... | collective-permute-start | bytes 798728 | tf_op jit(solution)/shard_map/ppermute | solution.py:261
  9.1 1.5 %collective-permute-start.1 = (bf16[208,640]{1,0:T(8,128)(2,1)}, bf16[208,640]{1,0:T(8,128)(2,1)S(1)}, u32[]{:S(2)}, u32[]{:S(2)}) collective-permute-start(bf16[208,640]{1,0:T(8,128)(2,1)} %pack.1.refs_0_), channel_id=1, source_target_pairs={{0,4},{4,0},{8,12},{12,8},{16,20},{20,16},{24,28},{28,24},{1,5},{5... | collective-permute-start | bytes 798728 | tf_op jit(solution)/shard_map/ppermute | solution.py:261
  10.6 2.2 %weights.1 = (bf16[768,1536]{1,0:T(8,128)(2,1)S(1)}, bf16[384,1536]{1,0:T(8,128)(2,1)S(1)}, bf16[192,768]{1,0:T(8,128)(2,1)S(1)}, bf16[192,384]{1,0:T(8,128)(2,1)S(1)}) custom-call(bf16[376,1536]{1,0:T(8,128)(2,1)} %fs_hbm.1, bf16[17,1536]{1,0:T(8,128)(2,1)} %fa_hbm.1, bf16[256,1536]{1,0:T(8,128)(2,1)} %fl_hbm.1, bf16[376,1536]{1,0:T(8,128)(2,1)} %bs_hbm.1), custom_call_target="tpu_custom_call" | custom-call | bytes 1000000 | tf_op jit(solution)/shard_map/weights/pallas_call | solution.py:340
  12.8 1.3 %collective-permute-start.4 = (bf16[208,640]{1,0:T(8,128)(2,1)S(1)}, bf16[208,640]{1,0:T(8,128)(2,1)S(1)}, u32[]{:S(2)}, u32[]{:S(2)}) collective-permute-start(bf16[208,640]{1,0:T(8,128)(2,1)S(1)} %collective-permute-done.3), channel_id=1, source_target_pairs={{8,0},{12,4},{16,24},{20,28},{9,1},{13,5},{17,25},{21,29},{10,2},{... | collective-permute-start | bytes 798728 | tf_op jit(solution)/shard_map/ppermute | solution.py:332
  14.1 1.3 %collective-permute-done.refs_0_.refs_7_ = bf16[208,640]{1,0:T(8,128)(2,1)S(1)} collective-permute-done((bf16[208,640]{1,0:T(8,128)(2,1)}, bf16[208,640]{1,0:T(8,128)(2,1)S(1)}, u32[]{:S(2)}, u32[]{:S(2)}) %collective-permute-start) | collective-permute-done | bytes 266272 | tf_op jit(solution)/shard_map/ppermute | solution.py:261
  16.1 2.0 %forward.5 = (bf16[192,768]{1,0:T(8,128)(2,1)S(1)}, bf16[192,384]{1,0:T(8,128)(2,1)S(1)}, bf16[192,256]{1,0:T(8,128)(2,1)S(1)}, f32[192,256]{1,0:T(8,128)S(1)}, ...) custom-call(bf16[208,640]{1,0:T(8,128)(2,1)S(1)} %copy-done.2, ...), custom_call_target="tpu_custom_call" | custom-call | flops 3246391296 | bytes 1000000 | tf_op jit(solution)/shard_map/forward/pallas_call | solution.py:386
  18.2 1.6 %collective-permute-start.2 = (bf16[208,640]{1,0:T(8,128)(2,1)S(1)}, bf16[208,640]{1,0:T(8,128)(2,1)S(1)}, u32[]{:S(2)}, u32[]{:S(2)}) collective-permute-start(bf16[208,640]{1,0:T(8,128)(2,1)S(1)} %collective-permute-done.refs_0_.refs_7_), channel_id=1, source_target_pairs={{0,4},{4,0},{8,12},{12,8},{16,20},{20,16},{24,28},{28,24},{1,5},{5... | collective-permute-start | bytes 798728 | tf_op jit(solution)/shard_map/ppermute | solution.py:261
  19.7 2.0 %forward.6 = (bf16[192,768]{1,0:T(8,128)(2,1)S(1)}, bf16[192,384]{1,0:T(8,128)(2,1)S(1)}, bf16[192,256]{1,0:T(8,128)(2,1)S(1)}, f32[192,256]{1,0:T(8,128)S(1)}, ...) custom-call(bf16[208,640]{1,0:T(8,128)(2,1)S(1)} %collective-permute-done.refs_0_.refs_7_, ...), custom_call_target="tpu_custom_call" | custom-call | flops 2164260864 | bytes 1000000 | tf_op jit(solution)/shard_map/forward/pallas_call | solution.py:386
  22.6 1.6 %collective-permute-start.7 = (bf16[208,640]{1,0:T(8,128)(2,1)S(1)}, bf16[208,640]{1,0:T(8,128)(2,1)S(1)}, u32[]{:S(2)}, u32[]{:S(2)}) collective-permute-start(bf16[208,640]{1,0:T(8,128)(2,1)S(1)} %add.12.refs_1_.refs_22_), channel_id=1, source_target_pairs={{0,4},{4,0},{8,12},{12,8},{16,20},{20,16},{24,28},{28,24},{1,5},{5... | collective-permute-start | bytes 798728 | tf_op jit(solution)/shard_map/ppermute | solution.py:261
  24.2 1.5 %collective-permute-start.6 = (bf16[208,640]{1,0:T(8,128)(2,1)S(1)}, bf16[208,640]{1,0:T(8,128)(2,1)S(1)}, u32[]{:S(2)}, u32[]{:S(2)}) collective-permute-start(bf16[208,640]{1,0:T(8,128)(2,1)S(1)} %collective-permute-done.5), channel_id=1, source_target_pairs={{8,0},{12,4},{16,24},{20,28},{9,1},{13,5},{17,25},{21,29},{10,2},{... | collective-permute-start | bytes 798728 | tf_op jit(solution)/shard_map/ppermute | solution.py:337
  25.7 2.0 %forward.7 = (bf16[192,768]{1,0:T(8,128)(2,1)S(1)}, bf16[192,384]{1,0:T(8,128)(2,1)S(1)}, bf16[192,256]{1,0:T(8,128)(2,1)S(1)}, f32[192,256]{1,0:T(8,128)S(1)}, ...) custom-call(bf16[208,640]{1,0:T(8,128)(2,1)S(1)} %collective-permute-done.1.refs_0_.refs_14_, ...), custom_call_target="tpu_custom_call" | custom-call | flops 1623195648 | bytes 1000000 | tf_op jit(solution)/shard_map/forward/pallas_call | solution.py:386
  27.7 3.5 %forward.8 = (bf16[384,768]{1,0:T(8,128)(2,1)S(1)}, bf16[384,384]{1,0:T(8,128)(2,1)S(1)}, bf16[384,256]{1,0:T(8,128)(2,1)S(1)}, f32[384,256]{1,0:T(8,128)S(1)}, ...) custom-call(bf16[208,640]{1,0:T(8,128)(2,1)S(1)} %collective-permute-done.2.refs_0_.refs_21_, ...), custom_call_target="tpu_custom_call" | custom-call | flops 2164260864 | bytes 1000000 | tf_op jit(solution)/shard_map/forward/pallas_call | solution.py:386
  31.3 1.6 %collective-permute-done.6 = bf16[208,640]{1,0:T(8,128)(2,1)S(1)} collective-permute-done((bf16[208,640]{1,0:T(8,128)(2,1)S(1)}, bf16[208,640]{1,0:T(8,128)(2,1)S(1)}, u32[]{:S(2)}, u32[]{:S(2)}) %collective-permute-start.6) | collective-permute-done | bytes 266272 | tf_op jit(solution)/shard_map/ppermute | solution.py:337
  33.0 1.6 %collective-permute-start.8 = (bf16[208,640]{1,0:T(8,128)(2,1)S(1)}, bf16[208,640]{1,0:T(8,128)(2,1)S(1)}, u32[]{:S(2)}, u32[]{:S(2)}) collective-permute-start(bf16[208,640]{1,0:T(8,128)(2,1)S(1)} %add.13.refs_0_.refs_29_), channel_id=1, source_target_pairs={{0,4},{4,0},{8,12},{12,8},{16,20},{20,16},{24,28},{28,24},{1,5},{5... | collective-permute-start | bytes 798728 | tf_op jit(solution)/shard_map/ppermute | solution.py:261
  34.5 3.5 %forward.9 = (bf16[384,768]{1,0:T(8,128)(2,1)S(1)}, bf16[384,384]{1,0:T(8,128)(2,1)S(1)}, bf16[384,256]{1,0:T(8,128)(2,1)S(1)}, f32[384,256]{1,0:T(8,128)S(1)}, ...) custom-call(bf16[208,640]{1,0:T(8,128)(2,1)S(1)} %add.13.refs_0_.refs_29_, ...), custom_call_target="tpu_custom_call" | custom-call | flops 6492782592 | bytes 1000000 | tf_op jit(solution)/shard_map/forward/pallas_call | solution.py:386
  38.0 1.4 %collective-permute-done.8.refs_37_ = bf16[208,640]{1,0:T(8,128)(2,1)S(1)} collective-permute-done((bf16[208,640]{1,0:T(8,128)(2,1)S(1)}, bf16[208,640]{1,0:T(8,128)(2,1)S(1)}, u32[]{:S(2)}, u32[]{:S(2)}) %collective-permute-start.8) | collective-permute-done | bytes 266272 | tf_op jit(solution)/shard_map/ppermute | solution.py:261
  39.5 6.1 %last.1 = (bf16[96,1664]{1,0:T(8,128)(2,1)S(1)}, f32[96,1664]{1,0:T(8,128)S(1)}) custom-call(bf16[208,640]{1,0:T(8,128)(2,1)S(1)} %copy-done.2, bf16[192,768]{1,0:T(8,128)(2,1)S(1)} %get-tuple-element.59.refs_1_, bf16[192,384]{1,0:T(8,128)(2,1)S(1)} %get-tuple-element.60.refs_2_, bf16[192,256]{1,0:T(8,128)(2,1)S(1)} %get-tuple-element.61.refs_3_, ...), custom_call_target="tpu_custom_call" | custom-call | flops 1962934272 | bytes 16000000 | tf_op jit(solution)/shard_map/last/pallas_call | solution.py:403
  45.6 1.6 %collective-permute-done.9 = bf16[96,1664]{1,0:T(8,128)(2,1)S(1)} collective-permute-done((bf16[96,1664]{1,0:T(8,128)(2,1)S(1)}, bf16[96,1664]{1,0:T(8,128)(2,1)S(1)}, u32[]{:S(2)}, u32[]{:S(2)}) %collective-permute-start.9) | collective-permute-done | bytes 319520 | tf_op jit(solution)/shard_map/ppermute | solution.py:261
  47.3 1.6 %collective-permute-start.10 = (bf16[96,1664]{1,0:T(8,128)(2,1)S(1)}, bf16[96,1664]{1,0:T(8,128)(2,1)S(1)}, u32[]{:S(2)}, u32[]{:S(2)}) collective-permute-start(bf16[96,1664]{1,0:T(8,128)(2,1)S(1)} %add_convert_fusion.1.one_ref), channel_id=1, source_target_pairs={{0,2},{1,3},{2,0},{3,1},{4,6},{5,7},{6,4},{7,5},{8,10},{9,11},{10,... | collective-permute-start | bytes 958472 | tf_op jit(solution)/shard_map/ppermute | solution.py:261
  48.9 8.1 %collective-permute-done.10.two_ref = bf16[96,1664]{1,0:T(8,128)(2,1)S(1)} collective-permute-done((bf16[96,1664]{1,0:T(8,128)(2,1)S(1)}, bf16[96,1664]{1,0:T(8,128)(2,1)S(1)}, u32[]{:S(2)}, u32[]{:S(2)}) %collective-permute-start.10) | collective-permute-done | bytes 319520 | tf_op jit(solution)/shard_map/ppermute | solution.py:261
  57.1 1.6 %collective-permute-done.11.far_ref = bf16[96,1664]{1,0:T(8,128)(2,1)S(1)} collective-permute-done((bf16[96,1664]{1,0:T(8,128)(2,1)S(1)}, bf16[96,1664]{1,0:T(8,128)(2,1)S(1)}, u32[]{:S(2)}, u32[]{:S(2)}) %collective-permute-start.11) | collective-permute-done | bytes 319520 | tf_op jit(solution)/shard_map/ppermute | solution.py:261
  58.7 0.9 %finish.1 = (bf16[192,376]{1,0:T(8,128)(2,1)}, bf16[17,192]{1,0:T(8,128)(2,1)}, bf16[192,256]{1,0:T(8,128)(2,1)}, bf16[192,256]{1,0:T(8,128)(2,1)}, bf16[192,376...) custom-call(bf16[96,1664]{1,0:T(8,128)(2,1)S(1)} %add_convert_fusion.1.one_ref, ...), custom_call_target="tpu_custom_call" | custom-call | tf_op jit(solution)/shard_map/finish/pallas_call | solution.py:421
  (21 shorter events, 1.9 us)
Async XLA Ops:
  2.4 13.7 %copy-start = (bf16[1536,256]{1,0:T(8,128)(2,1)S(1)}, bf16[1536,256]{1,0:T(8,128)(2,1)}, u32[]{:S(2)}) copy-start(bf16[1536,256]{1,0:T(8,128)(2,1)} %refs_40_.1) | copy-start | bytes 2359300
  2.4 13.7 %copy-start.1 = (bf16[1536,256]{1,0:T(8,128)(2,1)S(1)}, bf16[1536,256]{1,0:T(8,128)(2,1)}, u32[]{:S(2)}) copy-start(bf16[1536,256]{1,0:T(8,128)(2,1)} %refs_41_.1) | copy-start | bytes 2359300
  2.4 13.7 %copy-start.2 = (bf16[208,640]{1,0:T(8,128)(2,1)S(1)}, bf16[208,640]{1,0:T(8,128)(2,1)}, u32[]{:S(2)}) copy-start(bf16[208,640]{1,0:T(8,128)(2,1)} %pack.1.refs_0_) | copy-start | bytes 798724
  2.4 13.8 %copy-start.3 = (bf16[256,256]{1,0:T(8,128)(2,1)S(1)}, bf16[256,256]{1,0:T(8,128)(2,1)}, u32[]{:S(2)}) copy-start(bf16[256,256]{1,0:T(8,128)(2,1)} %refs_42_.1) | copy-start | bytes 393220
  2.4 10.4 %collective-permute-start.3 = (bf16[208,640]{1,0:T(8,128)(2,1)}, bf16[208,640]{1,0:T(8,128)(2,1)S(1)}, u32[]{:S(2)}, u32[]{:S(2)}) collective-permute-start(bf16[208,640]{1,0:T(8,128)(2,1)} %pack.1.refs_0_), channel_id=1, source_target_pairs={{8,16},{12,20},{16,8},{20,12},{9,17},{13,21},{17,9},{21,13},{10,18... | collective-permute-start | bytes 798728 | tf_op jit(solution)/shard_map/ppermute | solution.py:329
  3.2 12.2 %collective-permute-start = (bf16[208,640]{1,0:T(8,128)(2,1)}, bf16[208,640]{1,0:T(8,128)(2,1)S(1)}, u32[]{:S(2)}, u32[]{:S(2)}) collective-permute-start(bf16[208,640]{1,0:T(8,128)(2,1)} %pack.1.refs_0_), channel_id=1, source_target_pairs={{0,8},{4,12},{8,0},{12,4},{16,24},{20,28},{24,16},{28,20},{1,9},{5... | collective-permute-start | bytes 798728 | tf_op jit(solution)/shard_map/ppermute | solution.py:261
  9.1 16.6 %collective-permute-start.1 = (bf16[208,640]{1,0:T(8,128)(2,1)}, bf16[208,640]{1,0:T(8,128)(2,1)S(1)}, u32[]{:S(2)}, u32[]{:S(2)}) collective-permute-start(bf16[208,640]{1,0:T(8,128)(2,1)} %pack.1.refs_0_), channel_id=1, source_target_pairs={{0,4},{4,0},{8,12},{12,8},{16,20},{20,16},{24,28},{28,24},{1,5},{5... | collective-permute-start | bytes 798728 | tf_op jit(solution)/shard_map/ppermute | solution.py:261
  12.8 9.8 %collective-permute-start.4 = (bf16[208,640]{1,0:T(8,128)(2,1)S(1)}, bf16[208,640]{1,0:T(8,128)(2,1)S(1)}, u32[]{:S(2)}, u32[]{:S(2)}) collective-permute-start(bf16[208,640]{1,0:T(8,128)(2,1)S(1)} %collective-permute-done.3), channel_id=1, source_target_pairs={{8,0},{12,4},{16,24},{20,28},{9,1},{13,5},{17,25},{21,29},{10,2},{... | collective-permute-start | bytes 798728 | tf_op jit(solution)/shard_map/ppermute | solution.py:332
  15.4 8.8 %collective-permute-start.5 = (bf16[208,640]{1,0:T(8,128)(2,1)S(1)}, bf16[208,640]{1,0:T(8,128)(2,1)S(1)}, u32[]{:S(2)}, u32[]{:S(2)}) collective-permute-start(bf16[208,640]{1,0:T(8,128)(2,1)S(1)} %collective-permute-done.refs_0_.refs_7_), channel_id=1, source_target_pairs={{8,16},{12,20},{16,8},{20,12},{9,17},{13,21},{17,9},{21,13},{10,18... | collective-permute-start | bytes 798728 | tf_op jit(solution)/shard_map/ppermute | solution.py:334
  18.2 9.5 %collective-permute-start.2 = (bf16[208,640]{1,0:T(8,128)(2,1)S(1)}, bf16[208,640]{1,0:T(8,128)(2,1)S(1)}, u32[]{:S(2)}, u32[]{:S(2)}) collective-permute-start(bf16[208,640]{1,0:T(8,128)(2,1)S(1)} %collective-permute-done.refs_0_.refs_7_), channel_id=1, source_target_pairs={{0,4},{4,0},{8,12},{12,8},{16,20},{20,16},{24,28},{28,24},{1,5},{5... | collective-permute-start | bytes 798728 | tf_op jit(solution)/shard_map/ppermute | solution.py:261
  22.6 11.9 %collective-permute-start.7 = (bf16[208,640]{1,0:T(8,128)(2,1)S(1)}, bf16[208,640]{1,0:T(8,128)(2,1)S(1)}, u32[]{:S(2)}, u32[]{:S(2)}) collective-permute-start(bf16[208,640]{1,0:T(8,128)(2,1)S(1)} %add.12.refs_1_.refs_22_), channel_id=1, source_target_pairs={{0,4},{4,0},{8,12},{12,8},{16,20},{20,16},{24,28},{28,24},{1,5},{5... | collective-permute-start | bytes 798728 | tf_op jit(solution)/shard_map/ppermute | solution.py:261
  24.2 8.7 %collective-permute-start.6 = (bf16[208,640]{1,0:T(8,128)(2,1)S(1)}, bf16[208,640]{1,0:T(8,128)(2,1)S(1)}, u32[]{:S(2)}, u32[]{:S(2)}) collective-permute-start(bf16[208,640]{1,0:T(8,128)(2,1)S(1)} %collective-permute-done.5), channel_id=1, source_target_pairs={{8,0},{12,4},{16,24},{20,28},{9,1},{13,5},{17,25},{21,29},{10,2},{... | collective-permute-start | bytes 798728 | tf_op jit(solution)/shard_map/ppermute | solution.py:337
  33.0 6.5 %collective-permute-start.8 = (bf16[208,640]{1,0:T(8,128)(2,1)S(1)}, bf16[208,640]{1,0:T(8,128)(2,1)S(1)}, u32[]{:S(2)}, u32[]{:S(2)}) collective-permute-start(bf16[208,640]{1,0:T(8,128)(2,1)S(1)} %add.13.refs_0_.refs_29_), channel_id=1, source_target_pairs={{0,4},{4,0},{8,12},{12,8},{16,20},{20,16},{24,28},{28,24},{1,5},{5... | collective-permute-start | bytes 798728 | tf_op jit(solution)/shard_map/ppermute | solution.py:261
  45.6 1.7 %collective-permute-start.9 = (bf16[96,1664]{1,0:T(8,128)(2,1)S(1)}, bf16[96,1664]{1,0:T(8,128)(2,1)S(1)}, u32[]{:S(2)}, u32[]{:S(2)}) collective-permute-start(bf16[96,1664]{1,0:T(8,128)(2,1)S(1)} %get-tuple-element.95), channel_id=1, source_target_pairs={{0,1},{1,0},{2,3},{3,2},{4,5},{5,4},{6,7},{7,6},{8,9},{9,8},{10,11... | collective-permute-start | bytes 958472 | tf_op jit(solution)/shard_map/ppermute | solution.py:261
  47.3 9.6 %collective-permute-start.10 = (bf16[96,1664]{1,0:T(8,128)(2,1)S(1)}, bf16[96,1664]{1,0:T(8,128)(2,1)S(1)}, u32[]{:S(2)}, u32[]{:S(2)}) collective-permute-start(bf16[96,1664]{1,0:T(8,128)(2,1)S(1)} %add_convert_fusion.1.one_ref), channel_id=1, source_target_pairs={{0,2},{1,3},{2,0},{3,1},{4,6},{5,7},{6,4},{7,5},{8,10},{9,11},{10,... | collective-permute-start | bytes 958472 | tf_op jit(solution)/shard_map/ppermute | solution.py:261
  57.0 1.7 %collective-permute-start.11 = (bf16[96,1664]{1,0:T(8,128)(2,1)S(1)}, bf16[96,1664]{1,0:T(8,128)(2,1)S(1)}, u32[]{:S(2)}, u32[]{:S(2)}) collective-permute-start(bf16[96,1664]{1,0:T(8,128)(2,1)S(1)} %add_convert_fusion), channel_id=1, source_target_pairs={{0,1},{1,0},{2,3},{3,2},{4,5},{5,4},{6,7},{7,6},{8,9},{9,8},{10,11... | collective-permute-start | bytes 958472 | tf_op jit(solution)/shard_map/ppermute | solution.py:261

commit v7 on v6

--- a/solution.py
+++ b/solution.py
@@ -102,7 +102,6 @@
     rows, act, rank, side = cfg["rows"], cfg["act"], cfg["rank"], cfg["side"]
     obs_pad, x_pad, hidden, zcount = cfg["obs_pad"], cfg["x_pad"], cfg["hidden"], cfg["zcount"]
     tile, lane = cfg["tile"], cfg["lane"]
-    m = rows * len(xs)
     half = side // 2
     row_spots = lax.broadcasted_iota(jnp.int32, (rows, rows), 1).astype(F32)
     spots = lax.broadcasted_iota(jnp.int32, (rows, zcount), 1).astype(F32)
@@ -121,14 +120,11 @@
         later_ref[here, :] = dot_nn(hot, near).astype(BF16)
     whole = a_ref[...]
     later = later_ref[...]
-    f_acc = jnp.zeros((m, rank), F32)
-    u = jnp.zeros((m, rank), F32)
-    for n in range(0, hidden, tile):
-        h = jnp.maximum(dot_nn(whole, wf_ref[:, n : n + tile]), 0.0).astype(BF16)
-        f_acc = f_acc + dot_nn(h, fo_ref[n : n + tile, :])
-        g = jnp.maximum(dot_nn(later, wb_ref[:, n : n + tile]), 0.0).astype(BF16)
-        u = u + dot_nn(g, bo_ref[n : n + tile, :])
-    emb = f_acc.astype(BF16)
+    tiles = [slice(n, n + tile) for n in range(0, hidden, tile)]
+    hs = [jnp.maximum(dot_nn(whole, wf_ref[:, part]), 0.0).astype(BF16) for part in tiles]
+    emb = dot_nn(join(hs, 1), fo_ref[...]).astype(BF16)
+    gs = [jnp.maximum(dot_nn(later, wb_ref[:, part]), 0.0).astype(BF16) for part in tiles]
+    u = dot_nn(join(gs, 1), bo_ref[...])
     back = (u * lax.rsqrt(jnp.mean(u * u, axis=-1, keepdims=True) + EPSILON)).astype(BF16)
     f_ref[...] = emb
     u_ref[...] = u
@@ -310,7 +306,7 @@
         replicas=replicas,
         total=group * replicas,
         block=block,
-        tile=512,
+        tile=256,
         cols=(c1, c2, c3),
         loss_spot=obs_pad + side,
     )

time: 60 us -> 59.6 us (level)
  Pallas kernels: 24.1 us -> 23.2 us
    pallas_call x5, Pallas kernels: 13.1 us -> 12.4 us  [fast_local(): pl.pallas_call(functools.partial(forward_kernel, cfg, count, not early),...]
  transfers between devices with their start and end apart: 12 -> 12, of which waited for: 7 -> 7; matrix products, arithmetic and copies ran while one was open for 0% -> 0% of each run, Pallas kernels for 26% -> 25%
where the time goes in v7:
time: 59.6 us; the launch traced here: 59.4 us
  Pallas kernels  23.2 us (39%)
  starting transfers between devices  18 us (30%)
  waiting for transfers between devices  16.9 us (28%)
  between operations  0.97 us (2%)
    ppermute x8, waiting for transfers between devices, exchange(): return lax.ppermute(array, axis, [(i, i ^ bit) for i in range(size)])  14.2 us
    ppermute x8, starting transfers between devices, exchange(): return lax.ppermute(array, axis, [(i, i ^ bit) for i in range(size)])  13.8 us
    pallas_call x5, Pallas kernels, fast_local(): pl.pallas_call(functools.partial(forward_kernel, cfg, count, not early),...  12.4 us
    pallas_call x1, Pallas kernels, fast_local(): pl.pallas_call(functools.partial(last_kernel, cfg, [len(xs) for xs, _ in...  5.97 us
    pallas_call x1, Pallas kernels, fast_local(): pl.pallas_call(functools.partial(weights_kernel, cfg), out_shape=(shape((...  2.17 us
    pallas_call x1, Pallas kernels, fast_local(): pl.pallas_call(functools.partial(pack_kernel, cfg), out_shape=shape((rows...  1.74 us
    ppermute x1, waiting for transfers between devices, fast_local(): handed_two = lax.ppermute(across_two, 'dp', outward)  1.67 us
    ppermute x1, starting transfers between devices, fast_local(): handed_two = lax.ppermute(across_two, 'dp', outward)  1.46 us
  transfers between devices with their start and end apart: 12, of which 7 were waited for; matrix products, arithmetic and copies ran while one was open for 0% of the time, Pallas kernels for 25%

profile of v7, /device:TPU:0, one launch (start us, length us, event | category | flops | bytes accessed | tf_op | source)
XLA Modules:
  0.0 59.4 jit_solution(13476252738260969101)
XLA Ops:
  0.6 1.7 %pack.1.refs_0_ = bf16[208,640]{1,0:T(8,128)(2,1)} custom-call(bf16[1,192,376]{2,1,0:T(8,128)(2,1)} %state_ref.1, bf16[17,192]{1,0:T(8,128)(2,1)} %bitcast.7, s32[1,192]{1,0:T(1,128)} %next_ref.1, s32[1,192]{1,0:T(1,128)} %latent_ref.1, bf16[1,192,256]{2,1,0:T(8,128)(2,1)} %target_ref.1), custom_call_target="tpu_custom_call" | custom-call | tf_op jit(solution)/shard_map/pack/pallas_call | solution.py:315
  3.2 5.9 %collective-permute-start = (bf16[208,640]{1,0:T(8,128)(2,1)}, bf16[208,640]{1,0:T(8,128)(2,1)S(1)}, u32[]{:S(2)}, u32[]{:S(2)}) collective-permute-start(bf16[208,640]{1,0:T(8,128)(2,1)} %pack.1.refs_0_), channel_id=1, source_target_pairs={{0,8},{4,12},{8,0},{12,4},{16,24},{20,28},{24,16},{28,20},{1,9},{5... | collective-permute-start | bytes 798728 | tf_op jit(solution)/shard_map/ppermute | solution.py:257
  9.1 1.5 %collective-permute-start.1 = (bf16[208,640]{1,0:T(8,128)(2,1)}, bf16[208,640]{1,0:T(8,128)(2,1)S(1)}, u32[]{:S(2)}, u32[]{:S(2)}) collective-permute-start(bf16[208,640]{1,0:T(8,128)(2,1)} %pack.1.refs_0_), channel_id=1, source_target_pairs={{0,4},{4,0},{8,12},{12,8},{16,20},{20,16},{24,28},{28,24},{1,5},{5... | collective-permute-start | bytes 798728 | tf_op jit(solution)/shard_map/ppermute | solution.py:257
  10.6 2.2 %weights.1 = (bf16[768,1536]{1,0:T(8,128)(2,1)S(1)}, bf16[384,1536]{1,0:T(8,128)(2,1)S(1)}, bf16[192,768]{1,0:T(8,128)(2,1)S(1)}, bf16[192,384]{1,0:T(8,128)(2,1)S(1)}) custom-call(bf16[376,1536]{1,0:T(8,128)(2,1)} %fs_hbm.1, bf16[17,1536]{1,0:T(8,128)(2,1)} %fa_hbm.1, bf16[256,1536]{1,0:T(8,128)(2,1)} %fl_hbm.1, bf16[376,1536]{1,0:T(8,128)(2,1)} %bs_hbm.1), custom_call_target="tpu_custom_call" | custom-call | bytes 1000000 | tf_op jit(solution)/shard_map/weights/pallas_call | solution.py:336
  12.8 1.3 %collective-permute-start.4 = (bf16[208,640]{1,0:T(8,128)(2,1)S(1)}, bf16[208,640]{1,0:T(8,128)(2,1)S(1)}, u32[]{:S(2)}, u32[]{:S(2)}) collective-permute-start(bf16[208,640]{1,0:T(8,128)(2,1)S(1)} %collective-permute-done.3), channel_id=1, source_target_pairs={{8,0},{12,4},{16,24},{20,28},{9,1},{13,5},{17,25},{21,29},{10,2},{... | collective-permute-start | bytes 798728 | tf_op jit(solution)/shard_map/ppermute | solution.py:328
  14.1 1.3 %collective-permute-done.refs_0_.refs_7_ = bf16[208,640]{1,0:T(8,128)(2,1)S(1)} collective-permute-done((bf16[208,640]{1,0:T(8,128)(2,1)}, bf16[208,640]{1,0:T(8,128)(2,1)S(1)}, u32[]{:S(2)}, u32[]{:S(2)}) %collective-permute-start) | collective-permute-done | bytes 266272 | tf_op jit(solution)/shard_map/ppermute | solution.py:257
  16.1 1.9 %forward.5 = (bf16[192,768]{1,0:T(8,128)(2,1)S(1)}, bf16[192,384]{1,0:T(8,128)(2,1)S(1)}, bf16[192,256]{1,0:T(8,128)(2,1)S(1)}, f32[192,256]{1,0:T(8,128)S(1)}, ...) custom-call(bf16[208,640]{1,0:T(8,128)(2,1)S(1)} %copy-done.2, ...), custom_call_target="tpu_custom_call" | custom-call | flops 3246391296 | bytes 1000000 | tf_op jit(solution)/shard_map/forward/pallas_call | solution.py:382
  18.0 1.6 %collective-permute-start.2 = (bf16[208,640]{1,0:T(8,128)(2,1)S(1)}, bf16[208,640]{1,0:T(8,128)(2,1)S(1)}, u32[]{:S(2)}, u32[]{:S(2)}) collective-permute-start(bf16[208,640]{1,0:T(8,128)(2,1)S(1)} %collective-permute-done.refs_0_.refs_7_), channel_id=1, source_target_pairs={{0,4},{4,0},{8,12},{12,8},{16,20},{20,16},{24,28},{28,24},{1,5},{5... | collective-permute-start | bytes 798728 | tf_op jit(solution)/shard_map/ppermute | solution.py:257
  19.6 1.9 %forward.6 = (bf16[192,768]{1,0:T(8,128)(2,1)S(1)}, bf16[192,384]{1,0:T(8,128)(2,1)S(1)}, bf16[192,256]{1,0:T(8,128)(2,1)S(1)}, f32[192,256]{1,0:T(8,128)S(1)}, ...) custom-call(bf16[208,640]{1,0:T(8,128)(2,1)S(1)} %collective-permute-done.refs_0_.refs_7_, ...), custom_call_target="tpu_custom_call" | custom-call | flops 2164260864 | bytes 1000000 | tf_op jit(solution)/shard_map/forward/pallas_call | solution.py:382
  21.5 1.1 %collective-permute-done.4 = bf16[208,640]{1,0:T(8,128)(2,1)S(1)} collective-permute-done((bf16[208,640]{1,0:T(8,128)(2,1)S(1)}, bf16[208,640]{1,0:T(8,128)(2,1)S(1)}, u32[]{:S(2)}, u32[]{:S(2)}) %collective-permute-start.4) | collective-permute-done | bytes 266272 | tf_op jit(solution)/shard_map/ppermute | solution.py:328
  22.6 1.6 %collective-permute-start.7 = (bf16[208,640]{1,0:T(8,128)(2,1)S(1)}, bf16[208,640]{1,0:T(8,128)(2,1)S(1)}, u32[]{:S(2)}, u32[]{:S(2)}) collective-permute-start(bf16[208,640]{1,0:T(8,128)(2,1)S(1)} %add.12.refs_1_.refs_22_), channel_id=1, source_target_pairs={{0,4},{4,0},{8,12},{12,8},{16,20},{20,16},{24,28},{28,24},{1,5},{5... | collective-permute-start | bytes 798728 | tf_op jit(solution)/shard_map/ppermute | solution.py:257
  24.2 1.5 %collective-permute-start.6 = (bf16[208,640]{1,0:T(8,128)(2,1)S(1)}, bf16[208,640]{1,0:T(8,128)(2,1)S(1)}, u32[]{:S(2)}, u32[]{:S(2)}) collective-permute-start(bf16[208,640]{1,0:T(8,128)(2,1)S(1)} %collective-permute-done.5), channel_id=1, source_target_pairs={{8,0},{12,4},{16,24},{20,28},{9,1},{13,5},{17,25},{21,29},{10,2},{... | collective-permute-start | bytes 798728 | tf_op jit(solution)/shard_map/ppermute | solution.py:333
  25.7 1.9 %forward.7 = (bf16[192,768]{1,0:T(8,128)(2,1)S(1)}, bf16[192,384]{1,0:T(8,128)(2,1)S(1)}, bf16[192,256]{1,0:T(8,128)(2,1)S(1)}, f32[192,256]{1,0:T(8,128)S(1)}, ...) custom-call(bf16[208,640]{1,0:T(8,128)(2,1)S(1)} %collective-permute-done.1.refs_0_.refs_14_, ...), custom_call_target="tpu_custom_call" | custom-call | flops 1623195648 | bytes 1000000 | tf_op jit(solution)/shard_map/forward/pallas_call | solution.py:382
  27.6 3.3 %forward.8 = (bf16[384,768]{1,0:T(8,128)(2,1)S(1)}, bf16[384,384]{1,0:T(8,128)(2,1)S(1)}, bf16[384,256]{1,0:T(8,128)(2,1)S(1)}, f32[384,256]{1,0:T(8,128)S(1)}, ...) custom-call(bf16[208,640]{1,0:T(8,128)(2,1)S(1)} %collective-permute-done.2.refs_0_.refs_21_, ...), custom_call_target="tpu_custom_call" | custom-call | flops 2164260864 | bytes 1000000 | tf_op jit(solution)/shard_map/forward/pallas_call | solution.py:382
  31.0 1.7 %collective-permute-done.6 = bf16[208,640]{1,0:T(8,128)(2,1)S(1)} collective-permute-done((bf16[208,640]{1,0:T(8,128)(2,1)S(1)}, bf16[208,640]{1,0:T(8,128)(2,1)S(1)}, u32[]{:S(2)}, u32[]{:S(2)}) %collective-permute-start.6) | collective-permute-done | bytes 266272 | tf_op jit(solution)/shard_map/ppermute | solution.py:333
  32.7 1.6 %collective-permute-start.8 = (bf16[208,640]{1,0:T(8,128)(2,1)S(1)}, bf16[208,640]{1,0:T(8,128)(2,1)S(1)}, u32[]{:S(2)}, u32[]{:S(2)}) collective-permute-start(bf16[208,640]{1,0:T(8,128)(2,1)S(1)} %add.13.refs_0_.refs_29_), channel_id=1, source_target_pairs={{0,4},{4,0},{8,12},{12,8},{16,20},{20,16},{24,28},{28,24},{1,5},{5... | collective-permute-start | bytes 798728 | tf_op jit(solution)/shard_map/ppermute | solution.py:257
  34.3 3.3 %forward.9 = (bf16[384,768]{1,0:T(8,128)(2,1)S(1)}, bf16[384,384]{1,0:T(8,128)(2,1)S(1)}, bf16[384,256]{1,0:T(8,128)(2,1)S(1)}, f32[384,256]{1,0:T(8,128)S(1)}, ...) custom-call(bf16[208,640]{1,0:T(8,128)(2,1)S(1)} %add.13.refs_0_.refs_29_, ...), custom_call_target="tpu_custom_call" | custom-call | flops 6492782592 | bytes 1000000 | tf_op jit(solution)/shard_map/forward/pallas_call | solution.py:382
  37.6 1.6 %collective-permute-done.8.refs_37_ = bf16[208,640]{1,0:T(8,128)(2,1)S(1)} collective-permute-done((bf16[208,640]{1,0:T(8,128)(2,1)S(1)}, bf16[208,640]{1,0:T(8,128)(2,1)S(1)}, u32[]{:S(2)}, u32[]{:S(2)}) %collective-permute-start.8) | collective-permute-done | bytes 266272 | tf_op jit(solution)/shard_map/ppermute | solution.py:257
  39.2 6.0 %last.1 = (bf16[96,1664]{1,0:T(8,128)(2,1)S(1)}, f32[96,1664]{1,0:T(8,128)S(1)}) custom-call(bf16[208,640]{1,0:T(8,128)(2,1)S(1)} %copy-done.2, bf16[192,768]{1,0:T(8,128)(2,1)S(1)} %get-tuple-element.59.refs_1_, bf16[192,384]{1,0:T(8,128)(2,1)S(1)} %get-tuple-element.60.refs_2_, bf16[192,256]{1,0:T(8,128)(2,1)S(1)} %get-tuple-element.61.refs_3_, ...), custom_call_target="tpu_custom_call" | custom-call | flops 1962934272 | bytes 16000000 | tf_op jit(solution)/shard_map/last/pallas_call | solution.py:399
  45.2 1.6 %collective-permute-done.9 = bf16[96,1664]{1,0:T(8,128)(2,1)S(1)} collective-permute-done((bf16[96,1664]{1,0:T(8,128)(2,1)S(1)}, bf16[96,1664]{1,0:T(8,128)(2,1)S(1)}, u32[]{:S(2)}, u32[]{:S(2)}) %collective-permute-start.9) | collective-permute-done | bytes 319520 | tf_op jit(solution)/shard_map/ppermute | solution.py:257
  46.9 1.6 %collective-permute-start.10 = (bf16[96,1664]{1,0:T(8,128)(2,1)S(1)}, bf16[96,1664]{1,0:T(8,128)(2,1)S(1)}, u32[]{:S(2)}, u32[]{:S(2)}) collective-permute-start(bf16[96,1664]{1,0:T(8,128)(2,1)S(1)} %add_convert_fusion.1.one_ref), channel_id=1, source_target_pairs={{0,2},{1,3},{2,0},{3,1},{4,6},{5,7},{6,4},{7,5},{8,10},{9,11},{10,... | collective-permute-start | bytes 958472 | tf_op jit(solution)/shard_map/ppermute | solution.py:257
  48.5 8.1 %collective-permute-done.10.two_ref = bf16[96,1664]{1,0:T(8,128)(2,1)S(1)} collective-permute-done((bf16[96,1664]{1,0:T(8,128)(2,1)S(1)}, bf16[96,1664]{1,0:T(8,128)(2,1)S(1)}, u32[]{:S(2)}, u32[]{:S(2)}) %collective-permute-start.10) | collective-permute-done | bytes 319520 | tf_op jit(solution)/shard_map/ppermute | solution.py:257
  56.7 1.6 %collective-permute-done.11.far_ref = bf16[96,1664]{1,0:T(8,128)(2,1)S(1)} collective-permute-done((bf16[96,1664]{1,0:T(8,128)(2,1)S(1)}, bf16[96,1664]{1,0:T(8,128)(2,1)S(1)}, u32[]{:S(2)}, u32[]{:S(2)}) %collective-permute-start.11) | collective-permute-done | bytes 319520 | tf_op jit(solution)/shard_map/ppermute | solution.py:257
  58.3 0.9 %finish.1 = (bf16[192,376]{1,0:T(8,128)(2,1)}, bf16[17,192]{1,0:T(8,128)(2,1)}, bf16[192,256]{1,0:T(8,128)(2,1)}, bf16[192,256]{1,0:T(8,128)(2,1)}, bf16[192,376...) custom-call(bf16[96,1664]{1,0:T(8,128)(2,1)S(1)} %add_convert_fusion.1.one_ref, ...), custom_call_target="tpu_custom_call" | custom-call | tf_op jit(solution)/shard_map/finish/pallas_call | solution.py:417
  (21 shorter events, 1.9 us)
Async XLA Ops:
  2.4 13.7 %copy-start = (bf16[1536,256]{1,0:T(8,128)(2,1)S(1)}, bf16[1536,256]{1,0:T(8,128)(2,1)}, u32[]{:S(2)}) copy-start(bf16[1536,256]{1,0:T(8,128)(2,1)} %refs_40_.1) | copy-start | bytes 2359300
  2.4 13.7 %copy-start.1 = (bf16[1536,256]{1,0:T(8,128)(2,1)S(1)}, bf16[1536,256]{1,0:T(8,128)(2,1)}, u32[]{:S(2)}) copy-start(bf16[1536,256]{1,0:T(8,128)(2,1)} %refs_41_.1) | copy-start | bytes 2359300
  2.4 13.7 %copy-start.2 = (bf16[208,640]{1,0:T(8,128)(2,1)S(1)}, bf16[208,640]{1,0:T(8,128)(2,1)}, u32[]{:S(2)}) copy-start(bf16[208,640]{1,0:T(8,128)(2,1)} %pack.1.refs_0_) | copy-start | bytes 798724
  2.4 13.8 %copy-start.3 = (bf16[256,256]{1,0:T(8,128)(2,1)S(1)}, bf16[256,256]{1,0:T(8,128)(2,1)}, u32[]{:S(2)}) copy-start(bf16[256,256]{1,0:T(8,128)(2,1)} %refs_42_.1) | copy-start | bytes 393220
  2.4 10.4 %collective-permute-start.3 = (bf16[208,640]{1,0:T(8,128)(2,1)}, bf16[208,640]{1,0:T(8,128)(2,1)S(1)}, u32[]{:S(2)}, u32[]{:S(2)}) collective-permute-start(bf16[208,640]{1,0:T(8,128)(2,1)} %pack.1.refs_0_), channel_id=1, source_target_pairs={{8,16},{12,20},{16,8},{20,12},{9,17},{13,21},{17,9},{21,13},{10,18... | collective-permute-start | bytes 798728 | tf_op jit(solution)/shard_map/ppermute | solution.py:325
  3.2 12.2 %collective-permute-start = (bf16[208,640]{1,0:T(8,128)(2,1)}, bf16[208,640]{1,0:T(8,128)(2,1)S(1)}, u32[]{:S(2)}, u32[]{:S(2)}) collective-permute-start(bf16[208,640]{1,0:T(8,128)(2,1)} %pack.1.refs_0_), channel_id=1, source_target_pairs={{0,8},{4,12},{8,0},{12,4},{16,24},{20,28},{24,16},{28,20},{1,9},{5... | collective-permute-start | bytes 798728 | tf_op jit(solution)/shard_map/ppermute | solution.py:257
  9.1 16.6 %collective-permute-start.1 = (bf16[208,640]{1,0:T(8,128)(2,1)}, bf16[208,640]{1,0:T(8,128)(2,1)S(1)}, u32[]{:S(2)}, u32[]{:S(2)}) collective-permute-start(bf16[208,640]{1,0:T(8,128)(2,1)} %pack.1.refs_0_), channel_id=1, source_target_pairs={{0,4},{4,0},{8,12},{12,8},{16,20},{20,16},{24,28},{28,24},{1,5},{5... | collective-permute-start | bytes 798728 | tf_op jit(solution)/shard_map/ppermute | solution.py:257
  12.8 9.8 %collective-permute-start.4 = (bf16[208,640]{1,0:T(8,128)(2,1)S(1)}, bf16[208,640]{1,0:T(8,128)(2,1)S(1)}, u32[]{:S(2)}, u32[]{:S(2)}) collective-permute-start(bf16[208,640]{1,0:T(8,128)(2,1)S(1)} %collective-permute-done.3), channel_id=1, source_target_pairs={{8,0},{12,4},{16,24},{20,28},{9,1},{13,5},{17,25},{21,29},{10,2},{... | collective-permute-start | bytes 798728 | tf_op jit(solution)/shard_map/ppermute | solution.py:328
  15.4 8.8 %collective-permute-start.5 = (bf16[208,640]{1,0:T(8,128)(2,1)S(1)}, bf16[208,640]{1,0:T(8,128)(2,1)S(1)}, u32[]{:S(2)}, u32[]{:S(2)}) collective-permute-start(bf16[208,640]{1,0:T(8,128)(2,1)S(1)} %collective-permute-done.refs_0_.refs_7_), channel_id=1, source_target_pairs={{8,16},{12,20},{16,8},{20,12},{9,17},{13,21},{17,9},{21,13},{10,18... | collective-permute-start | bytes 798728 | tf_op jit(solution)/shard_map/ppermute | solution.py:330
  18.0 9.6 %collective-permute-start.2 = (bf16[208,640]{1,0:T(8,128)(2,1)S(1)}, bf16[208,640]{1,0:T(8,128)(2,1)S(1)}, u32[]{:S(2)}, u32[]{:S(2)}) collective-permute-start(bf16[208,640]{1,0:T(8,128)(2,1)S(1)} %collective-permute-done.refs_0_.refs_7_), channel_id=1, source_target_pairs={{0,4},{4,0},{8,12},{12,8},{16,20},{20,16},{24,28},{28,24},{1,5},{5... | collective-permute-start | bytes 798728 | tf_op jit(solution)/shard_map/ppermute | solution.py:257
  22.6 11.6 %collective-permute-start.7 = (bf16[208,640]{1,0:T(8,128)(2,1)S(1)}, bf16[208,640]{1,0:T(8,128)(2,1)S(1)}, u32[]{:S(2)}, u32[]{:S(2)}) collective-permute-start(bf16[208,640]{1,0:T(8,128)(2,1)S(1)} %add.12.refs_1_.refs_22_), channel_id=1, source_target_pairs={{0,4},{4,0},{8,12},{12,8},{16,20},{20,16},{24,28},{28,24},{1,5},{5... | collective-permute-start | bytes 798728 | tf_op jit(solution)/shard_map/ppermute | solution.py:257
  24.2 8.4 %collective-permute-start.6 = (bf16[208,640]{1,0:T(8,128)(2,1)S(1)}, bf16[208,640]{1,0:T(8,128)(2,1)S(1)}, u32[]{:S(2)}, u32[]{:S(2)}) collective-permute-start(bf16[208,640]{1,0:T(8,128)(2,1)S(1)} %collective-permute-done.5), channel_id=1, source_target_pairs={{8,0},{12,4},{16,24},{20,28},{9,1},{13,5},{17,25},{21,29},{10,2},{... | collective-permute-start | bytes 798728 | tf_op jit(solution)/shard_map/ppermute | solution.py:333
  32.7 6.5 %collective-permute-start.8 = (bf16[208,640]{1,0:T(8,128)(2,1)S(1)}, bf16[208,640]{1,0:T(8,128)(2,1)S(1)}, u32[]{:S(2)}, u32[]{:S(2)}) collective-permute-start(bf16[208,640]{1,0:T(8,128)(2,1)S(1)} %add.13.refs_0_.refs_29_), channel_id=1, source_target_pairs={{0,4},{4,0},{8,12},{12,8},{16,20},{20,16},{24,28},{28,24},{1,5},{5... | collective-permute-start | bytes 798728 | tf_op jit(solution)/shard_map/ppermute | solution.py:257
  45.2 1.7 %collective-permute-start.9 = (bf16[96,1664]{1,0:T(8,128)(2,1)S(1)}, bf16[96,1664]{1,0:T(8,128)(2,1)S(1)}, u32[]{:S(2)}, u32[]{:S(2)}) collective-permute-start(bf16[96,1664]{1,0:T(8,128)(2,1)S(1)} %get-tuple-element.95), channel_id=1, source_target_pairs={{0,1},{1,0},{2,3},{3,2},{4,5},{5,4},{6,7},{7,6},{8,9},{9,8},{10,11... | collective-permute-start | bytes 958472 | tf_op jit(solution)/shard_map/ppermute | solution.py:257
  46.9 9.6 %collective-permute-start.10 = (bf16[96,1664]{1,0:T(8,128)(2,1)S(1)}, bf16[96,1664]{1,0:T(8,128)(2,1)S(1)}, u32[]{:S(2)}, u32[]{:S(2)}) collective-permute-start(bf16[96,1664]{1,0:T(8,128)(2,1)S(1)} %add_convert_fusion.1.one_ref), channel_id=1, source_target_pairs={{0,2},{1,3},{2,0},{3,1},{4,6},{5,7},{6,4},{7,5},{8,10},{9,11},{10,... | collective-permute-start | bytes 958472 | tf_op jit(solution)/shard_map/ppermute | solution.py:257
  56.6 1.7 %collective-permute-start.11 = (bf16[96,1664]{1,0:T(8,128)(2,1)S(1)}, bf16[96,1664]{1,0:T(8,128)(2,1)S(1)}, u32[]{:S(2)}, u32[]{:S(2)}) collective-permute-start(bf16[96,1664]{1,0:T(8,128)(2,1)S(1)} %add_convert_fusion), channel_id=1, source_target_pairs={{0,1},{1,0},{2,3},{3,2},{4,5},{5,4},{6,7},{7,6},{8,9},{9,8},{10,11... | collective-permute-start | bytes 958472 | tf_op jit(solution)/shard_map/ppermute | solution.py:257

commit v8 on v7

--- a/solution.py
+++ b/solution.py
@@ -15,7 +15,6 @@
 F32 = jnp.float32
 LANES = 128
 ROW_TILE = 16
-VMEM_LIMIT = 56 * 1024 * 1024
 KERNEL_GROUP_LIMIT = 2048
 
 
@@ -257,6 +256,10 @@
     return lax.ppermute(array, axis, [(i, i ^ bit) for i in range(size)])
 
 
+def in_hbm(*arrays):
+    return [pltpu.with_memory_space_constraint(array, pltpu.HBM) for array in arrays]
+
+
 def shape(dims, kind):
     return jax.ShapeDtypeStruct(dims, kind)
 
@@ -316,9 +319,9 @@
         functools.partial(pack_kernel, cfg),
         out_shape=shape((rows + side // 2, obs_pad + rank), BF16),
         scratch_shapes=[pltpu.VMEM((side, lane), F32)],
-        compiler_params=pltpu.CompilerParams(vmem_limit_bytes=VMEM_LIMIT),
+        compiler_params=pltpu.CompilerParams(vmem_limit_bytes=8 * 1024 * 1024),
         name="pack",
-    )(states, actions[0].T, next_index, latent_ids, target_forward)
+    )(*in_hbm(states, actions[0].T, next_index, latent_ids, target_forward))
     x = {"own": own}
     middle = [(2 + i, 4 + i) for i in range(2)] + [(4 + i, 2 + i) for i in range(2)]
     outward = [(2 + i, i) for i in range(2)] + [(4 + i, 6 + i) for i in range(2)]
@@ -352,7 +355,7 @@
         compiler_params=pltpu.CompilerParams(vmem_limit_bytes=16 * 1024 * 1024),
         cost_estimate=pl.CostEstimate(flops=0, bytes_accessed=1_000_000, transcendentals=0),
         name="weights",
-    )(*(pltpu.with_memory_space_constraint(w, pltpu.HBM) for w in (f_state, f_action, f_latent, b_state)))
+    )(*in_hbm(f_state, f_action, f_latent, b_state))
     weights = (wf, wb, f_output, b_output, latents, wfb, wbb)
     row_flops = 2 * (c1 + 2 * rank + obs_pad) * hidden + 8 * rank * rank
 

time: 59.6 us -> 58.7 us (0.985)
  Pallas kernels: 23.2 us -> 22.5 us
    pallas_call x1, Pallas kernels: 1.74 us -> 1.04 us  [fast_local(): pl.pallas_call(functools.partial(pack_kernel, cfg), out_shape=shape((rows...]
where the time goes in v8:
time: 58.7 us; the launch traced here: 58.5 us
  Pallas kernels  22.5 us (38%)
  starting transfers between devices  18 us (31%)
  waiting for transfers between devices  16.7 us (28%)
  between operations  0.98 us (2%)
    ppermute x8, waiting for transfers between devices, exchange(): return lax.ppermute(array, axis, [(i, i ^ bit) for i in range(size)])  14 us
    ppermute x8, starting transfers between devices, exchange(): return lax.ppermute(array, axis, [(i, i ^ bit) for i in range(size)])  13.8 us
    pallas_call x5, Pallas kernels, fast_local(): pl.pallas_call(functools.partial(forward_kernel, cfg, count, not early),...  12.4 us
    pallas_call x1, Pallas kernels, fast_local(): pl.pallas_call(functools.partial(last_kernel, cfg, [len(xs) for xs, _ in...  6.01 us
    pallas_call x1, Pallas kernels, fast_local(): pl.pallas_call(functools.partial(weights_kernel, cfg), out_shape=(shape((...  2.17 us
    ppermute x1, waiting for transfers between devices, fast_local(): handed_two = lax.ppermute(across_two, 'dp', outward)  1.65 us
    ppermute x1, starting transfers between devices, fast_local(): handed_two = lax.ppermute(across_two, 'dp', outward)  1.46 us
    ppermute x1, starting transfers between devices, fast_local(): handed = lax.ppermute(across, 'dp', outward)  1.29 us
  transfers between devices with their start and end apart: 12, of which 7 were waited for; matrix products, arithmetic and copies ran while one was open for 0% of the time, Pallas kernels for 25%

profile of v8, /device:TPU:0, one launch (start us, length us, event | category | flops | bytes accessed | tf_op | source)
XLA Modules:
  0.0 58.5 jit_solution(1355628025632087649)
XLA Ops:
  0.6 1.0 %pack.1.refs_0_ = bf16[208,640]{1,0:T(8,128)(2,1)S(1)} custom-call(bf16[1,192,376]{2,1,0:T(8,128)(2,1)} %state_ref.1, bf16[17,192]{1,0:T(8,128)(2,1)} %bitcast.7, s32[1,192]{1,0:T(1,128)} %next_ref.1, s32[1,192]{1,0:T(1,128)} %latent_ref.1, bf16[1,192,256]{2,1,0:T(8,128)(2,1)} %target_ref.1), custom_call_target="tpu_custom_call" | custom-call | tf_op jit(solution)/shard_map/pack/pallas_call | solution.py:318
  2.5 5.9 %collective-permute-start = (bf16[208,640]{1,0:T(8,128)(2,1)S(1)}, bf16[208,640]{1,0:T(8,128)(2,1)S(1)}, u32[]{:S(2)}, u32[]{:S(2)}) collective-permute-start(bf16[208,640]{1,0:T(8,128)(2,1)S(1)} %pack.1.refs_0_), channel_id=1, source_target_pairs={{0,8},{4,12},{8,0},{12,4},{16,24},{20,28},{24,16},{28,20},{1,9},{5... | collective-permute-start | bytes 798728 | tf_op jit(solution)/shard_map/ppermute | solution.py:256
  8.4 1.5 %collective-permute-start.1 = (bf16[208,640]{1,0:T(8,128)(2,1)S(1)}, bf16[208,640]{1,0:T(8,128)(2,1)S(1)}, u32[]{:S(2)}, u32[]{:S(2)}) collective-permute-start(bf16[208,640]{1,0:T(8,128)(2,1)S(1)} %pack.1.refs_0_), channel_id=1, source_target_pairs={{0,4},{4,0},{8,12},{12,8},{16,20},{20,16},{24,28},{28,24},{1,5},{5... | collective-permute-start | bytes 798728 | tf_op jit(solution)/shard_map/ppermute | solution.py:256
  9.9 2.2 %weights.1 = (bf16[768,1536]{1,0:T(8,128)(2,1)S(1)}, bf16[384,1536]{1,0:T(8,128)(2,1)S(1)}, bf16[192,768]{1,0:T(8,128)(2,1)S(1)}, bf16[192,384]{1,0:T(8,128)(2,1)S(1)}) custom-call(bf16[376,1536]{1,0:T(8,128)(2,1)} %fs_hbm.1, bf16[17,1536]{1,0:T(8,128)(2,1)} %fa_hbm.1, bf16[256,1536]{1,0:T(8,128)(2,1)} %fl_hbm.1, bf16[376,1536]{1,0:T(8,128)(2,1)} %bs_hbm.1), custom_call_target="tpu_custom_call" | custom-call | bytes 1000000 | tf_op jit(solution)/shard_map/weights/pallas_call | solution.py:339
  12.1 1.3 %collective-permute-start.4 = (bf16[208,640]{1,0:T(8,128)(2,1)S(1)}, bf16[208,640]{1,0:T(8,128)(2,1)S(1)}, u32[]{:S(2)}, u32[]{:S(2)}) collective-permute-start(bf16[208,640]{1,0:T(8,128)(2,1)S(1)} %collective-permute-done.3), channel_id=1, source_target_pairs={{8,0},{12,4},{16,24},{20,28},{9,1},{13,5},{17,25},{21,29},{10,2},{... | collective-permute-start | bytes 798728 | tf_op jit(solution)/shard_map/ppermute | solution.py:331
  13.4 1.1 %collective-permute-done.refs_0_.refs_7_ = bf16[208,640]{1,0:T(8,128)(2,1)S(1)} collective-permute-done((bf16[208,640]{1,0:T(8,128)(2,1)S(1)}, bf16[208,640]{1,0:T(8,128)(2,1)S(1)}, u32[]{:S(2)}, u32[]{:S(2)}) %collective-permute-start) | collective-permute-done | bytes 266272 | tf_op jit(solution)/shard_map/ppermute | solution.py:256
  15.2 1.9 %forward.5 = (bf16[192,768]{1,0:T(8,128)(2,1)S(1)}, bf16[192,384]{1,0:T(8,128)(2,1)S(1)}, bf16[192,256]{1,0:T(8,128)(2,1)S(1)}, f32[192,256]{1,0:T(8,128)S(1)}, ...) custom-call(bf16[208,640]{1,0:T(8,128)(2,1)S(1)} %pack.1.refs_0_, ...), custom_call_target="tpu_custom_call" | custom-call | flops 3246391296 | bytes 1000000 | tf_op jit(solution)/shard_map/forward/pallas_call | solution.py:385
  17.1 1.6 %collective-permute-start.2 = (bf16[208,640]{1,0:T(8,128)(2,1)S(1)}, bf16[208,640]{1,0:T(8,128)(2,1)S(1)}, u32[]{:S(2)}, u32[]{:S(2)}) collective-permute-start(bf16[208,640]{1,0:T(8,128)(2,1)S(1)} %collective-permute-done.refs_0_.refs_7_), channel_id=1, source_target_pairs={{0,4},{4,0},{8,12},{12,8},{16,20},{20,16},{24,28},{28,24},{1,5},{5... | collective-permute-start | bytes 798728 | tf_op jit(solution)/shard_map/ppermute | solution.py:256
  18.7 1.9 %forward.6 = (bf16[192,768]{1,0:T(8,128)(2,1)S(1)}, bf16[192,384]{1,0:T(8,128)(2,1)S(1)}, bf16[192,256]{1,0:T(8,128)(2,1)S(1)}, f32[192,256]{1,0:T(8,128)S(1)}, ...) custom-call(bf16[208,640]{1,0:T(8,128)(2,1)S(1)} %collective-permute-done.refs_0_.refs_7_, ...), custom_call_target="tpu_custom_call" | custom-call | flops 2164260864 | bytes 1000000 | tf_op jit(solution)/shard_map/forward/pallas_call | solution.py:385
  20.6 1.1 %collective-permute-done.4 = bf16[208,640]{1,0:T(8,128)(2,1)S(1)} collective-permute-done((bf16[208,640]{1,0:T(8,128)(2,1)S(1)}, bf16[208,640]{1,0:T(8,128)(2,1)S(1)}, u32[]{:S(2)}, u32[]{:S(2)}) %collective-permute-start.4) | collective-permute-done | bytes 266272 | tf_op jit(solution)/shard_map/ppermute | solution.py:331
  21.8 1.6 %collective-permute-start.7 = (bf16[208,640]{1,0:T(8,128)(2,1)S(1)}, bf16[208,640]{1,0:T(8,128)(2,1)S(1)}, u32[]{:S(2)}, u32[]{:S(2)}) collective-permute-start(bf16[208,640]{1,0:T(8,128)(2,1)S(1)} %add.12.refs_1_.refs_22_), channel_id=1, source_target_pairs={{0,4},{4,0},{8,12},{12,8},{16,20},{20,16},{24,28},{28,24},{1,5},{5... | collective-permute-start | bytes 798728 | tf_op jit(solution)/shard_map/ppermute | solution.py:256
  23.3 1.5 %collective-permute-start.6 = (bf16[208,640]{1,0:T(8,128)(2,1)S(1)}, bf16[208,640]{1,0:T(8,128)(2,1)S(1)}, u32[]{:S(2)}, u32[]{:S(2)}) collective-permute-start(bf16[208,640]{1,0:T(8,128)(2,1)S(1)} %collective-permute-done.5), channel_id=1, source_target_pairs={{8,0},{12,4},{16,24},{20,28},{9,1},{13,5},{17,25},{21,29},{10,2},{... | collective-permute-start | bytes 798728 | tf_op jit(solution)/shard_map/ppermute | solution.py:336
  24.8 1.9 %forward.7 = (bf16[192,768]{1,0:T(8,128)(2,1)S(1)}, bf16[192,384]{1,0:T(8,128)(2,1)S(1)}, bf16[192,256]{1,0:T(8,128)(2,1)S(1)}, f32[192,256]{1,0:T(8,128)S(1)}, ...) custom-call(bf16[208,640]{1,0:T(8,128)(2,1)S(1)} %collective-permute-done.1.refs_0_.refs_14_, ...), custom_call_target="tpu_custom_call" | custom-call | flops 1623195648 | bytes 1000000 | tf_op jit(solution)/shard_map/forward/pallas_call | solution.py:385
  26.7 3.3 %forward.8 = (bf16[384,768]{1,0:T(8,128)(2,1)S(1)}, bf16[384,384]{1,0:T(8,128)(2,1)S(1)}, bf16[384,256]{1,0:T(8,128)(2,1)S(1)}, f32[384,256]{1,0:T(8,128)S(1)}, ...) custom-call(bf16[208,640]{1,0:T(8,128)(2,1)S(1)} %collective-permute-done.2.refs_0_.refs_21_, ...), custom_call_target="tpu_custom_call" | custom-call | flops 2164260864 | bytes 1000000 | tf_op jit(solution)/shard_map/forward/pallas_call | solution.py:385
  30.1 1.6 %collective-permute-done.6 = bf16[208,640]{1,0:T(8,128)(2,1)S(1)} collective-permute-done((bf16[208,640]{1,0:T(8,128)(2,1)S(1)}, bf16[208,640]{1,0:T(8,128)(2,1)S(1)}, u32[]{:S(2)}, u32[]{:S(2)}) %collective-permute-start.6) | collective-permute-done | bytes 266272 | tf_op jit(solution)/shard_map/ppermute | solution.py:336
  31.8 1.6 %collective-permute-start.8 = (bf16[208,640]{1,0:T(8,128)(2,1)S(1)}, bf16[208,640]{1,0:T(8,128)(2,1)S(1)}, u32[]{:S(2)}, u32[]{:S(2)}) collective-permute-start(bf16[208,640]{1,0:T(8,128)(2,1)S(1)} %add.13.refs_0_.refs_29_), channel_id=1, source_target_pairs={{0,4},{4,0},{8,12},{12,8},{16,20},{20,16},{24,28},{28,24},{1,5},{5... | collective-permute-start | bytes 798728 | tf_op jit(solution)/shard_map/ppermute | solution.py:256
  33.3 3.3 %forward.9 = (bf16[384,768]{1,0:T(8,128)(2,1)S(1)}, bf16[384,384]{1,0:T(8,128)(2,1)S(1)}, bf16[384,256]{1,0:T(8,128)(2,1)S(1)}, f32[384,256]{1,0:T(8,128)S(1)}, ...) custom-call(bf16[208,640]{1,0:T(8,128)(2,1)S(1)} %add.13.refs_0_.refs_29_, ...), custom_call_target="tpu_custom_call" | custom-call | flops 6492782592 | bytes 1000000 | tf_op jit(solution)/shard_map/forward/pallas_call | solution.py:385
  36.7 1.6 %collective-permute-done.8.refs_37_ = bf16[208,640]{1,0:T(8,128)(2,1)S(1)} collective-permute-done((bf16[208,640]{1,0:T(8,128)(2,1)S(1)}, bf16[208,640]{1,0:T(8,128)(2,1)S(1)}, u32[]{:S(2)}, u32[]{:S(2)}) %collective-permute-start.8) | collective-permute-done | bytes 266272 | tf_op jit(solution)/shard_map/ppermute | solution.py:256
  38.3 6.0 %last.1 = (bf16[96,1664]{1,0:T(8,128)(2,1)S(1)}, f32[96,1664]{1,0:T(8,128)S(1)}) custom-call(bf16[208,640]{1,0:T(8,128)(2,1)S(1)} %pack.1.refs_0_, bf16[192,768]{1,0:T(8,128)(2,1)S(1)} %get-tuple-element.59.refs_1_, bf16[192,384]{1,0:T(8,128)(2,1)S(1)} %get-tuple-element.60.refs_2_, bf16[192,256]{1,0:T(8,128)(2,1)S(1)} %get-tuple-element.61.refs_3_, ...), custom_call_target="tpu_custom_call" | custom-call | flops 1962934272 | bytes 16000000 | tf_op jit(solution)/shard_map/last/pallas_call | solution.py:402
  44.4 1.6 %collective-permute-done.9 = bf16[96,1664]{1,0:T(8,128)(2,1)S(1)} collective-permute-done((bf16[96,1664]{1,0:T(8,128)(2,1)S(1)}, bf16[96,1664]{1,0:T(8,128)(2,1)S(1)}, u32[]{:S(2)}, u32[]{:S(2)}) %collective-permute-start.9) | collective-permute-done | bytes 319520 | tf_op jit(solution)/shard_map/ppermute | solution.py:256
  46.0 1.6 %collective-permute-start.10 = (bf16[96,1664]{1,0:T(8,128)(2,1)S(1)}, bf16[96,1664]{1,0:T(8,128)(2,1)S(1)}, u32[]{:S(2)}, u32[]{:S(2)}) collective-permute-start(bf16[96,1664]{1,0:T(8,128)(2,1)S(1)} %add_convert_fusion.1.one_ref), channel_id=1, source_target_pairs={{0,2},{1,3},{2,0},{3,1},{4,6},{5,7},{6,4},{7,5},{8,10},{9,11},{10,... | collective-permute-start | bytes 958472 | tf_op jit(solution)/shard_map/ppermute | solution.py:256
  47.6 8.1 %collective-permute-done.10.two_ref = bf16[96,1664]{1,0:T(8,128)(2,1)S(1)} collective-permute-done((bf16[96,1664]{1,0:T(8,128)(2,1)S(1)}, bf16[96,1664]{1,0:T(8,128)(2,1)S(1)}, u32[]{:S(2)}, u32[]{:S(2)}) %collective-permute-start.10) | collective-permute-done | bytes 319520 | tf_op jit(solution)/shard_map/ppermute | solution.py:256
  55.8 1.6 %collective-permute-done.11.far_ref = bf16[96,1664]{1,0:T(8,128)(2,1)S(1)} collective-permute-done((bf16[96,1664]{1,0:T(8,128)(2,1)S(1)}, bf16[96,1664]{1,0:T(8,128)(2,1)S(1)}, u32[]{:S(2)}, u32[]{:S(2)}) %collective-permute-start.11) | collective-permute-done | bytes 319520 | tf_op jit(solution)/shard_map/ppermute | solution.py:256
  57.4 0.9 %finish.1 = (bf16[192,376]{1,0:T(8,128)(2,1)}, bf16[17,192]{1,0:T(8,128)(2,1)}, bf16[192,256]{1,0:T(8,128)(2,1)}, bf16[192,256]{1,0:T(8,128)(2,1)}, bf16[192,376...) custom-call(bf16[96,1664]{1,0:T(8,128)(2,1)S(1)} %add_convert_fusion.1.one_ref, ...), custom_call_target="tpu_custom_call" | custom-call | tf_op jit(solution)/shard_map/finish/pallas_call | solution.py:420
  (19 shorter events, 1.9 us)
Async XLA Ops:
  1.7 13.5 %copy-start = (bf16[1536,256]{1,0:T(8,128)(2,1)S(1)}, bf16[1536,256]{1,0:T(8,128)(2,1)}, u32[]{:S(2)}) copy-start(bf16[1536,256]{1,0:T(8,128)(2,1)} %refs_40_.1) | copy-start | bytes 2359300
  1.7 13.5 %copy-start.1 = (bf16[1536,256]{1,0:T(8,128)(2,1)S(1)}, bf16[1536,256]{1,0:T(8,128)(2,1)}, u32[]{:S(2)}) copy-start(bf16[1536,256]{1,0:T(8,128)(2,1)} %refs_41_.1) | copy-start | bytes 2359300
  1.7 13.5 %copy-start.2 = (bf16[256,256]{1,0:T(8,128)(2,1)S(1)}, bf16[256,256]{1,0:T(8,128)(2,1)}, u32[]{:S(2)}) copy-start(bf16[256,256]{1,0:T(8,128)(2,1)} %refs_42_.1) | copy-start | bytes 393220
  1.7 10.4 %collective-permute-start.3 = (bf16[208,640]{1,0:T(8,128)(2,1)S(1)}, bf16[208,640]{1,0:T(8,128)(2,1)S(1)}, u32[]{:S(2)}, u32[]{:S(2)}) collective-permute-start(bf16[208,640]{1,0:T(8,128)(2,1)S(1)} %pack.1.refs_0_), channel_id=1, source_target_pairs={{8,16},{12,20},{16,8},{20,12},{9,17},{13,21},{17,9},{21,13},{10,18... | collective-permute-start | bytes 798728 | tf_op jit(solution)/shard_map/ppermute | solution.py:328
  2.5 12.0 %collective-permute-start = (bf16[208,640]{1,0:T(8,128)(2,1)S(1)}, bf16[208,640]{1,0:T(8,128)(2,1)S(1)}, u32[]{:S(2)}, u32[]{:S(2)}) collective-permute-start(bf16[208,640]{1,0:T(8,128)(2,1)S(1)} %pack.1.refs_0_), channel_id=1, source_target_pairs={{0,8},{4,12},{8,0},{12,4},{16,24},{20,28},{24,16},{28,20},{1,9},{5... | collective-permute-start | bytes 798728 | tf_op jit(solution)/shard_map/ppermute | solution.py:256
  8.4 16.4 %collective-permute-start.1 = (bf16[208,640]{1,0:T(8,128)(2,1)S(1)}, bf16[208,640]{1,0:T(8,128)(2,1)S(1)}, u32[]{:S(2)}, u32[]{:S(2)}) collective-permute-start(bf16[208,640]{1,0:T(8,128)(2,1)S(1)} %pack.1.refs_0_), channel_id=1, source_target_pairs={{0,4},{4,0},{8,12},{12,8},{16,20},{20,16},{24,28},{28,24},{1,5},{5... | collective-permute-start | bytes 798728 | tf_op jit(solution)/shard_map/ppermute | solution.py:256
  12.1 9.6 %collective-permute-start.4 = (bf16[208,640]{1,0:T(8,128)(2,1)S(1)}, bf16[208,640]{1,0:T(8,128)(2,1)S(1)}, u32[]{:S(2)}, u32[]{:S(2)}) collective-permute-start(bf16[208,640]{1,0:T(8,128)(2,1)S(1)} %collective-permute-done.3), channel_id=1, source_target_pairs={{8,0},{12,4},{16,24},{20,28},{9,1},{13,5},{17,25},{21,29},{10,2},{... | collective-permute-start | bytes 798728 | tf_op jit(solution)/shard_map/ppermute | solution.py:331
  14.5 8.8 %collective-permute-start.5 = (bf16[208,640]{1,0:T(8,128)(2,1)S(1)}, bf16[208,640]{1,0:T(8,128)(2,1)S(1)}, u32[]{:S(2)}, u32[]{:S(2)}) collective-permute-start(bf16[208,640]{1,0:T(8,128)(2,1)S(1)} %collective-permute-done.refs_0_.refs_7_), channel_id=1, source_target_pairs={{8,16},{12,20},{16,8},{20,12},{9,17},{13,21},{17,9},{21,13},{10,18... | collective-permute-start | bytes 798728 | tf_op jit(solution)/shard_map/ppermute | solution.py:333
  17.1 9.6 %collective-permute-start.2 = (bf16[208,640]{1,0:T(8,128)(2,1)S(1)}, bf16[208,640]{1,0:T(8,128)(2,1)S(1)}, u32[]{:S(2)}, u32[]{:S(2)}) collective-permute-start(bf16[208,640]{1,0:T(8,128)(2,1)S(1)} %collective-permute-done.refs_0_.refs_7_), channel_id=1, source_target_pairs={{0,4},{4,0},{8,12},{12,8},{16,20},{20,16},{24,28},{28,24},{1,5},{5... | collective-permute-start | bytes 798728 | tf_op jit(solution)/shard_map/ppermute | solution.py:256
  21.8 11.6 %collective-permute-start.7 = (bf16[208,640]{1,0:T(8,128)(2,1)S(1)}, bf16[208,640]{1,0:T(8,128)(2,1)S(1)}, u32[]{:S(2)}, u32[]{:S(2)}) collective-permute-start(bf16[208,640]{1,0:T(8,128)(2,1)S(1)} %add.12.refs_1_.refs_22_), channel_id=1, source_target_pairs={{0,4},{4,0},{8,12},{12,8},{16,20},{20,16},{24,28},{28,24},{1,5},{5... | collective-permute-start | bytes 798728 | tf_op jit(solution)/shard_map/ppermute | solution.py:256
  23.3 8.4 %collective-permute-start.6 = (bf16[208,640]{1,0:T(8,128)(2,1)S(1)}, bf16[208,640]{1,0:T(8,128)(2,1)S(1)}, u32[]{:S(2)}, u32[]{:S(2)}) collective-permute-start(bf16[208,640]{1,0:T(8,128)(2,1)S(1)} %collective-permute-done.5), channel_id=1, source_target_pairs={{8,0},{12,4},{16,24},{20,28},{9,1},{13,5},{17,25},{21,29},{10,2},{... | collective-permute-start | bytes 798728 | tf_op jit(solution)/shard_map/ppermute | solution.py:336
  31.8 6.5 %collective-permute-start.8 = (bf16[208,640]{1,0:T(8,128)(2,1)S(1)}, bf16[208,640]{1,0:T(8,128)(2,1)S(1)}, u32[]{:S(2)}, u32[]{:S(2)}) collective-permute-start(bf16[208,640]{1,0:T(8,128)(2,1)S(1)} %add.13.refs_0_.refs_29_), channel_id=1, source_target_pairs={{0,4},{4,0},{8,12},{12,8},{16,20},{20,16},{24,28},{28,24},{1,5},{5... | collective-permute-start | bytes 798728 | tf_op jit(solution)/shard_map/ppermute | solution.py:256
  44.3 1.7 %collective-permute-start.9 = (bf16[96,1664]{1,0:T(8,128)(2,1)S(1)}, bf16[96,1664]{1,0:T(8,128)(2,1)S(1)}, u32[]{:S(2)}, u32[]{:S(2)}) collective-permute-start(bf16[96,1664]{1,0:T(8,128)(2,1)S(1)} %get-tuple-element.95), channel_id=1, source_target_pairs={{0,1},{1,0},{2,3},{3,2},{4,5},{5,4},{6,7},{7,6},{8,9},{9,8},{10,11... | collective-permute-start | bytes 958472 | tf_op jit(solution)/shard_map/ppermute | solution.py:256
  46.0 9.6 %collective-permute-start.10 = (bf16[96,1664]{1,0:T(8,128)(2,1)S(1)}, bf16[96,1664]{1,0:T(8,128)(2,1)S(1)}, u32[]{:S(2)}, u32[]{:S(2)}) collective-permute-start(bf16[96,1664]{1,0:T(8,128)(2,1)S(1)} %add_convert_fusion.1.one_ref), channel_id=1, source_target_pairs={{0,2},{1,3},{2,0},{3,1},{4,6},{5,7},{6,4},{7,5},{8,10},{9,11},{10,... | collective-permute-start | bytes 958472 | tf_op jit(solution)/shard_map/ppermute | solution.py:256
  55.8 1.7 %collective-permute-start.11 = (bf16[96,1664]{1,0:T(8,128)(2,1)S(1)}, bf16[96,1664]{1,0:T(8,128)(2,1)S(1)}, u32[]{:S(2)}, u32[]{:S(2)}) collective-permute-start(bf16[96,1664]{1,0:T(8,128)(2,1)S(1)} %add_convert_fusion), channel_id=1, source_target_pairs={{0,1},{1,0},{2,3},{3,2},{4,5},{5,4},{6,7},{7,6},{8,9},{9,8},{10,11... | collective-permute-start | bytes 958472 | tf_op jit(solution)/shard_map/ppermute | solution.py:256

commit v9 on v8

--- a/solution.py
+++ b/solution.py
@@ -129,10 +129,9 @@
     u_ref[...] = u
     fh_ref[...] = jnp.maximum(dot_nt(wfb_ref[...], whole), 0.0).astype(BF16)
     bh_ref[...] = jnp.maximum(dot_nt(wbb_ref[...], later), 0.0).astype(BF16)
-    cross = dot_tn(emb, emb)
-    for j, x_ref in enumerate(xs):
-        cross = cross - GAMMA * dot_tn(x_ref[0:rows, obs_pad:], emb[j * rows : (j + 1) * rows])
-    return dot_tn(back, back), cross
+    target = join([x_ref[0:rows, obs_pad:] for x_ref in xs], 0)
+    both = dot_tn(join([emb, target], 1), emb)
+    return dot_tn(back, back), both[:rank] - GAMMA * both[rank:]
 
 
 def forward_kernel(cfg, count, first, *refs):

time: 58.7 us -> 58.8 us (level)
  no operation moved by 1% of the time
where the time goes in v9:
time: 58.8 us; the launch traced here: 58.6 us
  Pallas kernels  22.6 us (38%)
  starting transfers between devices  18 us (31%)
  waiting for transfers between devices  16.6 us (28%)
  between operations  0.98 us (2%)
    ppermute x8, waiting for transfers between devices, exchange(): return lax.ppermute(array, axis, [(i, i ^ bit) for i in range(size)])  14 us
    ppermute x8, starting transfers between devices, exchange(): return lax.ppermute(array, axis, [(i, i ^ bit) for i in range(size)])  13.8 us
    pallas_call x5, Pallas kernels, fast_local(): pl.pallas_call(functools.partial(forward_kernel, cfg, count, not early),...  12.4 us
    pallas_call x1, Pallas kernels, fast_local(): pl.pallas_call(functools.partial(last_kernel, cfg, [len(xs) for xs, _ in...  6.04 us
    pallas_call x1, Pallas kernels, fast_local(): pl.pallas_call(functools.partial(weights_kernel, cfg), out_shape=(shape((...  2.17 us
    ppermute x1, waiting for transfers between devices, fast_local(): handed_two = lax.ppermute(across_two, 'dp', outward)  1.6 us
    ppermute x1, starting transfers between devices, fast_local(): handed_two = lax.ppermute(across_two, 'dp', outward)  1.46 us
    ppermute x1, starting transfers between devices, fast_local(): handed = lax.ppermute(across, 'dp', outward)  1.29 us
  transfers between devices with their start and end apart: 12, of which 7 were waited for; matrix products, arithmetic and copies ran while one was open for 0% of the time, Pallas kernels for 25%

profile of v9, /device:TPU:0, one launch (start us, length us, event | category | flops | bytes accessed | tf_op | source)
XLA Modules:
  0.0 58.6 jit_solution(8034977722025784487)
XLA Ops:
  0.6 1.0 %pack.1.refs_0_ = bf16[208,640]{1,0:T(8,128)(2,1)S(1)} custom-call(bf16[1,192,376]{2,1,0:T(8,128)(2,1)} %state_ref.1, bf16[17,192]{1,0:T(8,128)(2,1)} %bitcast.7, s32[1,192]{1,0:T(1,128)} %next_ref.1, s32[1,192]{1,0:T(1,128)} %latent_ref.1, bf16[1,192,256]{2,1,0:T(8,128)(2,1)} %target_ref.1), custom_call_target="tpu_custom_call" | custom-call | tf_op jit(solution)/shard_map/pack/pallas_call | solution.py:317
  2.5 5.9 %collective-permute-start = (bf16[208,640]{1,0:T(8,128)(2,1)S(1)}, bf16[208,640]{1,0:T(8,128)(2,1)S(1)}, u32[]{:S(2)}, u32[]{:S(2)}) collective-permute-start(bf16[208,640]{1,0:T(8,128)(2,1)S(1)} %pack.1.refs_0_), channel_id=1, source_target_pairs={{0,8},{4,12},{8,0},{12,4},{16,24},{20,28},{24,16},{28,20},{1,9},{5... | collective-permute-start | bytes 798728 | tf_op jit(solution)/shard_map/ppermute | solution.py:255
  8.4 1.5 %collective-permute-start.1 = (bf16[208,640]{1,0:T(8,128)(2,1)S(1)}, bf16[208,640]{1,0:T(8,128)(2,1)S(1)}, u32[]{:S(2)}, u32[]{:S(2)}) collective-permute-start(bf16[208,640]{1,0:T(8,128)(2,1)S(1)} %pack.1.refs_0_), channel_id=1, source_target_pairs={{0,4},{4,0},{8,12},{12,8},{16,20},{20,16},{24,28},{28,24},{1,5},{5... | collective-permute-start | bytes 798728 | tf_op jit(solution)/shard_map/ppermute | solution.py:255
  9.9 2.2 %weights.1 = (bf16[768,1536]{1,0:T(8,128)(2,1)S(1)}, bf16[384,1536]{1,0:T(8,128)(2,1)S(1)}, bf16[192,768]{1,0:T(8,128)(2,1)S(1)}, bf16[192,384]{1,0:T(8,128)(2,1)S(1)}) custom-call(bf16[376,1536]{1,0:T(8,128)(2,1)} %fs_hbm.1, bf16[17,1536]{1,0:T(8,128)(2,1)} %fa_hbm.1, bf16[256,1536]{1,0:T(8,128)(2,1)} %fl_hbm.1, bf16[376,1536]{1,0:T(8,128)(2,1)} %bs_hbm.1), custom_call_target="tpu_custom_call" | custom-call | bytes 1000000 | tf_op jit(solution)/shard_map/weights/pallas_call | solution.py:338
  12.1 1.3 %collective-permute-start.4 = (bf16[208,640]{1,0:T(8,128)(2,1)S(1)}, bf16[208,640]{1,0:T(8,128)(2,1)S(1)}, u32[]{:S(2)}, u32[]{:S(2)}) collective-permute-start(bf16[208,640]{1,0:T(8,128)(2,1)S(1)} %collective-permute-done.3), channel_id=1, source_target_pairs={{8,0},{12,4},{16,24},{20,28},{9,1},{13,5},{17,25},{21,29},{10,2},{... | collective-permute-start | bytes 798728 | tf_op jit(solution)/shard_map/ppermute | solution.py:330
  13.4 1.1 %collective-permute-done.refs_0_.refs_7_ = bf16[208,640]{1,0:T(8,128)(2,1)S(1)} collective-permute-done((bf16[208,640]{1,0:T(8,128)(2,1)S(1)}, bf16[208,640]{1,0:T(8,128)(2,1)S(1)}, u32[]{:S(2)}, u32[]{:S(2)}) %collective-permute-start) | collective-permute-done | bytes 266272 | tf_op jit(solution)/shard_map/ppermute | solution.py:255
  15.2 1.9 %forward.5 = (bf16[192,768]{1,0:T(8,128)(2,1)S(1)}, bf16[192,384]{1,0:T(8,128)(2,1)S(1)}, bf16[192,256]{1,0:T(8,128)(2,1)S(1)}, f32[192,256]{1,0:T(8,128)S(1)}, ...) custom-call(bf16[208,640]{1,0:T(8,128)(2,1)S(1)} %pack.1.refs_0_, ...), custom_call_target="tpu_custom_call" | custom-call | flops 3246391296 | bytes 1000000 | tf_op jit(solution)/shard_map/forward/pallas_call | solution.py:384
  17.1 1.6 %collective-permute-start.2 = (bf16[208,640]{1,0:T(8,128)(2,1)S(1)}, bf16[208,640]{1,0:T(8,128)(2,1)S(1)}, u32[]{:S(2)}, u32[]{:S(2)}) collective-permute-start(bf16[208,640]{1,0:T(8,128)(2,1)S(1)} %collective-permute-done.refs_0_.refs_7_), channel_id=1, source_target_pairs={{0,4},{4,0},{8,12},{12,8},{16,20},{20,16},{24,28},{28,24},{1,5},{5... | collective-permute-start | bytes 798728 | tf_op jit(solution)/shard_map/ppermute | solution.py:255
  18.7 1.9 %forward.6 = (bf16[192,768]{1,0:T(8,128)(2,1)S(1)}, bf16[192,384]{1,0:T(8,128)(2,1)S(1)}, bf16[192,256]{1,0:T(8,128)(2,1)S(1)}, f32[192,256]{1,0:T(8,128)S(1)}, ...) custom-call(bf16[208,640]{1,0:T(8,128)(2,1)S(1)} %collective-permute-done.refs_0_.refs_7_, ...), custom_call_target="tpu_custom_call" | custom-call | flops 2164260864 | bytes 1000000 | tf_op jit(solution)/shard_map/forward/pallas_call | solution.py:384
  20.6 1.1 %collective-permute-done.4 = bf16[208,640]{1,0:T(8,128)(2,1)S(1)} collective-permute-done((bf16[208,640]{1,0:T(8,128)(2,1)S(1)}, bf16[208,640]{1,0:T(8,128)(2,1)S(1)}, u32[]{:S(2)}, u32[]{:S(2)}) %collective-permute-start.4) | collective-permute-done | bytes 266272 | tf_op jit(solution)/shard_map/ppermute | solution.py:330
  21.8 1.6 %collective-permute-start.7 = (bf16[208,640]{1,0:T(8,128)(2,1)S(1)}, bf16[208,640]{1,0:T(8,128)(2,1)S(1)}, u32[]{:S(2)}, u32[]{:S(2)}) collective-permute-start(bf16[208,640]{1,0:T(8,128)(2,1)S(1)} %add.12.refs_1_.refs_22_), channel_id=1, source_target_pairs={{0,4},{4,0},{8,12},{12,8},{16,20},{20,16},{24,28},{28,24},{1,5},{5... | collective-permute-start | bytes 798728 | tf_op jit(solution)/shard_map/ppermute | solution.py:255
  23.3 1.5 %collective-permute-start.6 = (bf16[208,640]{1,0:T(8,128)(2,1)S(1)}, bf16[208,640]{1,0:T(8,128)(2,1)S(1)}, u32[]{:S(2)}, u32[]{:S(2)}) collective-permute-start(bf16[208,640]{1,0:T(8,128)(2,1)S(1)} %collective-permute-done.5), channel_id=1, source_target_pairs={{8,0},{12,4},{16,24},{20,28},{9,1},{13,5},{17,25},{21,29},{10,2},{... | collective-permute-start | bytes 798728 | tf_op jit(solution)/shard_map/ppermute | solution.py:335
  24.8 1.9 %forward.7 = (bf16[192,768]{1,0:T(8,128)(2,1)S(1)}, bf16[192,384]{1,0:T(8,128)(2,1)S(1)}, bf16[192,256]{1,0:T(8,128)(2,1)S(1)}, f32[192,256]{1,0:T(8,128)S(1)}, ...) custom-call(bf16[208,640]{1,0:T(8,128)(2,1)S(1)} %collective-permute-done.1.refs_0_.refs_14_, ...), custom_call_target="tpu_custom_call" | custom-call | flops 1623195648 | bytes 1000000 | tf_op jit(solution)/shard_map/forward/pallas_call | solution.py:384
  26.7 3.4 %forward.8 = (bf16[384,768]{1,0:T(8,128)(2,1)S(1)}, bf16[384,384]{1,0:T(8,128)(2,1)S(1)}, bf16[384,256]{1,0:T(8,128)(2,1)S(1)}, f32[384,256]{1,0:T(8,128)S(1)}, ...) custom-call(bf16[208,640]{1,0:T(8,128)(2,1)S(1)} %collective-permute-done.2.refs_0_.refs_21_, ...), custom_call_target="tpu_custom_call" | custom-call | flops 2164260864 | bytes 1000000 | tf_op jit(solution)/shard_map/forward/pallas_call | solution.py:384
  30.1 1.6 %collective-permute-done.6 = bf16[208,640]{1,0:T(8,128)(2,1)S(1)} collective-permute-done((bf16[208,640]{1,0:T(8,128)(2,1)S(1)}, bf16[208,640]{1,0:T(8,128)(2,1)S(1)}, u32[]{:S(2)}, u32[]{:S(2)}) %collective-permute-start.6) | collective-permute-done | bytes 266272 | tf_op jit(solution)/shard_map/ppermute | solution.py:335
  31.8 1.6 %collective-permute-start.8 = (bf16[208,640]{1,0:T(8,128)(2,1)S(1)}, bf16[208,640]{1,0:T(8,128)(2,1)S(1)}, u32[]{:S(2)}, u32[]{:S(2)}) collective-permute-start(bf16[208,640]{1,0:T(8,128)(2,1)S(1)} %add.13.refs_0_.refs_29_), channel_id=1, source_target_pairs={{0,4},{4,0},{8,12},{12,8},{16,20},{20,16},{24,28},{28,24},{1,5},{5... | collective-permute-start | bytes 798728 | tf_op jit(solution)/shard_map/ppermute | solution.py:255
  33.4 3.4 %forward.9 = (bf16[384,768]{1,0:T(8,128)(2,1)S(1)}, bf16[384,384]{1,0:T(8,128)(2,1)S(1)}, bf16[384,256]{1,0:T(8,128)(2,1)S(1)}, f32[384,256]{1,0:T(8,128)S(1)}, ...) custom-call(bf16[208,640]{1,0:T(8,128)(2,1)S(1)} %add.13.refs_0_.refs_29_, ...), custom_call_target="tpu_custom_call" | custom-call | flops 6492782592 | bytes 1000000 | tf_op jit(solution)/shard_map/forward/pallas_call | solution.py:384
  36.7 1.5 %collective-permute-done.8.refs_37_ = bf16[208,640]{1,0:T(8,128)(2,1)S(1)} collective-permute-done((bf16[208,640]{1,0:T(8,128)(2,1)S(1)}, bf16[208,640]{1,0:T(8,128)(2,1)S(1)}, u32[]{:S(2)}, u32[]{:S(2)}) %collective-permute-start.8) | collective-permute-done | bytes 266272 | tf_op jit(solution)/shard_map/ppermute | solution.py:255
  38.3 6.0 %last.1 = (bf16[96,1664]{1,0:T(8,128)(2,1)S(1)}, f32[96,1664]{1,0:T(8,128)S(1)}) custom-call(bf16[208,640]{1,0:T(8,128)(2,1)S(1)} %pack.1.refs_0_, bf16[192,768]{1,0:T(8,128)(2,1)S(1)} %get-tuple-element.59.refs_1_, bf16[192,384]{1,0:T(8,128)(2,1)S(1)} %get-tuple-element.60.refs_2_, bf16[192,256]{1,0:T(8,128)(2,1)S(1)} %get-tuple-element.61.refs_3_, ...), custom_call_target="tpu_custom_call" | custom-call | flops 1962934272 | bytes 16000000 | tf_op jit(solution)/shard_map/last/pallas_call | solution.py:401
  44.4 1.6 %collective-permute-done.9 = bf16[96,1664]{1,0:T(8,128)(2,1)S(1)} collective-permute-done((bf16[96,1664]{1,0:T(8,128)(2,1)S(1)}, bf16[96,1664]{1,0:T(8,128)(2,1)S(1)}, u32[]{:S(2)}, u32[]{:S(2)}) %collective-permute-start.9) | collective-permute-done | bytes 319520 | tf_op jit(solution)/shard_map/ppermute | solution.py:255
  46.1 1.6 %collective-permute-start.10 = (bf16[96,1664]{1,0:T(8,128)(2,1)S(1)}, bf16[96,1664]{1,0:T(8,128)(2,1)S(1)}, u32[]{:S(2)}, u32[]{:S(2)}) collective-permute-start(bf16[96,1664]{1,0:T(8,128)(2,1)S(1)} %add_convert_fusion.1.one_ref), channel_id=1, source_target_pairs={{0,2},{1,3},{2,0},{3,1},{4,6},{5,7},{6,4},{7,5},{8,10},{9,11},{10,... | collective-permute-start | bytes 958472 | tf_op jit(solution)/shard_map/ppermute | solution.py:255
  47.6 8.1 %collective-permute-done.10.two_ref = bf16[96,1664]{1,0:T(8,128)(2,1)S(1)} collective-permute-done((bf16[96,1664]{1,0:T(8,128)(2,1)S(1)}, bf16[96,1664]{1,0:T(8,128)(2,1)S(1)}, u32[]{:S(2)}, u32[]{:S(2)}) %collective-permute-start.10) | collective-permute-done | bytes 319520 | tf_op jit(solution)/shard_map/ppermute | solution.py:255
  55.9 1.6 %collective-permute-done.11.far_ref = bf16[96,1664]{1,0:T(8,128)(2,1)S(1)} collective-permute-done((bf16[96,1664]{1,0:T(8,128)(2,1)S(1)}, bf16[96,1664]{1,0:T(8,128)(2,1)S(1)}, u32[]{:S(2)}, u32[]{:S(2)}) %collective-permute-start.11) | collective-permute-done | bytes 319520 | tf_op jit(solution)/shard_map/ppermute | solution.py:255
  57.5 0.9 %finish.1 = (bf16[192,376]{1,0:T(8,128)(2,1)}, bf16[17,192]{1,0:T(8,128)(2,1)}, bf16[192,256]{1,0:T(8,128)(2,1)}, bf16[192,256]{1,0:T(8,128)(2,1)}, bf16[192,376...) custom-call(bf16[96,1664]{1,0:T(8,128)(2,1)S(1)} %add_convert_fusion.1.one_ref, ...), custom_call_target="tpu_custom_call" | custom-call | tf_op jit(solution)/shard_map/finish/pallas_call | solution.py:419
  (19 shorter events, 1.9 us)
Async XLA Ops:
  1.7 13.5 %copy-start = (bf16[1536,256]{1,0:T(8,128)(2,1)S(1)}, bf16[1536,256]{1,0:T(8,128)(2,1)}, u32[]{:S(2)}) copy-start(bf16[1536,256]{1,0:T(8,128)(2,1)} %refs_40_.1) | copy-start | bytes 2359300
  1.7 13.5 %copy-start.1 = (bf16[1536,256]{1,0:T(8,128)(2,1)S(1)}, bf16[1536,256]{1,0:T(8,128)(2,1)}, u32[]{:S(2)}) copy-start(bf16[1536,256]{1,0:T(8,128)(2,1)} %refs_41_.1) | copy-start | bytes 2359300
  1.7 13.5 %copy-start.2 = (bf16[256,256]{1,0:T(8,128)(2,1)S(1)}, bf16[256,256]{1,0:T(8,128)(2,1)}, u32[]{:S(2)}) copy-start(bf16[256,256]{1,0:T(8,128)(2,1)} %refs_42_.1) | copy-start | bytes 393220
  1.7 10.4 %collective-permute-start.3 = (bf16[208,640]{1,0:T(8,128)(2,1)S(1)}, bf16[208,640]{1,0:T(8,128)(2,1)S(1)}, u32[]{:S(2)}, u32[]{:S(2)}) collective-permute-start(bf16[208,640]{1,0:T(8,128)(2,1)S(1)} %pack.1.refs_0_), channel_id=1, source_target_pairs={{8,16},{12,20},{16,8},{20,12},{9,17},{13,21},{17,9},{21,13},{10,18... | collective-permute-start | bytes 798728 | tf_op jit(solution)/shard_map/ppermute | solution.py:327
  2.5 12.0 %collective-permute-start = (bf16[208,640]{1,0:T(8,128)(2,1)S(1)}, bf16[208,640]{1,0:T(8,128)(2,1)S(1)}, u32[]{:S(2)}, u32[]{:S(2)}) collective-permute-start(bf16[208,640]{1,0:T(8,128)(2,1)S(1)} %pack.1.refs_0_), channel_id=1, source_target_pairs={{0,8},{4,12},{8,0},{12,4},{16,24},{20,28},{24,16},{28,20},{1,9},{5... | collective-permute-start | bytes 798728 | tf_op jit(solution)/shard_map/ppermute | solution.py:255
  8.4 16.4 %collective-permute-start.1 = (bf16[208,640]{1,0:T(8,128)(2,1)S(1)}, bf16[208,640]{1,0:T(8,128)(2,1)S(1)}, u32[]{:S(2)}, u32[]{:S(2)}) collective-permute-start(bf16[208,640]{1,0:T(8,128)(2,1)S(1)} %pack.1.refs_0_), channel_id=1, source_target_pairs={{0,4},{4,0},{8,12},{12,8},{16,20},{20,16},{24,28},{28,24},{1,5},{5... | collective-permute-start | bytes 798728 | tf_op jit(solution)/shard_map/ppermute | solution.py:255
  12.1 9.6 %collective-permute-start.4 = (bf16[208,640]{1,0:T(8,128)(2,1)S(1)}, bf16[208,640]{1,0:T(8,128)(2,1)S(1)}, u32[]{:S(2)}, u32[]{:S(2)}) collective-permute-start(bf16[208,640]{1,0:T(8,128)(2,1)S(1)} %collective-permute-done.3), channel_id=1, source_target_pairs={{8,0},{12,4},{16,24},{20,28},{9,1},{13,5},{17,25},{21,29},{10,2},{... | collective-permute-start | bytes 798728 | tf_op jit(solution)/shard_map/ppermute | solution.py:330
  14.5 8.8 %collective-permute-start.5 = (bf16[208,640]{1,0:T(8,128)(2,1)S(1)}, bf16[208,640]{1,0:T(8,128)(2,1)S(1)}, u32[]{:S(2)}, u32[]{:S(2)}) collective-permute-start(bf16[208,640]{1,0:T(8,128)(2,1)S(1)} %collective-permute-done.refs_0_.refs_7_), channel_id=1, source_target_pairs={{8,16},{12,20},{16,8},{20,12},{9,17},{13,21},{17,9},{21,13},{10,18... | collective-permute-start | bytes 798728 | tf_op jit(solution)/shard_map/ppermute | solution.py:332
  17.1 9.6 %collective-permute-start.2 = (bf16[208,640]{1,0:T(8,128)(2,1)S(1)}, bf16[208,640]{1,0:T(8,128)(2,1)S(1)}, u32[]{:S(2)}, u32[]{:S(2)}) collective-permute-start(bf16[208,640]{1,0:T(8,128)(2,1)S(1)} %collective-permute-done.refs_0_.refs_7_), channel_id=1, source_target_pairs={{0,4},{4,0},{8,12},{12,8},{16,20},{20,16},{24,28},{28,24},{1,5},{5... | collective-permute-start | bytes 798728 | tf_op jit(solution)/shard_map/ppermute | solution.py:255
  21.8 11.6 %collective-permute-start.7 = (bf16[208,640]{1,0:T(8,128)(2,1)S(1)}, bf16[208,640]{1,0:T(8,128)(2,1)S(1)}, u32[]{:S(2)}, u32[]{:S(2)}) collective-permute-start(bf16[208,640]{1,0:T(8,128)(2,1)S(1)} %add.12.refs_1_.refs_22_), channel_id=1, source_target_pairs={{0,4},{4,0},{8,12},{12,8},{16,20},{20,16},{24,28},{28,24},{1,5},{5... | collective-permute-start | bytes 798728 | tf_op jit(solution)/shard_map/ppermute | solution.py:255
  23.3 8.4 %collective-permute-start.6 = (bf16[208,640]{1,0:T(8,128)(2,1)S(1)}, bf16[208,640]{1,0:T(8,128)(2,1)S(1)}, u32[]{:S(2)}, u32[]{:S(2)}) collective-permute-start(bf16[208,640]{1,0:T(8,128)(2,1)S(1)} %collective-permute-done.5), channel_id=1, source_target_pairs={{8,0},{12,4},{16,24},{20,28},{9,1},{13,5},{17,25},{21,29},{10,2},{... | collective-permute-start | bytes 798728 | tf_op jit(solution)/shard_map/ppermute | solution.py:335
  31.8 6.5 %collective-permute-start.8 = (bf16[208,640]{1,0:T(8,128)(2,1)S(1)}, bf16[208,640]{1,0:T(8,128)(2,1)S(1)}, u32[]{:S(2)}, u32[]{:S(2)}) collective-permute-start(bf16[208,640]{1,0:T(8,128)(2,1)S(1)} %add.13.refs_0_.refs_29_), channel_id=1, source_target_pairs={{0,4},{4,0},{8,12},{12,8},{16,20},{20,16},{24,28},{28,24},{1,5},{5... | collective-permute-start | bytes 798728 | tf_op jit(solution)/shard_map/ppermute | solution.py:255
  44.3 1.7 %collective-permute-start.9 = (bf16[96,1664]{1,0:T(8,128)(2,1)S(1)}, bf16[96,1664]{1,0:T(8,128)(2,1)S(1)}, u32[]{:S(2)}, u32[]{:S(2)}) collective-permute-start(bf16[96,1664]{1,0:T(8,128)(2,1)S(1)} %get-tuple-element.95), channel_id=1, source_target_pairs={{0,1},{1,0},{2,3},{3,2},{4,5},{5,4},{6,7},{7,6},{8,9},{9,8},{10,11... | collective-permute-start | bytes 958472 | tf_op jit(solution)/shard_map/ppermute | solution.py:255
  46.1 9.6 %collective-permute-start.10 = (bf16[96,1664]{1,0:T(8,128)(2,1)S(1)}, bf16[96,1664]{1,0:T(8,128)(2,1)S(1)}, u32[]{:S(2)}, u32[]{:S(2)}) collective-permute-start(bf16[96,1664]{1,0:T(8,128)(2,1)S(1)} %add_convert_fusion.1.one_ref), channel_id=1, source_target_pairs={{0,2},{1,3},{2,0},{3,1},{4,6},{5,7},{6,4},{7,5},{8,10},{9,11},{10,... | collective-permute-start | bytes 958472 | tf_op jit(solution)/shard_map/ppermute | solution.py:255
  55.8 1.7 %collective-permute-start.11 = (bf16[96,1664]{1,0:T(8,128)(2,1)S(1)}, bf16[96,1664]{1,0:T(8,128)(2,1)S(1)}, u32[]{:S(2)}, u32[]{:S(2)}) collective-permute-start(bf16[96,1664]{1,0:T(8,128)(2,1)S(1)} %add_convert_fusion), channel_id=1, source_target_pairs={{0,1},{1,0},{2,3},{3,2},{4,5},{5,4},{6,7},{7,6},{8,9},{9,8},{10,11... | collective-permute-start | bytes 958472 | tf_op jit(solution)/shard_map/ppermute | solution.py:255
